TPU v7x, 32 devices: a whole 2x2x4 slice. The times are simulated.
32 devices in a mesh: dp: 8 (over z, x), fsdp: 4 (over y, core).
Axes of the slice: x: 2, y: 2, z: 4, core: 2. Of those that a mesh axis runs over, the one named last changes fastest.
Arguments:
- hidden: bfloat16 [512, 64, 768], P(('dp', 'fsdp')), may hold values from -6 to 6
- lengths: int32 [512], P(('dp', 'fsdp')), may hold values from 3 to 64, as said below
- cotangent: bfloat16 [512, 64, 768], P(('dp', 'fsdp')), may hold values from -6 to 6
- attgain: bfloat16 [768], P(('dp', 'fsdp')), may hold values from 0.25 to 1.75
- attshift: bfloat16 [768], P(('dp', 'fsdp')), may hold values from -2 to 2
- querymat: bfloat16 [768, 768], P(None, ('dp', 'fsdp')), may hold values from -0.21875 to 0.21875
- querybias: bfloat16 [768], P(('dp', 'fsdp')), may hold values from -2 to 2
- keymat: bfloat16 [768, 768], P(None, ('dp', 'fsdp')), may hold values from -0.21875 to 0.21875
- valuemat: bfloat16 [768, 768], P(None, ('dp', 'fsdp')), may hold values from -0.21875 to 0.21875
- valuebias: bfloat16 [768], P(('dp', 'fsdp')), may hold values from -2 to 2
- mixmat: bfloat16 [768, 768], P(None, ('dp', 'fsdp')), may hold values from -0.625 to 0.625
- mixbias: bfloat16 [768], P(('dp', 'fsdp')), may hold values from -2 to 2
- mlpgain: bfloat16 [768], P(('dp', 'fsdp')), may hold values from 0.25 to 1.75
- mlpshift: bfloat16 [768], P(('dp', 'fsdp')), may hold values from -2 to 2
- upmat_w: bfloat16 [768, 3072], P(None, ('dp', 'fsdp')), may hold values from -0.21875 to 0.21875
- upbias: bfloat16 [3072], P(('dp', 'fsdp')), may hold values from -2 to 2
- downmat: bfloat16 [3072, 768], P(None, ('dp', 'fsdp')), may hold values from -0.109375 to 0.109375
- downbias: bfloat16 [768], P(('dp', 'fsdp')), may hold values from -2 to 2
Outputs:
- block_out: bfloat16 [512, 64, 768], P(('dp', 'fsdp'))
- input_grad: float32 [512, 64, 768], P(('dp', 'fsdp'))
- attgain_grad: float32 [768], P(('dp', 'fsdp'))
- attshift_grad: float32 [768], P(('dp', 'fsdp'))
- querymat_grad: float32 [768, 768], P(None, ('dp', 'fsdp'))
- querybias_grad: float32 [768], P(('dp', 'fsdp'))
- keymat_grad: float32 [768, 768], P(None, ('dp', 'fsdp'))
- valuemat_grad: float32 [768, 768], P(None, ('dp', 'fsdp'))
- valuebias_grad: float32 [768], P(('dp', 'fsdp'))
- mixmat_grad: float32 [768, 768], P(None, ('dp', 'fsdp'))
- mixbias_grad: float32 [768], P(('dp', 'fsdp'))
- mlpgain_grad: float32 [768], P(('dp', 'fsdp'))
- mlpshift_grad: float32 [768], P(('dp', 'fsdp'))
- upmat_grad: float32 [768, 3072], P(None, ('dp', 'fsdp'))
- upbias_grad: float32 [3072], P(('dp', 'fsdp'))
- downmat_grad: float32 [3072, 768], P(None, ('dp', 'fsdp'))
- downbias_grad: float32 [768], P(('dp', 'fsdp'))
Inputs may be any that keep to these rules, and one draw needn't show every extreme that they name: The first lengths[c] token slots of caption c are real, the rest padding; some caption has 64 real tokens and some has 3.
All inputs are finite; a program needn't handle non-finite values.
Results may differ from a plain program's by a relative error of at most 0.013.
Values may be sent and summed in bfloat16 or wider, within the bound.
No kernel may reach another device: no remote copies, remote signals or barrier semaphores. Data moves between devices by JAX's collectives and lax.ppermute only.
A program may use at most 192 MiB of HBM per device.

v0:
```python
import math

import jax
import jax.numpy as jnp
from jax import lax
from jax.sharding import PartitionSpec as P

HEADS = 12


def layer_norm(values, gain, shift):
    centre = jnp.mean(values, axis=-1, keepdims=True)
    centred = values - centre
    spread = jnp.mean(centred * centred, axis=-1, keepdims=True)
    return centred * lax.rsqrt(spread + 1e-06) * gain + shift


def smooth(values):
    return jax.nn.gelu(values, approximate=True)


def project(inputs, matrix):
    return jnp.einsum("cli,ij->clj", inputs, matrix, preferred_element_type=jnp.float32)


def project_back(grads, matrix):
    return jnp.einsum("clj,ij->cli", grads, matrix, preferred_element_type=jnp.float32)


def outer_sum(inputs, grads):
    return jnp.einsum("cli,clj->ij", inputs, grads, preferred_element_type=jnp.float32)


def token_sum(grads):
    return jnp.sum(grads.astype(jnp.float32), axis=(0, 1))


def masked_scores(query_low, keys_low, keymask, factor):
    raw = (
        jnp.einsum("clhd,cmhd->chlm", query_low, keys_low, preferred_element_type=jnp.float32)
        * factor
    )
    return jnp.where(keymask[:, None, None, :], raw, -1e30)


def per_device(
    hidden,
    lengths,
    cotangent,
    attgain,
    attshift,
    querymat,
    querybias,
    keymat,
    valuemat,
    valuebias,
    mixmat,
    mixbias,
    mlpgain,
    mlpshift,
    upmat_w,
    upbias,
    downmat,
    downbias,
):
    captions, length, width = hidden.shape
    head_size = width // HEADS
    factor = 1.0 / math.sqrt(head_size)
    positions = lax.broadcasted_iota(jnp.int32, (captions, length), 1)
    keymask = positions < lengths[:, None]
    rowmask = keymask.astype(jnp.float32)[..., None]
    gathered = (
        lax.all_gather(attgain, ("dp", "fsdp"), axis=0, tiled=True),
        lax.all_gather(attshift, ("dp", "fsdp"), axis=0, tiled=True),
        lax.all_gather(querymat, ("dp", "fsdp"), axis=1, tiled=True),
        lax.all_gather(querybias, ("dp", "fsdp"), axis=0, tiled=True),
        lax.all_gather(keymat, ("dp", "fsdp"), axis=1, tiled=True),
        lax.all_gather(valuemat, ("dp", "fsdp"), axis=1, tiled=True),
        lax.all_gather(valuebias, ("dp", "fsdp"), axis=0, tiled=True),
        lax.all_gather(mixmat, ("dp", "fsdp"), axis=1, tiled=True),
        lax.all_gather(mixbias, ("dp", "fsdp"), axis=0, tiled=True),
        lax.all_gather(mlpgain, ("dp", "fsdp"), axis=0, tiled=True),
        lax.all_gather(mlpshift, ("dp", "fsdp"), axis=0, tiled=True),
        lax.all_gather(upmat_w, ("dp", "fsdp"), axis=1, tiled=True),
        lax.all_gather(upbias, ("dp", "fsdp"), axis=0, tiled=True),
        lax.all_gather(downmat, ("dp", "fsdp"), axis=1, tiled=True),
        lax.all_gather(downbias, ("dp", "fsdp"), axis=0, tiled=True),
    )
    (
        gain_one,
        shift_one,
        query_w,
        query_b,
        keys_w,
        values_w,
        values_b,
        mixer_w,
        mixer_b,
        gain_two,
        shift_two,
        upper_w,
        upper_b,
        lower_w,
        lower_b,
    ) = gathered
    gain_one = gain_one.astype(jnp.float32)
    shift_one = shift_one.astype(jnp.float32)
    gain_two = gain_two.astype(jnp.float32)
    shift_two = shift_two.astype(jnp.float32)
    source = hidden.astype(jnp.float32)
    normed_low = layer_norm(source, gain_one, shift_one).astype(jnp.bfloat16)
    query_low = (project(normed_low, query_w) + query_b.astype(jnp.float32)).astype(jnp.bfloat16)
    keys_low = project(normed_low, keys_w).astype(jnp.bfloat16)
    values_low = (project(normed_low, values_w) + values_b.astype(jnp.float32)).astype(jnp.bfloat16)
    query_heads = query_low.reshape(captions, length, HEADS, head_size)
    keys_heads = keys_low.reshape(captions, length, HEADS, head_size)
    values_heads = values_low.reshape(captions, length, HEADS, head_size)
    scores = masked_scores(query_heads, keys_heads, keymask, factor)
    peak = jnp.max(scores, axis=-1, keepdims=True)
    logsum = peak + jnp.log(jnp.sum(jnp.exp(scores - peak), axis=-1, keepdims=True))
    probs_low = jnp.exp(scores - logsum).astype(jnp.bfloat16)
    mixed_low = (
        jnp.einsum("chlm,cmhd->clhd", probs_low, values_heads, preferred_element_type=jnp.float32)
        .reshape(captions, length, width)
        .astype(jnp.bfloat16)
    )
    middle = source + project(mixed_low, mixer_w) + mixer_b.astype(jnp.float32)
    normed2_low = layer_norm(middle, gain_two, shift_two).astype(jnp.bfloat16)
    upper = project(normed2_low, upper_w) + upper_b.astype(jnp.float32)
    active_low = smooth(upper).astype(jnp.bfloat16)
    result = middle + project(active_low, lower_w) + lower_b.astype(jnp.float32)
    block_out = result.astype(jnp.bfloat16)
    again = (
        lax.all_gather(attgain, ("dp", "fsdp"), axis=0, tiled=True),
        lax.all_gather(attshift, ("dp", "fsdp"), axis=0, tiled=True),
        lax.all_gather(querymat, ("dp", "fsdp"), axis=1, tiled=True),
        lax.all_gather(querybias, ("dp", "fsdp"), axis=0, tiled=True),
        lax.all_gather(keymat, ("dp", "fsdp"), axis=1, tiled=True),
        lax.all_gather(valuemat, ("dp", "fsdp"), axis=1, tiled=True),
        lax.all_gather(valuebias, ("dp", "fsdp"), axis=0, tiled=True),
        lax.all_gather(mixmat, ("dp", "fsdp"), axis=1, tiled=True),
        lax.all_gather(mixbias, ("dp", "fsdp"), axis=0, tiled=True),
        lax.all_gather(mlpgain, ("dp", "fsdp"), axis=0, tiled=True),
        lax.all_gather(mlpshift, ("dp", "fsdp"), axis=0, tiled=True),
        lax.all_gather(upmat_w, ("dp", "fsdp"), axis=1, tiled=True),
        lax.all_gather(upbias, ("dp", "fsdp"), axis=0, tiled=True),
        lax.all_gather(downmat, ("dp", "fsdp"), axis=1, tiled=True),
        lax.all_gather(downbias, ("dp", "fsdp"), axis=0, tiled=True),
    )
    (
        gain_one,
        shift_one,
        query_w,
        query_b,
        keys_w,
        values_w,
        values_b,
        mixer_w,
        mixer_b,
        gain_two,
        shift_two,
        upper_w,
        upper_b,
        lower_w,
        lower_b,
    ) = again
    gain_one = gain_one.astype(jnp.float32)
    shift_one = shift_one.astype(jnp.float32)
    gain_two = gain_two.astype(jnp.float32)
    shift_two = shift_two.astype(jnp.float32)
    grad_out = cotangent.astype(jnp.float32) * rowmask
    grad_low = grad_out.astype(jnp.bfloat16)
    downmat_grad = outer_sum(active_low, grad_low)
    downbias_grad = token_sum(grad_low)
    grad_active = project_back(grad_low, lower_w)
    gelu_pull = jax.vjp(smooth, upper)[1]
    grad_upper_low = gelu_pull(grad_active)[0].astype(jnp.bfloat16)
    upmat_grad = outer_sum(normed2_low, grad_upper_low)
    upbias_grad = token_sum(grad_upper_low)
    grad_normed2 = project_back(grad_upper_low, upper_w)
    norm_pull = jax.vjp(layer_norm, middle, gain_two, shift_two)[1]
    grad_ln_two, mlpgain_grad, mlpshift_grad = norm_pull(grad_normed2)
    grad_middle = grad_out + grad_ln_two
    mlpgain_grad, mlpshift_grad, upmat_grad, upbias_grad, downmat_grad, downbias_grad = (
        lax.psum_scatter(mlpgain_grad, ("dp", "fsdp"), scatter_dimension=0, tiled=True),
        lax.psum_scatter(mlpshift_grad, ("dp", "fsdp"), scatter_dimension=0, tiled=True),
        lax.psum_scatter(upmat_grad, ("dp", "fsdp"), scatter_dimension=1, tiled=True),
        lax.psum_scatter(upbias_grad, ("dp", "fsdp"), scatter_dimension=0, tiled=True),
        lax.psum_scatter(downmat_grad, ("dp", "fsdp"), scatter_dimension=1, tiled=True),
        lax.psum_scatter(downbias_grad, ("dp", "fsdp"), scatter_dimension=0, tiled=True),
    )
    grad_branch_low = grad_middle.astype(jnp.bfloat16)
    mixmat_grad = outer_sum(mixed_low, grad_branch_low)
    mixbias_grad = token_sum(grad_branch_low)
    grad_mixed_low = (
        project_back(grad_branch_low, mixer_w)
        .astype(jnp.bfloat16)
        .reshape(captions, length, HEADS, head_size)
    )
    scores_again = masked_scores(query_heads, keys_heads, keymask, factor)
    probs = jnp.exp(scores_again - logsum)
    probs_again = probs.astype(jnp.bfloat16)
    grad_values_low = jnp.einsum(
        "chlm,clhd->cmhd", probs_again, grad_mixed_low, preferred_element_type=jnp.float32
    ).astype(jnp.bfloat16)
    grad_probs = jnp.einsum(
        "clhd,cmhd->chlm", grad_mixed_low, values_heads, preferred_element_type=jnp.float32
    )
    weighted = jnp.sum(probs * grad_probs, axis=-1, keepdims=True)
    grad_scores_low = (probs * (grad_probs - weighted)).astype(jnp.bfloat16)
    grad_query_low = (
        jnp.einsum(
            "chlm,cmhd->clhd", grad_scores_low, keys_heads, preferred_element_type=jnp.float32
        )
        * factor
    ).astype(jnp.bfloat16)
    grad_keys_low = (
        jnp.einsum(
            "chlm,clhd->cmhd", grad_scores_low, query_heads, preferred_element_type=jnp.float32
        )
        * factor
    ).astype(jnp.bfloat16)
    grad_query_low = grad_query_low.reshape(captions, length, width)
    grad_keys_low = grad_keys_low.reshape(captions, length, width)
    grad_values_low = grad_values_low.reshape(captions, length, width)
    querymat_grad = outer_sum(normed_low, grad_query_low)
    querybias_grad = token_sum(grad_query_low)
    keymat_grad = outer_sum(normed_low, grad_keys_low)
    valuemat_grad = outer_sum(normed_low, grad_values_low)
    valuebias_grad = token_sum(grad_values_low)
    grad_normed = (
        project_back(grad_query_low, query_w)
        + project_back(grad_keys_low, keys_w)
        + project_back(grad_values_low, values_w)
    )
    first_pull = jax.vjp(layer_norm, source, gain_one, shift_one)[1]
    grad_ln_one, attgain_grad, attshift_grad = first_pull(grad_normed)
    input_grad = grad_middle + grad_ln_one
    (
        attgain_grad,
        attshift_grad,
        querymat_grad,
        querybias_grad,
        keymat_grad,
        valuemat_grad,
        valuebias_grad,
        mixmat_grad,
        mixbias_grad,
    ) = (
        lax.psum_scatter(attgain_grad, ("dp", "fsdp"), scatter_dimension=0, tiled=True),
        lax.psum_scatter(attshift_grad, ("dp", "fsdp"), scatter_dimension=0, tiled=True),
        lax.psum_scatter(querymat_grad, ("dp", "fsdp"), scatter_dimension=1, tiled=True),
        lax.psum_scatter(querybias_grad, ("dp", "fsdp"), scatter_dimension=0, tiled=True),
        lax.psum_scatter(keymat_grad, ("dp", "fsdp"), scatter_dimension=1, tiled=True),
        lax.psum_scatter(valuemat_grad, ("dp", "fsdp"), scatter_dimension=1, tiled=True),
        lax.psum_scatter(valuebias_grad, ("dp", "fsdp"), scatter_dimension=0, tiled=True),
        lax.psum_scatter(mixmat_grad, ("dp", "fsdp"), scatter_dimension=1, tiled=True),
        lax.psum_scatter(mixbias_grad, ("dp", "fsdp"), scatter_dimension=0, tiled=True),
    )
    return (
        block_out,
        input_grad,
        attgain_grad,
        attshift_grad,
        querymat_grad,
        querybias_grad,
        keymat_grad,
        valuemat_grad,
        valuebias_grad,
        mixmat_grad,
        mixbias_grad,
        mlpgain_grad,
        mlpshift_grad,
        upmat_grad,
        upbias_grad,
        downmat_grad,
        downbias_grad,
    )


def solution(mesh):
    placed = (
        P(("dp", "fsdp"), None, None),
        P(("dp", "fsdp")),
        P(("dp", "fsdp"), None, None),
        P(("dp", "fsdp")),
        P(("dp", "fsdp")),
        P(None, ("dp", "fsdp")),
        P(("dp", "fsdp")),
        P(None, ("dp", "fsdp")),
        P(None, ("dp", "fsdp")),
        P(("dp", "fsdp")),
        P(None, ("dp", "fsdp")),
        P(("dp", "fsdp")),
        P(("dp", "fsdp")),
        P(("dp", "fsdp")),
        P(None, ("dp", "fsdp")),
        P(("dp", "fsdp")),
        P(None, ("dp", "fsdp")),
        P(("dp", "fsdp")),
    )
    return jax.shard_map(
        per_device,
        mesh=mesh,
        in_specs=placed,
        out_specs=(
            P(("dp", "fsdp"), None, None),
            P(("dp", "fsdp"), None, None),
            P(("dp", "fsdp")),
            P(("dp", "fsdp")),
            P(None, ("dp", "fsdp")),
            P(("dp", "fsdp")),
            P(None, ("dp", "fsdp")),
            P(None, ("dp", "fsdp")),
            P(("dp", "fsdp")),
            P(None, ("dp", "fsdp")),
            P(("dp", "fsdp")),
            P(("dp", "fsdp")),
            P(("dp", "fsdp")),
            P(None, ("dp", "fsdp")),
            P(("dp", "fsdp")),
            P(None, ("dp", "fsdp")),
            P(("dp", "fsdp")),
        ),
        check_vma=False,
    )
```

profile of v0, /device:TPU:0, one launch (start us, length us, event | category | flops | bytes accessed | tf_op | source)
XLA Modules:
  0.0 1099.2 jit_solution(7005276852524164736)
XLA Ops:
  18.8 42.7 %all-reduce.19 = (bf16[768]{0:T(1024)(128)(2,1)S(1)}, bf16[768]{0:T(1024)(128)(2,1)S(1)}, bf16[768]{0:T(1024)(128)(2,1)S(1)}, bf16[768]{0:T(1024)(128)(2,1)S(1)}...) all-reduce(bf16[768]{0:T(1024)(128)(2,1)S(1)} %dynamic-update-slice, ...), channel_id=1, replica_groups=mesh['dp'=8,'fsdp'=4] {'dp','fsdp'}, use_global_device_ids=true, to_apply=%add.2 | all-reduce | flops 9216 | bytes 36864
  73.6 50.5 %all-gather.11.cloned.1.call-done = bf16[768,768]{0,1:T(8,128)(2,1)} async-done(((bf16[768,24]{0,1:T(8,128)(2,1)}), bf16[768,768]{0,1:T(8,128)(2,1)}) %all-gather.11.cloned.1.call-update) | async-done | bytes 1179664 | tf_op jit(solution)/shard_map/all_gather | solution.py:77
  130.9 49.2 %all-gather.7.cloned.1.call-done = bf16[768,768]{0,1:T(8,128)(2,1)} async-done(((bf16[768,24]{0,1:T(8,128)(2,1)}), bf16[768,768]{0,1:T(8,128)(2,1)}) %all-gather.7.cloned.1.call-update) | async-done | bytes 1179664 | tf_op jit(solution)/shard_map/all_gather | solution.py:78
  199.8 36.1 %all-gather.13.cloned.1.call-done = bf16[768,768]{0,1:T(8,128)(2,1)} async-done(((bf16[768,24]{0,1:T(8,128)(2,1)}), bf16[768,768]{0,1:T(8,128)(2,1)}) %all-gather.13.cloned.1.call-update) | async-done | bytes 1179664 | tf_op jit(solution)/shard_map/all_gather | solution.py:80
  243.0 58.2 %all-gather.15.cloned.1.call-done = bf16[768,3072]{0,1:T(8,128)(2,1)} async-done(((bf16[768,96]{0,1:T(8,128)(2,1)}), bf16[768,3072]{0,1:T(8,128)(2,1)}) %all-gather.15.cloned.1.call-update) | async-done | bytes 4718608 | tf_op jit(solution)/shard_map/all_gather | solution.py:84
  301.2 11.0 fusion.18
  312.2 54.2 %all-gather.17.cloned.1.call-done = bf16[3072,768]{0,1:T(8,128)(2,1)} async-done(((bf16[3072,24]{0,1:T(8,128)(2,1)}), bf16[3072,768]{0,1:T(8,128)(2,1)}) %all-gather.17.cloned.1.call-update) | async-done | bytes 4718608 | tf_op jit(solution)/shard_map/all_gather | solution.py:86
  366.4 16.6 %convert_reduce_fusion = (f32[3072]{0:T(1024)S(1)}, bf16[16,64,3072]{2,1,0:T(8,128)(2,1)S(1)}) fusion(f32[16,64,3072]{2,1,0:T(8,128)} %fusion.18, f32[3072]{0:T(1024)S(1)} %convert_element_type.143, bf16[3072,768]{0,1:T(8,128)(2,1)} %all-gather.17.cloned.1.call-done, bf16[16,64,768]{2,1,0:T(8,128)(2,1)S(1)} %copy-done.11, f32[16,64]{1,0:T(8,128)S(1)} %get-tuple-element.47), kind=kOutput, calls=%fused_computation.9 | convolution fusion | flops 4906546176 | bytes 25194496 | tf_op jit(solution)/shard_map/clj,ij->cli/dot_general | solution.py:27
  383.0 5.5 multiply_reduce_fusion.1
  401.6 6.2 reshape.174
  407.8 9.3 multiply_reduce_fusion
  426.1 6.2 reshape.176
  447.0 6.1 reshape.175
  458.2 6.6 convert_reduce_fusion.1
  469.4 5.2 reshape.177
  477.9 11.0 %convolution_bitcast_fusion.1 = f32[768,3072]{0,1:T(8,128)} fusion(bf16[16,64,3072]{2,1,0:T(8,128)(2,1)} %copy-done.23, f32[16,64,768]{2,1,0:T(8,128)} %copy-done.7, f32[768]{0:T(1024)S(1)} %convert_element_type.141, f32[768]{0:T(1024)S(1)} %convert_element_type.140, f32[16,64]{1,0:T(8,128)S(1)} %fusion.61, f32[16,64]{1,0:T(8,128)S(1)} %broadcast_multiply_fusion), kind=kOutput, calls=%fused_computation.21 | convolution fusion | flops 4835770368 | bytes 18888704 | tf_op jit(solution)/shard_map/cli,clj->ij/dot_general | solution.py:31
  489.2 12.2 %convolution_bitcast_fusion = f32[3072,768]{0,1:T(8,128)} fusion(bf16[16,64,768]{2,1,0:T(8,128)(2,1)} %param.20, f32[16,64]{1,0:T(8,128)S(1)} %get-tuple-element.47, f32[16,64,3072]{2,1,0:T(8,128)} %fusion.18, f32[3072]{0:T(1024)S(1)} %convert_element_type.143), kind=kOutput, calls=%fused_computation.20 | convolution fusion | flops 4865654784 | bytes 23609344 | tf_op jit(solution)/shard_map/cli,clj->ij/dot_general | solution.py:31
  512.3 40.7 %all-reduce.18 = (f32[768]{0:T(1024)S(1)}, f32[768]{0:T(1024)S(1)}, f32[768]{0:T(1024)S(1)}, f32[768]{0:T(1024)S(1)}, f32[768]{0:T(1024)S(1)}, /*index=5*/f32[76...) all-reduce(f32[768]{0:T(1024)S(1)} %get-tuple-element.19, ...), channel_id=2, replica_groups=mesh['dp'=8,'fsdp'=4] {'dp','fsdp'}, use_global_device_ids=true, to_apply=%region_12.13.clone | all-reduce | flops 9216 | bytes 73728
  563.2 13.2 %add_convert_fusion = bf16[16,64,768]{2,1,0:T(8,128)(2,1)} fusion(f32[16,64,768]{2,1,0:T(8,128)S(1)} %copy-done.9, bf16[3072,768]{0,1:T(8,128)(2,1)} %all-gather.17.cloned.1.call-done, f32[768]{0:T(1024)S(1)} %convert_element_type.145, f32[16,64,3072]{2,1,0:T(8,128)} %fusion.18, f32[3072]{0:T(1024)S(1)} %convert_element_type.143), kind=kOutput, calls=%fused_computation.61 | convolution fusion | flops 4865654784 | bytes 22035456 | tf_op jit(solution)/shard_map/cli,ij->clj/dot_general | solution.py:23
  576.5 24.1 %reduce-scatter.9.cloned.1.call-done = f32[768,24]{0,1:T(8,128)} async-done(((f32[768,768]{0,1:T(8,128)}), f32[768,24]{0,1:T(8,128)}) %reduce-scatter.9.cloned.1.call-update) | async-done | bytes 73744 | tf_op jit(solution)/shard_map/reduce_scatter | solution.py:254
  600.5 103.9 %reduce-scatter.7.cloned.1.call-done = f32[768,24]{0,1:T(8,128)} async-done(((f32[768,768]{0,1:T(8,128)}), f32[768,24]{0,1:T(8,128)}) %reduce-scatter.7.cloned.1.call-update) | async-done | bytes 73744 | tf_op jit(solution)/shard_map/reduce_scatter | solution.py:252
  704.4 104.7 %reduce-scatter.11.cloned.1.call-done = f32[768,24]{0,1:T(8,128)} async-done(((f32[768,768]{0,1:T(8,128)}), f32[768,24]{0,1:T(8,128)}) %reduce-scatter.11.cloned.1.call-update) | async-done | bytes 73744 | tf_op jit(solution)/shard_map/reduce_scatter | solution.py:255
  809.1 141.1 %reduce-scatter.15.cloned.1.call-done = f32[768,96]{0,1:T(8,128)} async-done(((f32[768,3072]{0,1:T(8,128)}), f32[768,96]{0,1:T(8,128)}) %reduce-scatter.15.cloned.1.call-update) | async-done | bytes 294928 | tf_op jit(solution)/shard_map/reduce_scatter | solution.py:187
  950.2 141.9 %reduce-scatter.17.cloned.1.call-done = f32[3072,24]{0,1:T(8,128)} async-done(((f32[3072,768]{0,1:T(8,128)}), f32[3072,24]{0,1:T(8,128)}) %reduce-scatter.17.cloned.1.call-update) | async-done | bytes 294928 | tf_op jit(solution)/shard_map/reduce_scatter | solution.py:189
  (158 shorter events, 127.8 us)
Async XLA Ops:
  7.2 56.8 %copy-start.1 = (bf16[16,64,768]{2,1,0:T(8,128)(2,1)S(1)}, bf16[16,64,768]{2,1,0:T(8,128)(2,1)}, u32[]{:S(2)}) copy-start(bf16[16,64,768]{2,1,0:T(8,128)(2,1)} %param.18) | copy-start | bytes 4718596
  7.2 60.8 %all-gather.9.cloned.1.call-start = ((), (), s32[]{:S(2)}) async-start(), calls=%async_computation.7 | async-start | bytes 1216512 | tf_op jit(solution)/shard_map/all_gather | solution.py:75
  7.9 116.2 %all-gather.11.cloned.1.call-start = ((), (), s32[]{:S(2)}) async-start(), calls=%async_computation.8 | async-start | bytes 1216512 | tf_op jit(solution)/shard_map/all_gather | solution.py:77
  8.7 171.4 %all-gather.7.cloned.1.call-start = ((), (), s32[]{:S(2)}) async-start(), calls=%async_computation.6 | async-start | bytes 1216512 | tf_op jit(solution)/shard_map/all_gather | solution.py:78
  9.4 226.5 %all-gather.13.cloned.1.call-start = ((), (), s32[]{:S(2)}) async-start(), calls=%async_computation.9 | async-start | bytes 1216512 | tf_op jit(solution)/shard_map/all_gather | solution.py:80
  10.0 291.2 %all-gather.15.cloned.1.call-start = ((), (), s32[]{:S(2)}) async-start(), calls=%async_computation.10 | async-start | bytes 4866048 | tf_op jit(solution)/shard_map/all_gather | solution.py:84
  10.6 355.8 %all-gather.17.cloned.1.call-start = ((), (), s32[]{:S(2)}) async-start(), calls=%async_computation.11 | async-start | bytes 4866048 | tf_op jit(solution)/shard_map/all_gather | solution.py:86
  11.2 565.3 %reduce-scatter.13.cloned.1.call-start = ((), (), s32[]{:S(2)}) async-start(), calls=%async_computation.15 | async-start | bytes 2433024 | tf_op jit(solution)/shard_map/reduce_scatter | solution.py:257
  191.7 4.5 copy-start.6
  243.0 123.4 %copy-start.11 = (bf16[16,64,768]{2,1,0:T(8,128)(2,1)S(1)}, bf16[16,64,768]{2,1,0:T(8,128)(2,1)}, u32[]{:S(2)}) copy-start(bf16[16,64,768]{2,1,0:T(8,128)(2,1)} %param.20) | copy-start | bytes 4718596
  366.4 16.6 %copy-start.8 = (f32[16,64,768]{2,1,0:T(8,128)S(1)}, f32[16,64,768]{2,1,0:T(8,128)}, u32[]{:S(2)}) copy-start(f32[16,64,768]{2,1,0:T(8,128)} %copy-done.7) | copy-start | bytes 9437188
  366.4 16.6 %copy-start.20 = (bf16[768,3072]{0,1:T(8,128)(2,1)S(1)}, bf16[768,3072]{0,1:T(8,128)(2,1)}, u32[]{:S(2)}) copy-start(bf16[768,3072]{0,1:T(8,128)(2,1)} %all-gather.15.cloned.1.call-done) | copy-start | bytes 14155780
  383.0 5.6 copy-start.23
  393.5 4.1 copy-start.22
  397.6 203.0 %reduce-scatter.9.cloned.1.call-start = ((), (), s32[]{:S(2)}) async-start(), calls=%async_computation.13 | async-start | bytes 2433024 | tf_op jit(solution)/shard_map/reduce_scatter | solution.py:254
  401.6 15.5 %slice-start = ((s8[6291456]{0:T(1024)(128)(4,1)}), s8[2097152]{0:T(1024)(128)(4,1)S(1)}, s32[]{:S(2)}) async-start(s8[6291456]{0:T(1024)(128)(4,1)} %bitcast.80), calls=%async_computation.18 | async-start | bytes 4194304
  407.8 9.3 slice-start.1
  426.1 6.2 copy-start.2
  437.1 267.3 %reduce-scatter.7.cloned.1.call-start = ((), (), s32[]{:S(2)}) async-start(), calls=%async_computation.12 | async-start | bytes 2433024 | tf_op jit(solution)/shard_map/reduce_scatter | solution.py:252
  457.8 351.3 %reduce-scatter.11.cloned.1.call-start = ((), (), s32[]{:S(2)}) async-start(), calls=%async_computation.14 | async-start | bytes 2433024 | tf_op jit(solution)/shard_map/reduce_scatter | solution.py:255
  477.9 472.3 %reduce-scatter.15.cloned.1.call-start = ((), (), s32[]{:S(2)}) async-start(), calls=%async_computation.16 | async-start | bytes 9732096 | tf_op jit(solution)/shard_map/reduce_scatter | solution.py:187
  489.0 603.1 %reduce-scatter.17.cloned.1.call-start = ((), (), s32[]{:S(2)}) async-start(), calls=%async_computation.17 | async-start | bytes 9732096 | tf_op jit(solution)/shard_map/reduce_scatter | solution.py:189
  508.9 49.3 %copy-start.12 = (bf16[16,64,768]{2,1,0:T(8,128)(2,1)S(1)}, bf16[16,64,768]{2,1,0:T(8,128)(2,1)}, u32[]{:S(2)}) copy-start(bf16[16,64,768]{2,1,0:T(8,128)(2,1)} %param.20) | copy-start | bytes 4718596
  558.2 5.0 copy-start.9
  (14 other events, 28.6 us)
Sparse Core Ops, SparseCore 0:
  10.9 56.9 all-gather.8
  70.9 53.1 all-gather.10
  127.0 53.0 all-gather.6
  182.8 53.0 all-gather.12
  238.6 62.5 all-gather.14
  304.0 62.3 all-gather.16
  397.7 97.7 reduce-scatter.12
  502.2 98.3 reduce-scatter.8
  606.4 97.9 reduce-scatter.6
  711.0 98.0 reduce-scatter.10
  815.6 134.5 reduce-scatter.14
  957.5 134.5 reduce-scatter.16
where the time goes:
time: 1110 us; the launch traced here: 1100 us
  waiting for transfers between devices  770 us (69%)
  matrix products  142 us (13%)
  blocking collectives  83.4 us (8%)
  local copies, waits for them, and re-layouts  71 us (6%)
  other arithmetic  16.6 us (1%)
  between operations  15 us (1%)
    reduce_scatter x1, waiting for transfers between devices, per_device(): lax.psum_scatter(downmat_grad, ('dp', 'fsdp'), scatter_dimension=1, tiled...  142 us
    reduce_scatter x1, waiting for transfers between devices, per_device(): lax.psum_scatter(upmat_grad, ('dp', 'fsdp'), scatter_dimension=1, tiled=T...  141 us
    reduce_scatter x1, waiting for transfers between devices, per_device(): lax.psum_scatter(valuemat_grad, ('dp', 'fsdp'), scatter_dimension=1, tile...  105 us
    reduce_scatter x1, waiting for transfers between devices, per_device(): lax.psum_scatter(querymat_grad, ('dp', 'fsdp'), scatter_dimension=1, tile...  104 us
    unnamed x2, blocking collectives  83.4 us
    all_gather x1, waiting for transfers between devices, per_device(): lax.all_gather(upmat_w, ('dp', 'fsdp'), axis=1, tiled=True)  58.2 us
    all_gather x1, waiting for transfers between devices, per_device(): lax.all_gather(downmat, ('dp', 'fsdp'), axis=1, tiled=True)  54.2 us
    all_gather x1, waiting for transfers between devices, per_device(): lax.all_gather(keymat, ('dp', 'fsdp'), axis=1, tiled=True)  50.5 us
  transfers between devices with their start and end apart: 12, of which 11 were waited for; matrix products, arithmetic and copies ran while one was open for 17% of the time, Pallas kernels for 0%

commit v1 on v0

--- a/solution.py
+++ b/solution.py
@@ -1,8 +1,11 @@
+import functools
 import math
 
 import jax
 import jax.numpy as jnp
 from jax import lax
+from jax.experimental import pallas as pl
+from jax.experimental.pallas import tpu as pltpu
 from jax.sharding import PartitionSpec as P
 
 HEADS = 12
@@ -278,6 +281,663 @@
     )
 
 
+NT = (((1,), (1,)), ((), ()))
+NN = (((1,), (0,)), ((), ()))
+TN = (((0,), (0,)), ((), ()))
+F32 = jnp.float32
+BF16 = jnp.bfloat16
+AXES = ("dp", "fsdp")
+QUAD = 4
+VMEM_LIMIT = 56 * 1024 * 1024
+
+
+def dot(left, right, dims):
+    return lax.dot_general(left, right, dims, preferred_element_type=F32)
+
+
+class Grid3:
+    def __init__(self, dp, fsdp):
+        self.c = 2
+        self.y = fsdp // 2
+        self.x = self.y
+        self.z = dp // self.x
+        self.count = dp * fsdp
+
+    def index(self, z, x, y, c):
+        return ((z * self.x + x) * self.y + y) * self.c + c
+
+    def shift(self, values, kz=0, kx=0, ky=0, kc=0):
+        pairs = []
+        for z in range(self.z):
+            for x in range(self.x):
+                for y in range(self.y):
+                    for c in range(self.c):
+                        target = self.index(
+                            (z + kz) % self.z, (x + kx) % self.x, (y + ky) % self.y, (c + kc) % self.c
+                        )
+                        pairs.append((self.index(z, x, y, c), target))
+        return lax.ppermute(values, AXES, pairs)
+
+    def here(self):
+        dp, fsdp = lax.axis_index("dp"), lax.axis_index("fsdp")
+        return lax.div(dp, self.x), lax.rem(dp, self.x), lax.div(fsdp, self.c), lax.rem(fsdp, self.c)
+
+    def away(self, kz, kx, ky, kc):
+        z, x, y, c = self.here()
+        return self.index(
+            lax.rem(z + (kz % self.z), self.z),
+            lax.rem(x + (kx % self.x), self.x),
+            lax.rem(y + (ky % self.y), self.y),
+            lax.rem(c + (kc % self.c), self.c),
+        )
+
+
+def gather(grid, own):
+    rows = [own]
+    for _ in range(grid.z - 1):
+        rows.append(grid.shift(rows[-1], kz=1))
+    half = grid.z // 2
+    first = jnp.stack(rows[:half])
+    second = jnp.stack(rows[half:])
+    first_x = grid.shift(first, kx=1)
+    second_y = grid.shift(second, ky=1)
+    first_y = grid.shift(first, ky=1)
+    second_x = grid.shift(second, kx=1)
+    first_xy = grid.shift(first_x, ky=1)
+    second_xy = grid.shift(second_y, kx=1)
+    arrays, places = [], []
+    for array, start, kx, ky in (
+        (first, 0, 0, 0),
+        (second, half, 0, 0),
+        (first_x, 0, 1, 0),
+        (second_y, half, 0, 1),
+        (first_y, 0, 0, 1),
+        (second_x, half, 1, 0),
+        (first_xy, 0, 1, 1),
+        (second_xy, half, 1, 1),
+    ):
+        arrays.append(array)
+        places.append([(-(start + k), -kx, -ky, 0) for k in range(half)])
+        arrays.append(grid.shift(array, kc=1))
+        places.append([(-(start + k), -kx, -ky, -1) for k in range(half)])
+    return arrays, places
+
+
+def place(grid, places, refs, held, sems):
+    copies = []
+    for ref, spots in zip(refs, places):
+        for slot, spot in enumerate(spots):
+            copies.append(
+                pltpu.make_async_copy(ref.at[slot], held.at[grid.away(*spot)], sems.at[len(copies)])
+            )
+    for copy in copies:
+        copy.start()
+    for copy in copies:
+        copy.wait()
+
+
+def outgoing(grid, core):
+    half = grid.z // 2
+    slots = []
+    for which in range(2):
+        for one in range(2):
+            for two in range(2):
+                for low in range(half):
+                    kx, ky = (one, two) if which == 0 else (two, one)
+                    slots.append((which * half + low, kx, ky, core))
+    return slots
+
+
+def scatter(grid, own, other):
+    half = grid.z // 2
+
+    def plus(left, right):
+        return (left.astype(F32) + right.astype(F32)).astype(BF16)
+
+    arrived = grid.shift(other, kc=1)
+    tail = own.shape[1:]
+    shape = (2, 2, 2, half) + tail
+    own = own.reshape(shape)
+    arrived = arrived.reshape(shape)
+    send_a = plus(own[0, 1], arrived[0, 1])
+    send_b = plus(own[1, 1], arrived[1, 1])
+    got_a = grid.shift(send_a, kx=1)
+    got_b = grid.shift(send_b, ky=1)
+    keep_a = plus(own[0, 0], arrived[0, 0])
+    keep_b = plus(own[1, 0], arrived[1, 0])
+    next_a = plus(keep_a[1], got_a[1])
+    next_b = plus(keep_b[1], got_b[1])
+    last_a = grid.shift(next_a, ky=1)
+    last_b = grid.shift(next_b, kx=1)
+    rest_a = keep_a[0].astype(F32) + got_a[0].astype(F32) + last_a.astype(F32)
+    rest_b = keep_b[0].astype(F32) + got_b[0].astype(F32) + last_b.astype(F32)
+    parts = [rest_a[k] for k in range(half)] + [rest_b[k] for k in range(half)]
+    total = parts[0]
+    for k in range(1, grid.z):
+        total = total + grid.shift(parts[k].astype(BF16), kz=k).astype(F32)
+    return total
+
+
+def lanes_of(rows):
+    return lax.broadcasted_iota(jnp.int32, (rows, 256), 1) // 64
+
+
+def spread(block):
+    head = lanes_of(block.shape[0])
+    zero = jnp.zeros_like(block)
+    return jnp.concatenate([jnp.where(head == g, block, zero) for g in range(QUAD)], axis=0)
+
+
+def collect(square):
+    head = lanes_of(64)
+    total = jnp.where(head == 0, square[0:64], 0.0)
+    for g in range(1, QUAD):
+        total = jnp.where(head == g, square[64 * g : 64 * g + 64], total)
+    return total
+
+
+def normal(values):
+    centre = jnp.mean(values, axis=-1, keepdims=True)
+    centred = values - centre
+    spread_of = jnp.mean(centred * centred, axis=-1, keepdims=True)
+    scale = lax.rsqrt(spread_of + 1e-06)
+    return centred * scale, scale
+
+
+def normal_back(hat, scale, gain, grads):
+    weighted = grads * gain
+    middle = jnp.mean(weighted, axis=-1, keepdims=True)
+    along = jnp.mean(weighted * hat, axis=-1, keepdims=True)
+    return scale * (weighted - middle - hat * along)
+
+
+def row_mask(lengths_ref, step, captions, length):
+    position = lax.broadcasted_iota(jnp.int32, (length, 1), 0)
+    return jnp.concatenate(
+        [(position < lengths_ref[step * captions + k]).astype(F32) for k in range(captions)], axis=0
+    )
+
+
+def pack_kernel(grid, small_ref, up_ref, q_ref, k_ref, v_ref, out_ref, wide):
+    wide[...] = jnp.zeros_like(wide)
+    wide[0:8, 0:24] = small_ref[...]
+    wide[8:9, 0:96] = up_ref[...]
+    me = lax.axis_index("dp") * (grid.y * grid.c) + lax.axis_index("fsdp")
+    eight = pltpu.roll(wide[0:8, :], me * 24, 1)
+    four = pltpu.roll(wide[8:16, :], lax.rem(me, 8) * 96, 1)
+    row = lax.broadcasted_iota(jnp.int32, (8, 768), 0)
+    four = jnp.where(row == lax.div(me, 8), jnp.broadcast_to(four[0:1], (8, 768)), 0.0)
+    zero = jnp.zeros((8, 768), F32)
+    out_ref[0] = jnp.concatenate([eight, four, zero], axis=0).astype(BF16)
+    out_ref[1] = q_ref[...]
+    out_ref[2] = k_ref[...]
+    out_ref[3] = v_ref[...]
+
+
+def attend_kernel(grid, places, length, lengths_ref, hidden_ref, *rest):
+    count = len(places)
+    refs, rest = rest[:count], rest[count:]
+    normed_ref, q_ref, k_ref, v_ref, probs_ref, mixed_ref, vec_ref, held, sems = rest
+    step = pl.program_id(0)
+
+    @pl.when(step == 0)
+    def _():
+        place(grid, places, refs, held, sems)
+        total = held[0, 0].astype(F32)
+        for j in range(1, grid.count):
+            total = total + held[j, 0].astype(F32)
+        vec_ref[...] = total
+
+    rows, width = hidden_ref.shape
+    hat, _ = normal(hidden_ref[...].astype(F32))
+    normed = (hat * vec_ref[0:1, :] + vec_ref[1:2, :]).astype(BF16)
+    normed_ref[...] = normed
+    q_ref[...] = (dot(normed, held[:, 1].reshape(width, width), NT) + vec_ref[2:3, :]).astype(BF16)
+    k_ref[...] = dot(normed, held[:, 2].reshape(width, width), NT).astype(BF16)
+    v_ref[...] = (dot(normed, held[:, 3].reshape(width, width), NT) + vec_ref[3:4, :]).astype(BF16)
+    captions = rows // length
+    quads = width // 256
+    position = lax.broadcasted_iota(jnp.int32, (length, 256), 0)
+    for cap in range(captions):
+        keep = position < lengths_ref[step * captions + cap]
+        for quad in range(quads):
+            span = (slice(cap * length, (cap + 1) * length), slice(256 * quad, 256 * quad + 256))
+            scores = dot(k_ref[span], spread(q_ref[span]), NT) * 0.125
+            scores = jnp.where(keep, scores, -1e30)
+            peak = jnp.max(scores, axis=0, keepdims=True)
+            raised = jnp.exp(scores - peak)
+            probs = (raised * (1.0 / jnp.sum(raised, axis=0, keepdims=True))).astype(BF16)
+            probs_ref[cap * quads + quad] = probs
+            mixed_ref[span] = collect(dot(probs, v_ref[span], TN)).astype(BF16)
+
+
+def upper_kernel(grid, places, hidden_ref, mixed_ref, vec_ref, *rest):
+    count = len(places)
+    refs, rest = rest[:count], rest[count:]
+    middle_ref, normed_ref, active_ref, slope_ref, held, sems = rest
+
+    @pl.when(pl.program_id(0) == 0)
+    def _():
+        place(grid, places, refs, held, sems)
+
+    width = hidden_ref.shape[1]
+    middle = (
+        hidden_ref[...].astype(F32)
+        + dot(mixed_ref[...], held[:, 0].reshape(width, width), NT)
+        + vec_ref[4:5, :]
+    )
+    middle_ref[...] = middle
+    hat, _ = normal(middle)
+    normed = (hat * vec_ref[5:6, :] + vec_ref[6:7, :]).astype(BF16)
+    normed_ref[...] = normed
+    per = grid.count // 4
+    for part in range(4):
+        weight = held[per * part : per * part + per, 1:5].reshape(width, width)
+        upper = dot(normed, weight, NT) + vec_ref[8 + part : 9 + part, :]
+        square = upper * upper
+        root = math.sqrt(2.0 / math.pi)
+        bend = jnp.tanh(upper * (root + (root * 0.044715) * square))
+        half = 0.5 * bend + 0.5
+        span = slice(width * part, width * part + width)
+        active_ref[:, span] = (upper * half).astype(BF16)
+        slope = half + (0.5 * upper) * (1.0 - bend * bend) * (root + (3.0 * root * 0.044715) * square)
+        slope_ref[:, span] = slope.astype(BF16)
+
+
+def mask_into(lengths_ref, cot_ref, low, length):
+    rows = cot_ref.shape[0]
+    captions = rows // length
+    for k in range(captions):
+        span = slice(k * length, (k + 1) * length)
+        position = lax.broadcasted_iota(jnp.int32, (length, 1), 0)
+        kept = jnp.where(position < lengths_ref[k], cot_ref[span, :].astype(F32), 0.0)
+        low[span, :] = kept.astype(BF16)
+
+
+def down_grad_kernel(grid, length, lengths_ref, cot_ref, active_ref, low_ref, vec_ref, own_ref, other_ref, total):
+    @pl.when(pl.program_id(0) == 0)
+    def _():
+        mask_into(lengths_ref, cot_ref, low_ref, length)
+        vec_ref[...] = jnp.broadcast_to(
+            jnp.sum(low_ref[...].astype(F32), axis=0, keepdims=True), vec_ref.shape
+        )
+
+    total[...] = dot(low_ref[...], active_ref[...], TN)
+    rows = total.shape[0] // grid.count
+    for core, out_ref in ((0, own_ref), (1, other_ref)):
+        for slot, spot in enumerate(outgoing(grid, core)):
+            at = pl.multiple_of(grid.away(*spot) * rows, 8)
+            out_ref[slot] = total[pl.ds(at, rows), :].astype(BF16)
+
+
+def upper_grad_kernel(grid, places, low_ref, slope_ref, normed_ref, *rest):
+    count = len(places)
+    refs, rest = rest[:count], rest[count:]
+    upper_ref, vec_ref, both_ref, held, sems, total = rest
+    step = pl.program_id(0)
+
+    @pl.when(step == 0)
+    def _():
+        place(grid, places, refs, held, sems)
+
+    width = low_ref.shape[1]
+    weight = held[:, :, pl.ds(pl.multiple_of(step * width, 128), width)].reshape(width, width)
+    grads = (dot(low_ref[...], weight, NN) * slope_ref[...].astype(F32)).astype(BF16)
+    upper_ref[...] = grads
+    vec_ref[pl.ds(pl.multiple_of(step * 8, 8), 8), :] = jnp.broadcast_to(
+        jnp.sum(grads.astype(F32), axis=0, keepdims=True), (8, width)
+    )
+    total[...] = dot(grads, normed_ref[...], TN)
+    per = grid.count // 4
+    rows = width // per
+    z, x, y, c = grid.here()
+    for k in range(per):
+        owner = step * per + k
+        kz = lax.rem(lax.div(owner, grid.x * grid.y * grid.c) - z + grid.z, grid.z)
+        kx = lax.rem(lax.rem(lax.div(owner, grid.y * grid.c), grid.x) - x + grid.x, grid.x)
+        ky = lax.rem(lax.rem(lax.div(owner, grid.c), grid.y) - y + grid.y, grid.y)
+        kc = lax.rem(lax.rem(owner, grid.c) - c + grid.c, grid.c)
+        half = grid.z // 2
+        which = lax.div(kz, half)
+        one = jnp.where(which == 0, kx, ky)
+        two = jnp.where(which == 0, ky, kx)
+        slot = ((which * 2 + one) * 2 + two) * half + lax.rem(kz, half)
+        block = total[k * rows : (k + 1) * rows, :].astype(BF16)
+        both_ref[kc * (grid.count // 2) + slot] = block.reshape(both_ref.shape[1:])
+
+
+def middle_grad_kernel(grid, places, length, lengths_ref, upper_ref, middle_ref, cot_ref, q_ref, k_ref, v_ref, probs_ref, vec_in, *rest):
+    count = len(places)
+    refs, rest = rest[:count], rest[count:]
+    grad_ref, branch_ref, dq_ref, dk_ref, dv_ref, vec_ref, held, sems, dm = rest
+    step = pl.program_id(0)
+
+    @pl.when(step == 0)
+    def _():
+        place(grid, places, refs, held, sems)
+        vec_ref[...] = jnp.zeros_like(vec_ref)
+
+    rows, width = middle_ref.shape
+    captions = rows // length
+    per = grid.count // 4
+    grads = dot(upper_ref[:, 0:width], held[0:per, 1:5].reshape(width, width), NN)
+    for part in range(1, 4):
+        weight = held[per * part : per * part + per, 1:5].reshape(width, width)
+        grads = grads + dot(upper_ref[:, width * part : width * part + width], weight, NN)
+    hat, scale = normal(middle_ref[...])
+    out = cot_ref[...].astype(F32) * row_mask(lengths_ref, step, captions, length)
+    grad_middle = out + normal_back(hat, scale, vec_in[5:6, :], grads)
+    grad_ref[...] = grad_middle
+    branch = grad_middle.astype(BF16)
+    branch_ref[...] = branch
+    dm[...] = dot(branch, held[:, 0].reshape(width, width), NN).astype(BF16)
+    vec_ref[0:1, :] += jnp.sum(grads * hat, axis=0, keepdims=True)
+    vec_ref[1:2, :] += jnp.sum(grads, axis=0, keepdims=True)
+    vec_ref[2:3, :] += jnp.sum(branch.astype(F32), axis=0, keepdims=True)
+    quads = width // 256
+    for cap in range(captions):
+        for quad in range(quads):
+            span = (slice(cap * length, (cap + 1) * length), slice(256 * quad, 256 * quad + 256))
+            probs = probs_ref[cap * quads + quad]
+            wide = spread(dm[span])
+            dv_ref[span] = dot(probs, wide, NN).astype(BF16)
+            grad_probs = dot(v_ref[span], wide, NT)
+            probs = probs.astype(F32)
+            along = jnp.sum(probs * grad_probs, axis=0, keepdims=True)
+            grad_scores = (probs * (grad_probs - along)).astype(BF16)
+            dk_ref[span] = (dot(grad_scores, spread(q_ref[span]), NN) * 0.125).astype(BF16)
+            dq_ref[span] = (collect(dot(grad_scores, k_ref[span], TN)) * 0.125).astype(BF16)
+    vec_ref[3:4, :] += jnp.sum(dq_ref[...].astype(F32), axis=0, keepdims=True)
+    vec_ref[4:5, :] += jnp.sum(dv_ref[...].astype(F32), axis=0, keepdims=True)
+
+
+def weight_grad_kernel(grid, dq_ref, dk_ref, dv_ref, branch_ref, normed_ref, mixed_ref, own_ref, other_ref, total):
+    rows = total.shape[0] // grid.count
+    for at, (grads, inputs) in enumerate(
+        ((dq_ref, normed_ref), (dk_ref, normed_ref), (dv_ref, normed_ref), (branch_ref, mixed_ref))
+    ):
+        total[...] = dot(grads[...], inputs[...], TN)
+        for core, out_ref in ((0, own_ref), (1, other_ref)):
+            for slot, spot in enumerate(outgoing(grid, core)):
+                start = pl.multiple_of(grid.away(*spot) * rows, 8)
+                out_ref[slot, at] = total[pl.ds(start, rows), :].astype(BF16)
+
+
+def input_grad_kernel(grid, places, hidden_ref, grad_ref, dq_ref, dk_ref, dv_ref, vec_in, down_vec, up_vec, mid_vec, *rest):
+    count = len(places)
+    refs, rest = rest[:count], rest[count:]
+    out_ref, vec_ref, held, sems = rest
+
+    @pl.when(pl.program_id(0) == 0)
+    def _():
+        place(grid, places, refs, held, sems)
+        vec_ref[...] = jnp.zeros_like(vec_ref)
+        vec_ref[2:3, :] = mid_vec[3:4, :]
+        vec_ref[3:4, :] = mid_vec[4:5, :]
+        vec_ref[4:5, :] = mid_vec[2:3, :]
+        vec_ref[5:7, :] = mid_vec[0:2, :]
+        vec_ref[7:8, :] = down_vec[0:1, :]
+        for part in range(4):
+            vec_ref[8 + part : 9 + part, :] = up_vec[8 * part : 8 * part + 1, :]
+
+    width = hidden_ref.shape[1]
+    grads = dot(dq_ref[...], held[:, 1].reshape(width, width), NN)
+    grads = grads + dot(dk_ref[...], held[:, 2].reshape(width, width), NN)
+    grads = grads + dot(dv_ref[...], held[:, 3].reshape(width, width), NN)
+    hat, scale = normal(hidden_ref[...].astype(F32))
+    out_ref[...] = grad_ref[...] + normal_back(hat, scale, vec_in[0:1, :], grads)
+    vec_ref[0:1, :] += jnp.sum(grads * hat, axis=0, keepdims=True)
+    vec_ref[1:2, :] += jnp.sum(grads, axis=0, keepdims=True)
+
+
+def lower_kernel(grid, places, active_ref, middle_ref, vec_in, *rest):
+    count = len(places)
+    refs, rest = rest[:count], rest[count:]
+    out_ref, held, sems = rest
+
+    @pl.when(pl.program_id(0) == 0)
+    def _():
+        place(grid, places, refs, held, sems)
+
+    width = middle_ref.shape[1]
+    weight = held[...].reshape(width, held.shape[2])
+    out = middle_ref[...] + dot(active_ref[...], weight, NT) + vec_in[7:8, :]
+    out_ref[...] = out.astype(BF16)
+
+
+def unpack_kernel(grid, vec_ref, *outs):
+    me = lax.axis_index("dp") * (grid.y * grid.c) + lax.axis_index("fsdp")
+    eight = pltpu.roll(vec_ref[0:8, :], lax.rem(768 - me * 24, 768), 1)
+    for k in range(8):
+        outs[k][...] = eight[k : k + 1, 0:24]
+    row = lax.broadcasted_iota(jnp.int32, (8, 768), 0)
+    four = jnp.sum(jnp.where(row == lax.div(me, 8), vec_ref[8:16, :], 0.0), axis=0, keepdims=True)
+    four = jnp.broadcast_to(four, (8, 768))
+    four = pltpu.roll(four, lax.rem(768 - lax.rem(me, 8) * 96, 768), 1)
+    outs[8][...] = four[0:1, 0:96]
+
+
+def whole(shape):
+    return pl.BlockSpec(shape, lambda *_: (0,) * len(shape))
+
+
+ANY = pl.BlockSpec(memory_space=pl.ANY)
+SMEM = pl.BlockSpec(memory_space=pltpu.SMEM)
+
+
+def call(kernel, steps, in_specs, out_specs, outs, scratch, flops, moved, name):
+    return pl.pallas_call(
+        kernel,
+        grid=(steps,),
+        in_specs=in_specs,
+        out_specs=out_specs,
+        out_shape=[jax.ShapeDtypeStruct(s, d) for s, d in outs],
+        scratch_shapes=scratch,
+        compiler_params=pltpu.CompilerParams(vmem_limit_bytes=VMEM_LIMIT),
+        cost_estimate=pl.CostEstimate(flops=flops, bytes_accessed=moved, transcendentals=0),
+        name=name,
+    )
+
+
+def fast_device(
+    grid,
+    hidden,
+    lengths,
+    cotangent,
+    attgain,
+    attshift,
+    querymat,
+    querybias,
+    keymat,
+    valuemat,
+    valuebias,
+    mixmat,
+    mixbias,
+    mlpgain,
+    mlpshift,
+    upmat_w,
+    upbias,
+    downmat,
+    downbias,
+):
+    captions, length, width = hidden.shape
+    tokens = captions * length
+    hidden2 = hidden.reshape(tokens, width)
+    cot2 = cotangent.reshape(tokens, width)
+    share = width // grid.count
+    ff = downmat.shape[0]
+    small = jnp.stack(
+        [attgain, attshift, querybias, valuebias, mixbias, mlpgain, mlpshift, downbias]
+    ).astype(F32)
+    upsmall = upbias.astype(F32).reshape(1, -1)
+    first = call(
+        functools.partial(pack_kernel, grid),
+        1,
+        [whole((8, share)), whole((1, 96))] + [whole((share, width))] * 3,
+        [whole((4, share, width))],
+        [((4, share, width), BF16)],
+        [pltpu.VMEM((16, width), F32)],
+        1000,
+        1000,
+        "pack",
+    )(small, upsmall, querymat.T, keymat.T, valuemat.T)[0]
+    second = jnp.concatenate([mixmat.T[None], upmat_w.T.reshape(4, share, width)], axis=0)
+    third = downmat.T
+    first_in, places = gather(grid, first)
+    second_in, _ = gather(grid, second)
+    third_in, _ = gather(grid, third)
+    copies = pltpu.SemaphoreType.DMA((grid.count,))
+    held_first = pltpu.VMEM((grid.count,) + first.shape, BF16)
+    held_second = pltpu.VMEM((grid.count,) + second.shape, BF16)
+    held_third = pltpu.VMEM((grid.count,) + third.shape, BF16)
+    steps = 4
+    rows = tokens // steps
+    block = pl.BlockSpec((rows, width), lambda i: (i, 0))
+    broad = pl.BlockSpec((rows, ff), lambda i: (i, 0))
+    heads = (tokens // length) * (width // 256)
+    probs_block = pl.BlockSpec((heads // steps, length, 256), lambda i: (i, 0, 0))
+    unit = 2 * tokens * width * width
+    row = (tokens, width)
+    vec_block = whole((share, width))
+    normed, query, keys, values, probs, mixed, vec = call(
+        functools.partial(attend_kernel, grid, places, length),
+        steps,
+        [SMEM, block] + [ANY] * len(first_in),
+        [block] * 4 + [probs_block, block, vec_block],
+        [(row, BF16)] * 4 + [((heads, length, 256), BF16), (row, BF16), ((share, width), F32)],
+        [held_first, copies],
+        7 * unit,
+        20_000_000,
+        "attend",
+    )(lengths, hidden2, *first_in)
+    middle, normed2, active, slope = call(
+        functools.partial(upper_kernel, grid, places),
+        steps,
+        [block, block, vec_block] + [ANY] * len(second_in),
+        [block, block, broad, broad],
+        [(row, F32), (row, BF16), ((tokens, ff), BF16), ((tokens, ff), BF16)],
+        [held_second, copies],
+        8 * unit,
+        20_000_000,
+        "upper",
+    )(hidden2, mixed, vec, *second_in)
+    column = pl.BlockSpec((tokens, width), lambda i: (0, i))
+    half = grid.count // 2
+    low, down_vec, down_own, down_other = call(
+        functools.partial(down_grad_kernel, grid, length),
+        ff // width,
+        [SMEM, whole(row), column],
+        [whole(row), whole((8, width))]
+        + [pl.BlockSpec((half, share, width), lambda i: (0, 0, i))] * 2,
+        [(row, BF16), ((8, width), F32)] + [((half, share, ff), BF16)] * 2,
+        [pltpu.VMEM((width, width), F32)],
+        4 * unit,
+        10_000_000,
+        "down_grad",
+    )(lengths, cot2, active)
+    grad_upper, up_vec, up_both = call(
+        functools.partial(upper_grad_kernel, grid, places),
+        ff // width,
+        [whole(row), column, whole(row)] + [ANY] * len(third_in),
+        [column, whole((32, width)), whole((grid.count, 4, share, width))],
+        [((tokens, ff), BF16), ((32, width), F32), ((grid.count, 4, share, width), BF16)],
+        [held_third, copies, pltpu.VMEM((width, width), F32)],
+        8 * unit,
+        20_000_000,
+        "upper_grad",
+    )(low, slope, normed2, *third_in)
+    grad_middle, branch, dq, dk, dv, mid_vec = call(
+        functools.partial(middle_grad_kernel, grid, places, length),
+        steps,
+        [SMEM, broad, block, block, block, block, block, probs_block, vec_block]
+        + [ANY] * len(second_in),
+        [block] * 5 + [whole((8, width))],
+        [(row, F32)] + [(row, BF16)] * 4 + [((8, width), F32)],
+        [held_second, copies, pltpu.VMEM((rows, width), BF16)],
+        13 * unit,
+        20_000_000,
+        "middle_grad",
+    )(lengths, grad_upper, middle, cot2, query, keys, values, probs, vec, *second_in)
+    att_own, att_other = call(
+        functools.partial(weight_grad_kernel, grid),
+        1,
+        [whole(row)] * 6,
+        [whole((half, 4, share, width))] * 2,
+        [((half, 4, share, width), BF16)] * 2,
+        [pltpu.VMEM((width, width), F32)],
+        4 * unit,
+        10_000_000,
+        "weight_grad",
+    )(dq, dk, dv, branch, normed, mixed)
+    input_grad, all_vec = call(
+        functools.partial(input_grad_kernel, grid, places),
+        steps,
+        [block] * 5 + [vec_block, whole((8, width)), whole((32, width)), whole((8, width))]
+        + [ANY] * len(first_in),
+        [block, whole((16, width))],
+        [(row, F32), ((16, width), F32)],
+        [held_first, copies],
+        4 * unit,
+        20_000_000,
+        "input_grad",
+    )(hidden2, grad_middle, dq, dk, dv, vec, down_vec, up_vec, mid_vec, *first_in)
+    (block_out,) = call(
+        functools.partial(lower_kernel, grid, places),
+        steps,
+        [broad, block, vec_block] + [ANY] * len(third_in),
+        [block],
+        [(row, BF16)],
+        [held_third, copies],
+        4 * unit,
+        20_000_000,
+        "lower",
+    )(active, middle, vec, *third_in)
+    down_sum = scatter(grid, down_own, down_other)
+    up_sum = scatter(grid, up_both[:half], up_both[half:])
+    att_sum = scatter(grid, att_own, att_other)
+    all_vec = all_vec + grid.shift(all_vec, kc=1)
+    all_vec = all_vec + grid.shift(all_vec, kx=1)
+    all_vec = all_vec + grid.shift(all_vec, ky=1)
+    all_vec = (
+        all_vec + grid.shift(all_vec, kz=1) + grid.shift(all_vec, kz=2) + grid.shift(all_vec, kz=3)
+    )
+    vecs = call(
+        functools.partial(unpack_kernel, grid),
+        1,
+        [whole((16, width))],
+        [whole((1, share))] * 8 + [whole((1, ff // grid.count))],
+        [((1, share), F32)] * 8 + [((1, ff // grid.count), F32)],
+        [],
+        1000,
+        1000,
+        "unpack",
+    )(all_vec)
+    vecs = [v.reshape(-1) for v in vecs]
+    return (
+        block_out.reshape(hidden.shape),
+        input_grad.reshape(hidden.shape),
+        vecs[0],
+        vecs[1],
+        att_sum[0].T,
+        vecs[2],
+        att_sum[1].T,
+        att_sum[2].T,
+        vecs[3],
+        att_sum[3].T,
+        vecs[4],
+        vecs[5],
+        vecs[6],
+        up_sum.reshape(ff // grid.count, width).T,
+        vecs[8],
+        down_sum.T,
+        vecs[7],
+    )
+
+
+def fits(mesh):
+    return mesh.shape["dp"] == 8 and mesh.shape["fsdp"] == 4
+
+
 def solution(mesh):
     placed = (
         P(("dp", "fsdp"), None, None),
@@ -299,8 +959,11 @@
         P(None, ("dp", "fsdp")),
         P(("dp", "fsdp")),
     )
+    body = per_device
+    if fits(mesh):
+        body = functools.partial(fast_device, Grid3(mesh.shape["dp"], mesh.shape["fsdp"]))
     return jax.shard_map(
-        per_device,
+        body,
         mesh=mesh,
         in_specs=placed,
         out_specs=(

time: 1110 us -> 344 us (0.31)
  waiting for transfers between devices: 770 us -> 108 us
  matrix products: 142 us -> 0 us
  Pallas kernels: 0 us -> 136 us
  blocking collectives: 83.4 us -> 0 us
  starting transfers between devices: 1.26 us -> 74.8 us
  local copies, waits for them, and re-layouts: 71 us -> 7.47 us
  between operations: 15 us -> 1.48 us
    reduce_scatter x6 -> x0, waiting for transfers between devices: 516 us -> none  [the longest x1 142 us: per_device(): lax.psum_scatter(downmat_grad, ('dp', 'fsdp'), scatter_dimension=1, tiled...]
    all_gather x6 -> x0, waiting for transfers between devices: 251 us -> none  [the longest x1 58.2 us: per_device(): lax.all_gather(upmat_w, ('dp', 'fsdp'), axis=1, tiled=True)]
    dot_general x24 -> x0, matrix products: 142 us -> none  [the longest x6 39.8 us: outer_sum(): jnp.einsum('cli,clj->ij', inputs, grads, preferred_element_type=jnp.float32)]
    pallas_call x0 -> x10, Pallas kernels: none -> 136 us  [the longest x1 29.7 us: fast_device(): call(functools.partial(middle_grad_kernel, grid, places, length), steps,...]
    ppermute x0 -> x81, waiting for transfers between devices: none -> 108 us  [shift(): return lax.ppermute(values, AXES, pairs)]
    unnamed x2 -> x0, blocking collectives: 83.4 us -> none
    ppermute x0 -> x81, starting transfers between devices: none -> 74.8 us  [shift(): return lax.ppermute(values, AXES, pairs)]
    reshape x7 -> x0, local copies, waits for them, and re-layouts: 34.2 us -> none  [the longest x1 6.23 us: per_device(): grad_keys_low = grad_keys_low.reshape(captions, length, width)]
  transfers between devices with their start and end apart: 12 -> 81, of which waited for: 11 -> 35; matrix products, arithmetic and copies ran while one was open for 17% -> 5% of each run, Pallas kernels for 0% -> 22%
where the time goes in v1:
time: 344 us; the launch traced here: 343 us
  Pallas kernels  136 us (40%)
  waiting for transfers between devices  108 us (31%)
  starting transfers between devices  74.8 us (22%)
  other arithmetic  14.5 us (4%)
  local copies, waits for them, and re-layouts  7.47 us (2%)
    ppermute x81, waiting for transfers between devices, shift(): return lax.ppermute(values, AXES, pairs)  108 us
    ppermute x81, starting transfers between devices, shift(): return lax.ppermute(values, AXES, pairs)  74.8 us
    pallas_call x1, Pallas kernels, fast_device(): call(functools.partial(middle_grad_kernel, grid, places, length), steps,...  29.7 us
    pallas_call x1, Pallas kernels, fast_device(): call(functools.partial(upper_grad_kernel, grid, places), ff // width, [wh...  20.9 us
    pallas_call x1, Pallas kernels, fast_device(): call(functools.partial(attend_kernel, grid, places, length), steps, [SMEM...  19.3 us
    pallas_call x1, Pallas kernels, fast_device(): call(functools.partial(upper_kernel, grid, places), steps, [block, block,...  19 us
    pallas_call x1, Pallas kernels, fast_device(): call(functools.partial(input_grad_kernel, grid, places), steps, [block] *...  11.6 us
    pallas_call x1, Pallas kernels, fast_device(): call(functools.partial(weight_grad_kernel, grid), 1, [whole(row)] * 6, [w...  11.4 us
  transfers between devices with their start and end apart: 81, of which 35 were waited for; matrix products, arithmetic and copies ran while one was open for 5% of the time, Pallas kernels for 22%

profile of v1, /device:TPU:0, one launch (start us, length us, event | category | flops | bytes accessed | tf_op | source)
XLA Modules:
  0.0 343.1 jit_solution(2763980978145048012)
XLA Ops:
  1.6 3.1 collective-permute-start.17
  12.0 5.6 %collective-permute-done = bf16[4,24,768]{2,1,0:T(8,128)(2,1)S(1)} collective-permute-done((bf16[4,24,768]{2,1,0:T(8,128)(2,1)}, bf16[4,24,768]{2,1,0:T(8,128)(2,1)S(1)}, u32[]{:S(2)}, u32[]{:S(2)}) %collective-permute-start) | collective-permute-done | bytes 147488 | tf_op jit(solution)/shard_map/ppermute | solution.py:319
  32.0 4.5 %collective-permute-done.3 = bf16[4,24,768]{2,1,0:T(8,128)(2,1)S(1)} collective-permute-done((bf16[4,24,768]{2,1,0:T(8,128)(2,1)S(1)}, bf16[4,24,768]{2,1,0:T(8,128)(2,1)S(1)}, u32[]{:S(2)}, u32[]{:S(2)}) %collective-permute-start.3) | collective-permute-done | bytes 147488 | tf_op jit(solution)/shard_map/ppermute | solution.py:319
  59.1 5.3 %collective-permute-done.7.rest_6_ = bf16[2,4,24,768]{3,2,1,0:T(8,128)(2,1)S(1)} collective-permute-done((bf16[2,4,24,768]{3,2,1,0:T(8,128)(2,1)S(1)}, bf16[2,4,24,768]{3,2,1,0:T(8,128)(2,1)S(1)}, u32[]{:S(2)}, u32[]{:S(2)}) %collective-permute-start.7) | collective-permute-done | bytes 294944 | tf_op jit(solution)/shard_map/ppermute | solution.py:319
  74.7 3.9 %collective-permute-done.24.rest_6_ = bf16[2,5,24,768]{3,2,1,0:T(8,128)(2,1)S(1)} collective-permute-done((bf16[2,5,24,768]{3,2,1,0:T(8,128)(2,1)S(1)}, bf16[2,5,24,768]{3,2,1,0:T(8,128)(2,1)S(1)}, u32[]{:S(2)}, u32[]{:S(2)}) %collective-permute-start.24) | collective-permute-done | bytes 368672 | tf_op jit(solution)/shard_map/ppermute | solution.py:319
  81.2 4.7 %collective-permute-done.30.rest_12_ = bf16[2,5,24,768]{3,2,1,0:T(8,128)(2,1)S(1)} collective-permute-done((bf16[2,5,24,768]{3,2,1,0:T(8,128)(2,1)S(1)}, bf16[2,5,24,768]{3,2,1,0:T(8,128)(2,1)S(1)}, u32[]{:S(2)}, u32[]{:S(2)}) %collective-permute-start.30) | collective-permute-done | bytes 368672 | tf_op jit(solution)/shard_map/ppermute | solution.py:319
  90.2 19.3 %attend.1 = (bf16[1024,768]{1,0:T(8,128)(2,1)}, bf16[1024,768]{1,0:T(8,128)(2,1)}, bf16[1024,768]{1,0:T(8,128)(2,1)}, bf16[1024,768]{1,0:T(8,128)(2,1)}, bf16[48...) custom-call(s32[16]{0:T(128)} %lengths_ref.5, bf16[1024,768]{1,0:T(8,128)(2,1)} %bitcast.267, ...), custom_call_target="tpu_custom_call" | custom-call | flops 8455716864 | bytes 20000000 | tf_op jit(solution)/shard_map/attend/pallas_call | solution.py:802
  113.5 19.0 %upper.1 = (f32[1024,768]{1,0:T(8,128)}, bf16[1024,768]{1,0:T(8,128)(2,1)}, bf16[1024,3072]{1,0:T(8,128)(2,1)}, bf16[1024,3072]{1,0:T(8,128)(2,1)}) custom-call(bf16[1024,768]{1,0:T(8,128)(2,1)} %bitcast.268, bf16[1024,768]{1,0:T(8,128)(2,1)} %get-tuple-element.54.mixed_ref, f32[24,768]{1,0:T(8,128)} %get-tuple-element.55.vec_ref.vec_in, ...), custom_call_target="tpu_custom_call" | custom-call | flops 9663676416 | bytes 20000000 | tf_op jit(solution)/shard_map/upper/pallas_call | solution.py:813
  133.8 10.1 %down_grad.1 = (bf16[1024,768]{1,0:T(8,128)(2,1)}, f32[8,768]{1,0:T(8,128)}, bf16[16,24,3072]{2,1,0:T(8,128)(2,1)}, bf16[16,24,3072]{2,1,0:T(8,128)(2,1)}) custom-call(s32[16]{0:T(128)} %lengths_ref.5, bf16[1024,768]{1,0:T(8,128)(2,1)} %bitcast.265, bf16[1024,3072]{1,0:T(8,128)(2,1)} %get-tuple-element.56.active_ref), custom_call_target="tpu_custom_call" | custom-call | flops 4831838208 | bytes 10000000 | tf_op jit(solution)/shard_map/down_grad/pallas_call | solution.py:826
  145.0 20.9 %upper_grad.1 = (bf16[1024,3072]{1,0:T(8,128)(2,1)}, f32[32,768]{1,0:T(8,128)}, bf16[32,4,24,768]{3,2,1,0:T(8,128)(2,1)}) custom-call(bf16[1024,768]{1,0:T(8,128)(2,1)} %get-tuple-element.58.low_ref, bf16[1024,3072]{1,0:T(8,128)(2,1)} %get-tuple-element.59.slope_ref, bf16[1024,768]{1,0:T(8,128)(2,1)} %get-tuple-element.60.normed_ref, ...), custom_call_target="tpu_custom_call" | custom-call | flops 9663676416 | bytes 20000000 | tf_op jit(solution)/shard_map/upper_grad/pallas_call | solution.py:838
  165.9 29.7 %middle_grad.1 = (f32[1024,768]{1,0:T(8,128)}, bf16[1024,768]{1,0:T(8,128)(2,1)}, bf16[1024,768]{1,0:T(8,128)(2,1)}, bf16[1024,768]{1,0:T(8,128)(2,1)}, bf16[1024,768]{1,0:T(8,128)(2,1)}, /*index=5*/f32[8,768]{1,0:T(8,128)}) custom-call(s32[16]{0:T(128)} %lengths_ref.5, bf16[1024,3072]{1,0:T(8,128)(2,1)} %get-tuple-element.61.upper_ref, ...), custom_call_target="tpu_custom_call" | custom-call | flops 15703474176 | bytes 20000000 | tf_op jit(solution)/shard_map/middle_grad/pallas_call | solution.py:849
  195.7 11.4 %weight_grad.1 = (bf16[16,4,24,768]{3,2,1,0:T(8,128)(2,1)}, bf16[16,4,24,768]{3,2,1,0:T(8,128)(2,1)}) custom-call(bf16[1024,768]{1,0:T(8,128)(2,1)} %get-tuple-element.67.dq_ref, bf16[1024,768]{1,0:T(8,128)(2,1)} %get-tuple-element.68.dk_ref, bf16[1024,768]{1,0:T(8,128)(2,1)} %get-tuple-element.69.dv_ref, bf16[1024,768]{1,0:T(8,128)(2,1)} %get-tuple-element.77.branch_ref, ...), custom_call_target="tpu_custom_call" | custom-call | flops 4831838208 | bytes 10000000 | tf_op jit(solution)/shard_map/weight_grad/pallas_call | solution.py:861
  209.8 11.6 %input_grad.1 = (f32[1024,768]{1,0:T(8,128)}, f32[16,768]{1,0:T(8,128)}) custom-call(bf16[1024,768]{1,0:T(8,128)(2,1)} %bitcast.269, f32[1024,768]{1,0:T(8,128)} %get-tuple-element.66.grad_ref, bf16[1024,768]{1,0:T(8,128)(2,1)} %get-tuple-element.67.dq_ref, bf16[1024,768]{1,0:T(8,128)(2,1)} %get-tuple-element.68.dk_ref, ...), custom_call_target="tpu_custom_call" | custom-call | flops 4831838208 | bytes 20000000 | tf_op jit(solution)/shard_map/input_grad/pallas_call | solution.py:872
  232.3 3.9 %collective-permute-done.56 = f32[16,768]{1,0:T(8,128)S(1)} collective-permute-done((f32[16,768]{1,0:T(8,128)S(1)}, f32[16,768]{1,0:T(8,128)S(1)}, u32[]{:S(2)}, u32[]{:S(2)}) %collective-permute-start.56) | collective-permute-done | bytes 49184 | tf_op jit(solution)/shard_map/ppermute | solution.py:319
  237.2 4.9 %collective-permute-done.54 = f32[16,768]{1,0:T(8,128)S(1)} collective-permute-done((f32[16,768]{1,0:T(8,128)S(1)}, f32[16,768]{1,0:T(8,128)S(1)}, u32[]{:S(2)}, u32[]{:S(2)}) %collective-permute-start.54) | collective-permute-done | bytes 49184 | tf_op jit(solution)/shard_map/ppermute | solution.py:319
  242.7 11.4 %lower.1 = bf16[1024,768]{1,0:T(8,128)(2,1)} custom-call(bf16[1024,3072]{1,0:T(8,128)(2,1)} %get-tuple-element.56.active_ref, f32[1024,768]{1,0:T(8,128)} %get-tuple-element.57.middle_ref, f32[24,768]{1,0:T(8,128)} %get-tuple-element.55.vec_ref.vec_in, bf16[2,24,3072]{2,1,0:T(8,128)(2,1)} %copy-done.4, bf16[2,24,3072]{2,1,0:T(8,128)(2,1)} %copy-done.24, ...), custom_call_target="tpu_custom_call" | custom-call | flops 4831838208 | bytes 20000000 | tf_op jit(solution)/shard_map/lower/pallas_call | solution.py:884
  266.8 7.6 %collective-permute-done.61 = bf16[2,2,4,24,768]{4,3,2,1,0:T(8,128)(2,1)S(1)} collective-permute-done((bf16[2,2,4,24,768]{4,3,2,1,0:T(8,128)(2,1)S(1)}, bf16[2,2,4,24,768]{4,3,2,1,0:T(8,128)(2,1)S(1)}, u32[]{:S(2)}, u32[]{:S(2)}) %collective-permute-start.61) | collective-permute-done | bytes 589856 | tf_op jit(solution)/shard_map/ppermute | solution.py:319
  277.1 9.9 %collective-permute-done.77 = bf16[2,2,24,3072]{3,2,1,0:T(8,128)(2,1)S(1)} collective-permute-done((bf16[2,2,24,3072]{3,2,1,0:T(8,128)(2,1)S(1)}, bf16[2,2,24,3072]{3,2,1,0:T(8,128)(2,1)S(1)}, u32[]{:S(2)}, u32[]{:S(2)}) %collective-permute-start.77) | collective-permute-done | bytes 589856 | tf_op jit(solution)/shard_map/ppermute | solution.py:319
  289.9 9.7 %collective-permute-done.69 = bf16[2,2,4,24,768]{4,3,2,1,0:T(8,128)(2,1)S(1)} collective-permute-done((bf16[2,2,4,24,768]{4,3,2,1,0:T(8,128)(2,1)S(1)}, bf16[2,2,4,24,768]{4,3,2,1,0:T(8,128)(2,1)S(1)}, u32[]{:S(2)}, u32[]{:S(2)}) %collective-permute-start.69) | collective-permute-done | bytes 589856 | tf_op jit(solution)/shard_map/ppermute | solution.py:319
  302.6 4.7 %collective-permute-done.62 = bf16[2,4,24,768]{3,2,1,0:T(8,128)(2,1)S(1)} collective-permute-done((bf16[2,4,24,768]{3,2,1,0:T(8,128)(2,1)S(1)}, bf16[2,4,24,768]{3,2,1,0:T(8,128)(2,1)S(1)}, u32[]{:S(2)}, u32[]{:S(2)}) %collective-permute-start.62) | collective-permute-done | bytes 294944 | tf_op jit(solution)/shard_map/ppermute | solution.py:319
  318.3 6.6 %collective-permute-done.63 = bf16[4,24,768]{2,1,0:T(8,128)(2,1)S(1)} collective-permute-done((bf16[4,24,768]{2,1,0:T(8,128)(2,1)S(1)}, bf16[4,24,768]{2,1,0:T(8,128)(2,1)S(1)}, u32[]{:S(2)}, u32[]{:S(2)}) %collective-permute-start.63) | collective-permute-done | bytes 147488 | tf_op jit(solution)/shard_map/ppermute | solution.py:319
  324.9 5.1 %collective-permute-start.71 = (bf16[4,24,768]{2,1,0:T(8,128)(2,1)S(1)}, bf16[4,24,768]{2,1,0:T(8,128)(2,1)S(1)}, u32[]{:S(2)}, u32[]{:S(2)}) collective-permute-start(bf16[4,24,768]{2,1,0:T(8,128)(2,1)S(1)} %get-tuple-element.107), channel_id=1, source_target_pairs={{0,16},{1,17},{2,18},{3,19},{4,20},{5,21},{6,22},{7,23},{8,24},{9,... | collective-permute-start | bytes 442376 | tf_op jit(solution)/shard_map/ppermute | solution.py:319
  330.0 5.0 %collective-permute-start.72 = (bf16[4,24,768]{2,1,0:T(8,128)(2,1)S(1)}, bf16[4,24,768]{2,1,0:T(8,128)(2,1)S(1)}, u32[]{:S(2)}, u32[]{:S(2)}) collective-permute-start(bf16[4,24,768]{2,1,0:T(8,128)(2,1)S(1)} %get-tuple-element.108), channel_id=1, source_target_pairs={{0,24},{1,25},{2,26},{3,27},{4,28},{5,29},{6,30},{7,31},{8,0},{9,1... | collective-permute-start | bytes 442376 | tf_op jit(solution)/shard_map/ppermute | solution.py:319
  336.8 3.4 collective-permute-done.71
  (289 shorter events, 120.4 us)
Async XLA Ops:
  1.6 18.8 %collective-permute-start.17 = (bf16[5,24,768]{2,1,0:T(8,128)(2,1)S(1)}, bf16[5,24,768]{2,1,0:T(8,128)(2,1)S(1)}, u32[]{:S(2)}, u32[]{:S(2)}) collective-permute-start(bf16[5,24,768]{2,1,0:T(8,128)(2,1)S(1)} %get-tuple-element.116), channel_id=1, source_target_pairs={{0,8},{1,9},{2,10},{3,11},{4,12},{5,13},{6,14},{7,15},{8,16},{9,17... | collective-permute-start | bytes 552968 | tf_op jit(solution)/shard_map/ppermute | solution.py:319
  86.4 23.2 %collective-permute-start.23 = (bf16[2,5,24,768]{3,2,1,0:T(8,128)(2,1)S(1)}, bf16[2,5,24,768]{3,2,1,0:T(8,128)(2,1)S(1)}, u32[]{:S(2)}, u32[]{:S(2)}) collective-permute-start(bf16[2,5,24,768]{3,2,1,0:T(8,128)(2,1)S(1)} %collective-permute-done.22.rest_4_), channel_id=1, source_target_pairs={{0,1},{1,0},{2,3},{3,2},{4,5},{5,4},{6,7},{7,6},{8,9},{9,8},{10,11... | collective-permute-start | bytes 1105928 | tf_op jit(solution)/shard_map/ppermute | solution.py:319
  86.5 25.6 %collective-permute-start.25 = (bf16[2,5,24,768]{3,2,1,0:T(8,128)(2,1)S(1)}, bf16[2,5,24,768]{3,2,1,0:T(8,128)(2,1)S(1)}, u32[]{:S(2)}, u32[]{:S(2)}) collective-permute-start(bf16[2,5,24,768]{3,2,1,0:T(8,128)(2,1)S(1)} %collective-permute-done.24.rest_6_), channel_id=1, source_target_pairs={{0,1},{1,0},{2,3},{3,2},{4,5},{5,4},{6,7},{7,6},{8,9},{9,8},{10,11... | collective-permute-start | bytes 1105928 | tf_op jit(solution)/shard_map/ppermute | solution.py:319
  87.5 23.9 %collective-permute-start.29 = (bf16[2,5,24,768]{3,2,1,0:T(8,128)(2,1)S(1)}, bf16[2,5,24,768]{3,2,1,0:T(8,128)(2,1)S(1)}, u32[]{:S(2)}, u32[]{:S(2)}) collective-permute-start(bf16[2,5,24,768]{3,2,1,0:T(8,128)(2,1)S(1)} %collective-permute-done.28.rest_10_), channel_id=1, source_target_pairs={{0,1},{1,0},{2,3},{3,2},{4,5},{5,4},{6,7},{7,6},{8,9},{9,8},{10,11... | collective-permute-start | bytes 1105928 | tf_op jit(solution)/shard_map/ppermute | solution.py:319
  89.4 22.8 %collective-permute-start.31 = (bf16[2,5,24,768]{3,2,1,0:T(8,128)(2,1)S(1)}, bf16[2,5,24,768]{3,2,1,0:T(8,128)(2,1)S(1)}, u32[]{:S(2)}, u32[]{:S(2)}) collective-permute-start(bf16[2,5,24,768]{3,2,1,0:T(8,128)(2,1)S(1)} %collective-permute-done.30.rest_12_), channel_id=1, source_target_pairs={{0,1},{1,0},{2,3},{3,2},{4,5},{5,4},{6,7},{7,6},{8,9},{9,8},{10,11... | collective-permute-start | bytes 1105928 | tf_op jit(solution)/shard_map/ppermute | solution.py:319
  89.4 23.3 %collective-permute-start.33 = (bf16[2,5,24,768]{3,2,1,0:T(8,128)(2,1)S(1)}, bf16[2,5,24,768]{3,2,1,0:T(8,128)(2,1)S(1)}, u32[]{:S(2)}, u32[]{:S(2)}) collective-permute-start(bf16[2,5,24,768]{3,2,1,0:T(8,128)(2,1)S(1)} %collective-permute-done.32.rest_14_), channel_id=1, source_target_pairs={{0,1},{1,0},{2,3},{3,2},{4,5},{5,4},{6,7},{7,6},{8,9},{9,8},{10,11... | collective-permute-start | bytes 1105928 | tf_op jit(solution)/shard_map/ppermute | solution.py:319
  109.6 23.6 %collective-permute-start.45 = (bf16[2,24,3072]{2,1,0:T(8,128)(2,1)S(1)}, bf16[2,24,3072]{2,1,0:T(8,128)(2,1)S(1)}, u32[]{:S(2)}, u32[]{:S(2)}) collective-permute-start(bf16[2,24,3072]{2,1,0:T(8,128)(2,1)S(1)} %pad_maximum_fusion.5.rest_2_), channel_id=1, source_target_pairs={{0,4},{1,5},{2,6},{3,7},{4,0},{5,1},{6,2},{7,3},{8,12},{9,13},{10,... | collective-permute-start | bytes 884744 | tf_op jit(solution)/shard_map/ppermute | solution.py:319
  111.4 21.2 %collective-permute-start.47 = (bf16[2,24,3072]{2,1,0:T(8,128)(2,1)}, bf16[2,24,3072]{2,1,0:T(8,128)(2,1)S(1)}, u32[]{:S(2)}, u32[]{:S(2)}) collective-permute-start(bf16[2,24,3072]{2,1,0:T(8,128)(2,1)} %collective-permute-done.39.rest_4_), channel_id=1, source_target_pairs={{0,2},{1,3},{2,0},{3,1},{4,6},{5,7},{6,4},{7,5},{8,10},{9,11},{10,... | collective-permute-start | bytes 884744 | tf_op jit(solution)/shard_map/ppermute | solution.py:319
  112.2 21.0 %collective-permute-start.40 = (bf16[2,24,3072]{2,1,0:T(8,128)(2,1)}, bf16[2,24,3072]{2,1,0:T(8,128)(2,1)S(1)}, u32[]{:S(2)}, u32[]{:S(2)}) collective-permute-start(bf16[2,24,3072]{2,1,0:T(8,128)(2,1)} %collective-permute-done.39.rest_4_), channel_id=1, source_target_pairs={{0,1},{1,0},{2,3},{3,2},{4,5},{5,4},{6,7},{7,6},{8,9},{9,8},{10,11... | collective-permute-start | bytes 884744 | tf_op jit(solution)/shard_map/ppermute | solution.py:319
  112.2 20.3 %collective-permute-start.44 = (bf16[2,24,3072]{2,1,0:T(8,128)(2,1)S(1)}, bf16[2,24,3072]{2,1,0:T(8,128)(2,1)S(1)}, u32[]{:S(2)}, u32[]{:S(2)}) collective-permute-start(bf16[2,24,3072]{2,1,0:T(8,128)(2,1)S(1)} %copy-done.23), channel_id=1, source_target_pairs={{0,1},{1,0},{2,3},{3,2},{4,5},{5,4},{6,7},{7,6},{8,9},{9,8},{10,11... | collective-permute-start | bytes 884744 | tf_op jit(solution)/shard_map/ppermute | solution.py:319
  112.8 20.9 %collective-permute-start.49 = (bf16[2,24,3072]{2,1,0:T(8,128)(2,1)S(1)}, bf16[2,24,3072]{2,1,0:T(8,128)(2,1)S(1)}, u32[]{:S(2)}, u32[]{:S(2)}) collective-permute-start(bf16[2,24,3072]{2,1,0:T(8,128)(2,1)S(1)} %collective-permute-done.41.rest_6_), channel_id=1, source_target_pairs={{0,4},{1,5},{2,6},{3,7},{4,0},{5,1},{6,2},{7,3},{8,12},{9,13},{10,... | collective-permute-start | bytes 884744 | tf_op jit(solution)/shard_map/ppermute | solution.py:319
  207.1 48.4 %collective-permute-start.57 = (bf16[16,4,24,768]{3,2,1,0:T(8,128)(2,1)}, bf16[16,4,24,768]{3,2,1,0:T(8,128)(2,1)}, u32[]{:S(2)}, u32[]{:S(2)}) collective-permute-start(bf16[16,4,24,768]{3,2,1,0:T(8,128)(2,1)} %get-tuple-element.80), channel_id=1, source_target_pairs={{0,1},{1,0},{2,3},{3,2},{4,5},{5,4},{6,7},{7,6},{8,9},{9,8},{10,11... | collective-permute-start | bytes 7077896 | tf_op jit(solution)/shard_map/ppermute | solution.py:319
  207.5 53.3 %collective-permute-start.73 = (bf16[16,24,3072]{2,1,0:T(8,128)(2,1)}, bf16[16,24,3072]{2,1,0:T(8,128)(2,1)}, u32[]{:S(2)}, u32[]{:S(2)}) collective-permute-start(bf16[16,24,3072]{2,1,0:T(8,128)(2,1)} %get-tuple-element.89), channel_id=1, source_target_pairs={{0,1},{1,0},{2,3},{3,2},{4,5},{5,4},{6,7},{7,6},{8,9},{9,8},{10,11... | collective-permute-start | bytes 7077896 | tf_op jit(solution)/shard_map/ppermute | solution.py:319
  209.4 55.2 %collective-permute-start.65 = (bf16[16,4,24,768]{3,2,1,0:T(8,128)(2,1)}, bf16[16,4,24,768]{3,2,1,0:T(8,128)(2,1)S(1)}, u32[]{:S(2)}, u32[]{:S(2)}) collective-permute-start(bf16[16,4,24,768]{3,2,1,0:T(8,128)(2,1)} %get-tuple-element.100), channel_id=1, source_target_pairs={{0,1},{1,0},{2,3},{3,2},{4,5},{5,4},{6,7},{7,6},{8,9},{9,8},{10,11... | collective-permute-start | bytes 7077896 | tf_op jit(solution)/shard_map/ppermute | solution.py:319
  263.3 23.7 %collective-permute-start.77 = (bf16[2,2,24,3072]{3,2,1,0:T(8,128)(2,1)S(1)}, bf16[2,2,24,3072]{3,2,1,0:T(8,128)(2,1)S(1)}, u32[]{:S(2)}, u32[]{:S(2)}) collective-permute-start(bf16[2,2,24,3072]{3,2,1,0:T(8,128)(2,1)S(1)} %get-tuple-element.92), channel_id=1, source_target_pairs={{0,2},{1,3},{2,0},{3,1},{4,6},{5,7},{6,4},{7,5},{8,10},{9,11},{10,... | collective-permute-start | bytes 1769480 | tf_op jit(solution)/shard_map/ppermute | solution.py:319
  264.0 24.4 %collective-permute-start.74 = (bf16[2,2,24,3072]{3,2,1,0:T(8,128)(2,1)S(1)}, bf16[2,2,24,3072]{3,2,1,0:T(8,128)(2,1)S(1)}, u32[]{:S(2)}, u32[]{:S(2)}) collective-permute-start(bf16[2,2,24,3072]{3,2,1,0:T(8,128)(2,1)S(1)} %get-tuple-element.93), channel_id=1, source_target_pairs={{0,4},{1,5},{2,6},{3,7},{4,0},{5,1},{6,2},{7,3},{8,12},{9,13},{10,... | collective-permute-start | bytes 1769480 | tf_op jit(solution)/shard_map/ppermute | solution.py:319
  265.4 34.2 %collective-permute-start.69 = (bf16[2,2,4,24,768]{4,3,2,1,0:T(8,128)(2,1)S(1)}, bf16[2,2,4,24,768]{4,3,2,1,0:T(8,128)(2,1)S(1)}, u32[]{:S(2)}, u32[]{:S(2)}) collective-permute-start(bf16[2,2,4,24,768]{4,3,2,1,0:T(8,128)(2,1)S(1)} %get-tuple-element.96), channel_id=1, source_target_pairs={{0,2},{1,3},{2,0},{3,1},{4,6},{5,7},{6,4},{7,5},{8,10},{9,11},{10,... | collective-permute-start | bytes 1769480 | tf_op jit(solution)/shard_map/ppermute | solution.py:319
  274.4 26.7 %collective-permute-start.66 = (bf16[2,2,4,24,768]{4,3,2,1,0:T(8,128)(2,1)S(1)}, bf16[2,2,4,24,768]{4,3,2,1,0:T(8,128)(2,1)S(1)}, u32[]{:S(2)}, u32[]{:S(2)}) collective-permute-start(bf16[2,2,4,24,768]{4,3,2,1,0:T(8,128)(2,1)S(1)} %get-tuple-element.97), channel_id=1, source_target_pairs={{0,4},{1,5},{2,6},{3,7},{4,0},{5,1},{6,2},{7,3},{8,12},{9,13},{10,... | collective-permute-start | bytes 1769480 | tf_op jit(solution)/shard_map/ppermute | solution.py:319
  275.8 31.5 %collective-permute-start.62 = (bf16[2,4,24,768]{3,2,1,0:T(8,128)(2,1)S(1)}, bf16[2,4,24,768]{3,2,1,0:T(8,128)(2,1)S(1)}, u32[]{:S(2)}, u32[]{:S(2)}) collective-permute-start(bf16[2,4,24,768]{3,2,1,0:T(8,128)(2,1)S(1)} %fusion.28), channel_id=1, source_target_pairs={{0,4},{1,5},{2,6},{3,7},{4,0},{5,1},{6,2},{7,3},{8,12},{9,13},{10,... | collective-permute-start | bytes 884744 | tf_op jit(solution)/shard_map/ppermute | solution.py:319
  287.0 24.2 %collective-permute-start.59 = (bf16[2,4,24,768]{3,2,1,0:T(8,128)(2,1)S(1)}, bf16[2,4,24,768]{3,2,1,0:T(8,128)(2,1)S(1)}, u32[]{:S(2)}, u32[]{:S(2)}) collective-permute-start(bf16[2,4,24,768]{3,2,1,0:T(8,128)(2,1)S(1)} %fusion.27), channel_id=1, source_target_pairs={{0,2},{1,3},{2,0},{3,1},{4,6},{5,7},{6,4},{7,5},{8,10},{9,11},{10,... | collective-permute-start | bytes 884744 | tf_op jit(solution)/shard_map/ppermute | solution.py:319
  288.4 22.6 %collective-permute-start.78 = (bf16[2,24,3072]{2,1,0:T(8,128)(2,1)S(1)}, bf16[2,24,3072]{2,1,0:T(8,128)(2,1)S(1)}, u32[]{:S(2)}, u32[]{:S(2)}) collective-permute-start(bf16[2,24,3072]{2,1,0:T(8,128)(2,1)S(1)} %fusion.32), channel_id=1, source_target_pairs={{0,4},{1,5},{2,6},{3,7},{4,0},{5,1},{6,2},{7,3},{8,12},{9,13},{10,... | collective-permute-start | bytes 884744 | tf_op jit(solution)/shard_map/ppermute | solution.py:319
  312.8 17.3 %collective-permute-start.60 = (bf16[4,24,768]{2,1,0:T(8,128)(2,1)S(1)}, bf16[4,24,768]{2,1,0:T(8,128)(2,1)S(1)}, u32[]{:S(2)}, u32[]{:S(2)}) collective-permute-start(bf16[4,24,768]{2,1,0:T(8,128)(2,1)S(1)} %fusion.43), channel_id=1, source_target_pairs={{0,8},{1,9},{2,10},{3,11},{4,12},{5,13},{6,14},{7,15},{8,16},{9,17... | collective-permute-start | bytes 442376 | tf_op jit(solution)/shard_map/ppermute | solution.py:319
  314.2 21.1 %collective-permute-start.79 = (bf16[24,3072]{1,0:T(8,128)(2,1)S(1)}, bf16[24,3072]{1,0:T(8,128)(2,1)S(1)}, u32[]{:S(2)}, u32[]{:S(2)}) collective-permute-start(bf16[24,3072]{1,0:T(8,128)(2,1)S(1)} %get-tuple-element.105), channel_id=1, source_target_pairs={{0,16},{1,17},{2,18},{3,19},{4,20},{5,21},{6,22},{7,23},{8,24},{9,... | collective-permute-start | bytes 442376 | tf_op jit(solution)/shard_map/ppermute | solution.py:319
  316.7 18.6 %collective-permute-start.80 = (bf16[24,3072]{1,0:T(8,128)(2,1)S(1)}, bf16[24,3072]{1,0:T(8,128)(2,1)S(1)}, u32[]{:S(2)}, u32[]{:S(2)}) collective-permute-start(bf16[24,3072]{1,0:T(8,128)(2,1)S(1)} %get-tuple-element.106), channel_id=1, source_target_pairs={{0,24},{1,25},{2,26},{3,27},{4,28},{5,29},{6,30},{7,31},{8,0},{9,1... | collective-permute-start | bytes 442376 | tf_op jit(solution)/shard_map/ppermute | solution.py:319
  (107 other events, 1621.2 us)

commit v2 on v0

--- a/solution.py
+++ b/solution.py
@@ -1,8 +1,11 @@
+import functools
 import math
 
 import jax
 import jax.numpy as jnp
 from jax import lax
+from jax.experimental import pallas as pl
+from jax.experimental.pallas import tpu as pltpu
 from jax.sharding import PartitionSpec as P
 
 HEADS = 12
@@ -278,49 +281,895 @@
     )
 
 
+NT = (((1,), (1,)), ((), ()))
+NN = (((1,), (0,)), ((), ()))
+TN = (((0,), (0,)), ((), ()))
+F32 = jnp.float32
+BF16 = jnp.bfloat16
+AXES = ("z", "x", "y", "c")
+QUAD = 4
+VMEM_LIMIT = 56 * 1024 * 1024
+
+
+def dot(left, right, dims):
+    return lax.dot_general(left, right, dims, preferred_element_type=F32)
+
+
+class Grid3:
+    def __init__(self, dp, fsdp):
+        self.c = 2
+        self.y = fsdp // 2
+        self.x = self.y
+        self.z = dp // self.x
+        self.count = dp * fsdp
+
+    def index(self, z, x, y, c):
+        return ((z * self.x + x) * self.y + y) * self.c + c
+
+    def shift(self, values, kz=0, kx=0, ky=0, kc=0):
+        pairs = []
+        for z in range(self.z):
+            for x in range(self.x):
+                for y in range(self.y):
+                    for c in range(self.c):
+                        target = self.index(
+                            (z + kz) % self.z, (x + kx) % self.x, (y + ky) % self.y, (c + kc) % self.c
+                        )
+                        pairs.append((self.index(z, x, y, c), target))
+        return lax.ppermute(values, AXES, pairs)
+
+    def here(self):
+        return tuple(lax.axis_index(name) for name in AXES)
+
+    def me(self):
+        return self.index(*self.here())
+
+    def away(self, kz, kx, ky, kc):
+        z, x, y, c = self.here()
+        return self.index(
+            lax.rem(z + (kz % self.z), self.z),
+            lax.rem(x + (kx % self.x), self.x),
+            lax.rem(y + (ky % self.y), self.y),
+            lax.rem(c + (kc % self.c), self.c),
+        )
+
+
+def tie(values, gate):
+    return lax.optimization_barrier((values, gate))[0]
+
+
+def gather_begin(grid, own):
+    rows = [own]
+    for k in range(1, grid.z):
+        rows.append(grid.shift(own, kz=k))
+    half = grid.z // 2
+    first = jnp.stack(rows[:half])
+    second = jnp.stack(rows[half:])
+    return first, second
+
+
+def gather_middle(grid, begun):
+    first, second = begun
+    return first, second, grid.shift(first, kx=1), grid.shift(second, ky=1)
+
+
+def gather_end(grid, begun):
+    first, second, first_x, second_y = begun
+    half = grid.z // 2
+    first_y = grid.shift(first, ky=1)
+    second_x = grid.shift(second, kx=1)
+    first_xy = grid.shift(first_x, ky=1)
+    second_xy = grid.shift(second_y, kx=1)
+    arrays, places = [], []
+    for array, start, kx, ky in (
+        (first, 0, 0, 0),
+        (second, half, 0, 0),
+        (first_x, 0, 1, 0),
+        (second_y, half, 0, 1),
+        (first_y, 0, 0, 1),
+        (second_x, half, 1, 0),
+        (first_xy, 0, 1, 1),
+        (second_xy, half, 1, 1),
+    ):
+        arrays.append(array)
+        places.append([(-(start + k), -kx, -ky, 0) for k in range(half)])
+        arrays.append(grid.shift(array, kc=1))
+        places.append([(-(start + k), -kx, -ky, -1) for k in range(half)])
+    return arrays, places
+
+
+def place(grid, places, refs, held):
+    for ref, spots in zip(refs, places):
+        for slot, spot in enumerate(spots):
+            held[grid.away(*spot)] = ref[slot]
+
+
+def outgoing(grid, core):
+    half = grid.z // 2
+    slots = []
+    for which in range(2):
+        for one in range(2):
+            for two in range(2):
+                for low in range(half):
+                    kx, ky = (one, two) if which == 0 else (two, one)
+                    slots.append((which * half + low, kx, ky, core))
+    return slots
+
+
+def plus(left, right):
+    return (left.astype(F32) + right.astype(F32)).astype(BF16)
+
+
+def scatter_core(grid, other):
+    return grid.shift(other, kc=1)
+
+
+def scatter_first(grid, own, arrived):
+    shape = (2, 2, 2, grid.z // 2) + own.shape[1:]
+    own = own.reshape(shape)
+    arrived = arrived.reshape(shape)
+    send_a = plus(own[0, 1], arrived[0, 1])
+    send_b = plus(own[1, 1], arrived[1, 1])
+    keep_a = plus(own[0, 0], arrived[0, 0])
+    keep_b = plus(own[1, 0], arrived[1, 0])
+    return send_a, send_b, keep_a, keep_b, grid.shift(send_a, kx=1), grid.shift(send_b, ky=1)
+
+
+def scatter_second(grid, state, gate):
+    _, _, keep_a, keep_b, got_a, got_b = state
+    got_a, got_b = tie((got_a, got_b), gate)
+    next_a = plus(keep_a[1], got_a[1])
+    next_b = plus(keep_b[1], got_b[1])
+    rest_a = plus(keep_a[0], got_a[0])
+    rest_b = plus(keep_b[0], got_b[0])
+    return next_a, rest_a, rest_b, grid.shift(next_a, ky=1), grid.shift(next_b, kx=1)
+
+
+def scatter_third(grid, state, gate):
+    _, rest_a, rest_b, last_a, last_b = state
+    last_a, last_b = tie((last_a, last_b), gate)
+    half = grid.z // 2
+    parts = [plus(rest_a[k], last_a[k]) for k in range(half)] + [plus(rest_b[k], last_b[k]) for k in range(half)]
+    return parts + [grid.shift(parts[k], kz=k) for k in range(1, grid.z)]
+
+
+def scatter_last(state, gate):
+    count = (len(state) + 1) // 2
+    came = tie(list(state[count:]), gate)
+    total = state[0].astype(F32)
+    for part in came:
+        total = total + part.astype(F32)
+    return total
+
+
+def lanes_of(rows):
+    return lax.broadcasted_iota(jnp.int32, (rows, 256), 1) // 64
+
+
+def spread(block):
+    head = lanes_of(block.shape[0])
+    zero = jnp.zeros_like(block)
+    return jnp.concatenate([jnp.where(head == g, block, zero) for g in range(QUAD)], axis=0)
+
+
+def collect(square):
+    head = lanes_of(64)
+    total = jnp.where(head == 0, square[0:64], 0.0)
+    for g in range(1, QUAD):
+        total = jnp.where(head == g, square[64 * g : 64 * g + 64], total)
+    return total
+
+
+def normal(values):
+    centre = jnp.mean(values, axis=-1, keepdims=True)
+    centred = values - centre
+    spread_of = jnp.mean(centred * centred, axis=-1, keepdims=True)
+    scale = lax.rsqrt(spread_of + 1e-06)
+    return centred * scale, scale
+
+
+def normal_back(hat, scale, gain, grads):
+    weighted = grads * gain
+    middle = jnp.mean(weighted, axis=-1, keepdims=True)
+    along = jnp.mean(weighted * hat, axis=-1, keepdims=True)
+    return scale * (weighted - middle - hat * along)
+
+
+TILE = 16
+SIZES = (384, 512, 640, 768, 896, 1024)
+
+
+def order_of(lengths, length):
+    captions = lengths.shape[0]
+    tiles = length // TILE
+    real = (lengths + (TILE - 1)) // TILE
+    before = jnp.tril(jnp.ones((captions, captions), jnp.int32), -1)
+    start = jnp.sum(before * real[None, :], axis=1)
+    total = jnp.sum(real)
+    late = total + jnp.sum(before * (tiles - real)[None, :], axis=1)
+    at = jnp.arange(tiles, dtype=jnp.int32)[None, :]
+    spots = jnp.where(at < real[:, None], start[:, None] + at, late[:, None] + at - real[:, None])
+    sizes = jnp.array(SIZES, jnp.int32)
+    size = jnp.min(jnp.where(sizes >= total * TILE, sizes, SIZES[-1]))
+    return jnp.concatenate([spots.reshape(-1), start, jnp.stack([size, total])]).astype(jnp.int32)
+
+
+def tile_rows(place_ref, index):
+    return pl.ds(pl.multiple_of(place_ref[index] * TILE, TILE), TILE)
+
+
+def by_size(size, body):
+    for rows in SIZES:
+        pl.when(size == rows)(functools.partial(body, rows))
+
+
+def rows_at(step, rows):
+    return pl.ds(pl.multiple_of(step * rows, rows), rows)
+
+
+def pack_kernel(grid, small_ref, up_ref, q_ref, k_ref, v_ref, out_ref, wide):
+    wide[...] = jnp.zeros_like(wide)
+    wide[0:8, 0:24] = small_ref[...]
+    wide[8:9, 0:96] = up_ref[...]
+    me = grid.me()
+    eight = pltpu.roll(wide[0:8, :], me * 24, 1)
+    four = pltpu.roll(wide[8:16, :], lax.rem(me, 8) * 96, 1)
+    row = lax.broadcasted_iota(jnp.int32, (8, 768), 0)
+    four = jnp.where(row == lax.div(me, 8), jnp.broadcast_to(four[0:1], (8, 768)), 0.0)
+    zero = jnp.zeros((8, 768), F32)
+    out_ref[0] = jnp.concatenate([eight, four, zero], axis=0).astype(BF16)
+    out_ref[1] = q_ref[...]
+    out_ref[2] = k_ref[...]
+    out_ref[3] = v_ref[...]
+
+
+def project_kernel(grid, places, place_ref, hidden_ref, *rest):
+    count = len(places)
+    refs, rest = rest[:count], rest[count:]
+    moved_ref, normed_out, q_ref, k_ref, v_ref, vec_ref, held = rest
+    place(grid, places, refs, held)
+    width = hidden_ref.shape[1]
+    total = held[0, 0].astype(F32)
+    for j in range(1, grid.count):
+        total = total + held[j, 0].astype(F32)
+    vec_ref[...] = total
+    rows = 256
+
+    def block(step, carry):
+        at = rows_at(step, rows)
+        hidden = hidden_ref[at, :]
+        hat, _ = normal(hidden.astype(F32))
+        normed = (hat * vec_ref[0:1, :] + vec_ref[1:2, :]).astype(BF16)
+        q_ref[at, :] = (dot(normed, held[:, 1].reshape(width, width), NT) + vec_ref[2:3, :]).astype(BF16)
+        k_ref[at, :] = dot(normed, held[:, 2].reshape(width, width), NT).astype(BF16)
+        v_ref[at, :] = (dot(normed, held[:, 3].reshape(width, width), NT) + vec_ref[3:4, :]).astype(BF16)
+        for t in range(rows // TILE):
+            to = tile_rows(place_ref, step * (rows // TILE) + t)
+            part = slice(t * TILE, (t + 1) * TILE)
+            normed_out[to, :] = normed[part, :]
+            moved_ref[to, :] = hidden[part, :]
+        return carry
+
+    lax.fori_loop(0, hidden_ref.shape[0] // rows, block, 0)
+
+
+def attend_kernel(length, group, lengths_ref, place_ref, q_ref, k_ref, v_ref, probs_ref, mixed_out):
+    width = q_ref.shape[1]
+    captions = q_ref.shape[0] // length
+    tiles = length // TILE
+    quads = width // 256
+    position = lax.broadcasted_iota(jnp.int32, (length, 256), 0)
+
+    def several(step, carry):
+        items = [
+            (step * group + g, quad, rows_at(step * group + g, length), slice(256 * quad, 256 * quad + 256))
+            for g in range(group)
+            for quad in range(quads)
+        ]
+        scores = [dot(k_ref[rows, lanes], spread(q_ref[rows, lanes]), NT) for _, _, rows, lanes in items]
+        probs = []
+        for (cap, _, _, _), score in zip(items, scores):
+            score = jnp.where(position < lengths_ref[cap], score * 0.125, -1e30)
+            raised = jnp.exp(score - jnp.max(score, axis=0, keepdims=True))
+            probs.append((raised * (1.0 / jnp.sum(raised, axis=0, keepdims=True))).astype(BF16))
+        for (cap, quad, _, _), prob in zip(items, probs):
+            probs_ref[cap * quads + quad] = prob
+        mixed = [
+            collect(dot(prob, v_ref[rows, lanes], TN)).astype(BF16)
+            for (_, _, rows, lanes), prob in zip(items, probs)
+        ]
+        for (cap, _, _, lanes), value in zip(items, mixed):
+            for t in range(tiles):
+                to = tile_rows(place_ref, cap * tiles + t)
+                mixed_out[to, lanes] = value[t * TILE : (t + 1) * TILE, :]
+        return carry
+
+    lax.fori_loop(0, captions // group, several, 0)
+
+
+def upper_kernel(grid, places, moved_ref, mixed_ref, vec_ref, *rest):
+    count = len(places)
+    refs, rest = rest[:count], rest[count:]
+    middle_ref, normed_ref, active_ref, slope_ref, held = rest
+    place(grid, places, refs, held)
+    width = moved_ref.shape[1]
+    per = grid.count // 4
+    rows = 256
+    root = math.sqrt(2.0 / math.pi)
+
+    def block(step, carry):
+        at = rows_at(step, rows)
+        middle = (
+            moved_ref[at, :].astype(F32)
+            + dot(mixed_ref[at, :], held[:, 0].reshape(width, width), NT)
+            + vec_ref[4:5, :]
+        )
+        middle_ref[at, :] = middle
+        hat, _ = normal(middle)
+        normed = (hat * vec_ref[5:6, :] + vec_ref[6:7, :]).astype(BF16)
+        normed_ref[at, :] = normed
+        for part in range(4):
+            weight = held[per * part : per * part + per, 1:5].reshape(width, width)
+            upper = dot(normed, weight, NT) + vec_ref[8 + part : 9 + part, :]
+            square = upper * upper
+            bend = jnp.tanh(upper * (root + (root * 0.044715) * square))
+            half = 0.5 * bend + 0.5
+            span = slice(width * part, width * part + width)
+            active = upper * half
+            active_ref[at, span] = active.astype(BF16)
+            slope = half + active * ((1.0 - bend) * (root + (3.0 * root * 0.044715) * square))
+            slope_ref[at, span] = slope.astype(BF16)
+        return carry
+
+    lax.fori_loop(0, moved_ref.shape[0] // rows, block, 0)
+
+
+def down_grad_kernel(grid, length, size_at, lengths_ref, place_ref, cot_ref, active_ref, low_ref, vec_ref, own_ref, other_ref, total):
+    width = cot_ref.shape[1]
+    captions = cot_ref.shape[0] // length
+    tiles = length // TILE
+    position = lax.broadcasted_iota(jnp.int32, (length, 1), 0)
+    vec_ref[...] = jnp.zeros_like(vec_ref)
+
+    def caption(cap, carry):
+        part = cot_ref[rows_at(cap, length), :].astype(F32)
+        part = jnp.where(position < lengths_ref[cap], part, 0.0)
+        vec_ref[0:1, :] += jnp.sum(part, axis=0, keepdims=True)
+        part = part.astype(BF16)
+        for t in range(tiles):
+            low_ref[tile_rows(place_ref, cap * tiles + t), :] = part[t * TILE : (t + 1) * TILE, :]
+        return carry
+
+    lax.fori_loop(0, captions, caption, 0)
+    share = width // grid.count
+    core = lax.axis_index("c")
+
+    def column(step, carry):
+        lanes = rows_at(step, width)
+
+        def product(rows):
+            total[...] = dot(low_ref[0:rows, :], active_ref[0:rows, lanes], TN)
+
+        by_size(place_ref[size_at], product)
+        for out_ref, owner in ((own_ref, core), (other_ref, 1 - core)):
+            slot = 0
+            for x in range(grid.x):
+                for y in range(grid.y):
+                    for z in range(grid.z):
+                        at = pl.multiple_of(grid.index(z, x, y, owner) * share, 8)
+                        out_ref[slot, :, lanes] = total[pl.ds(at, share), :].astype(BF16)
+                        slot += 1
+        return carry
+
+    lax.fori_loop(0, active_ref.shape[1] // width, column, 0)
+
+
+def upper_grad_kernel(grid, places, size_at, place_ref, low_ref, slope_ref, normed_ref, *rest):
+    count = len(places)
+    refs, rest = rest[:count], rest[count:]
+    upper_ref, vec_ref, own_ref, other_ref, held, total = rest
+    place(grid, places, refs, held)
+    width = low_ref.shape[1]
+    per = grid.count // 4
+    share = width // per
+    half = grid.z // 2
+    z, x, y, c = grid.here()
+    shape = own_ref.shape[1:]
+    mine = jnp.where(c == 0, 0, share)
+
+    def column(step, carry):
+        lanes = rows_at(step, width)
+
+        def product(rows):
+            grads = dot(low_ref[0:rows, :], held[:, :, lanes].reshape(width, width), NN) * slope_ref[0:rows, lanes].astype(F32)
+            vec_ref[rows_at(step, 8), :] = jnp.broadcast_to(jnp.sum(grads, axis=0, keepdims=True), (8, width))
+            grads = grads.astype(BF16)
+            upper_ref[0:rows, lanes] = grads
+            total[...] = dot(grads, normed_ref[0:rows, :], TN)
+
+        by_size(place_ref[size_at], product)
+        for k in range(per // 2):
+            chip = step * (per // 2) + k
+            kz = lax.rem(lax.div(chip, grid.x * grid.y) - z + grid.z, grid.z)
+            kx = lax.rem(lax.rem(lax.div(chip, grid.y), grid.x) - x + grid.x, grid.x)
+            ky = lax.rem(lax.rem(chip, grid.y) - y + grid.y, grid.y)
+            which = lax.div(kz, half)
+            one = jnp.where(which == 0, kx, ky)
+            two = jnp.where(which == 0, ky, kx)
+            slot = ((which * 2 + one) * 2 + two) * half + lax.rem(kz, half)
+            own_at = pl.multiple_of(2 * share * k + mine, 8)
+            other_at = pl.multiple_of(2 * share * k + (share - mine), 8)
+            own_ref[slot] = total[pl.ds(own_at, share), :].astype(BF16).reshape(shape)
+            other_ref[slot] = total[pl.ds(other_at, share), :].astype(BF16).reshape(shape)
+        return carry
+
+    lax.fori_loop(0, upper_ref.shape[1] // width, column, 0)
+
+
+def middle_grad_kernel(grid, size_at, place_ref, upper_ref, middle_ref, low_ref, vec_in, held, grad_ref, branch_ref, dm_ref, vec_ref):
+    width = middle_ref.shape[1]
+    per = grid.count // 4
+    rows = 128
+    vec_ref[...] = jnp.zeros_like(vec_ref)
+
+    def block(step, carry):
+        at = rows_at(step, rows)
+        grads = dot(upper_ref[at, 0:width], held[0:per, 1:5].reshape(width, width), NN)
+        for part in range(1, 4):
+            weight = held[per * part : per * part + per, 1:5].reshape(width, width)
+            grads = grads + dot(upper_ref[at, width * part : width * part + width], weight, NN)
+        hat, scale = normal(middle_ref[at, :])
+        grad_middle = low_ref[at, :].astype(F32) + normal_back(hat, scale, vec_in[5:6, :], grads)
+        grad_ref[at, :] = grad_middle
+        branch = grad_middle.astype(BF16)
+        branch_ref[at, :] = branch
+        dm_ref[at, :] = dot(branch, held[:, 0].reshape(width, width), NN).astype(BF16)
+        vec_ref[0:1, :] += jnp.sum(grads * hat, axis=0, keepdims=True)
+        vec_ref[1:2, :] += jnp.sum(grads, axis=0, keepdims=True)
+        vec_ref[2:3, :] += jnp.sum(grad_middle, axis=0, keepdims=True)
+        return carry
+
+    lax.fori_loop(0, lax.div(place_ref[size_at], rows), block, 0)
+
+
+def attend_grad_kernel(length, group, lengths_ref, place_ref, dm_ref, q_ref, k_ref, v_ref, probs_ref, grads_ref, vec_ref):
+    width = dm_ref.shape[1]
+    quads = width // 256
+    tiles = length // TILE
+    captions = probs_ref.shape[0] // quads
+    starts = captions * tiles
+    end = place_ref[starts + captions + 1]
+    clear = pl.ds(pl.multiple_of(end * TILE, TILE), 256)
+    for which in range(3):
+        grads_ref[which, clear, :] = jnp.zeros((256, width), BF16)
+    vec_ref[...] = jnp.zeros_like(vec_ref)
+    row = lax.broadcasted_iota(jnp.int32, (length, 1), 0)
+
+    def several(step, carry):
+        items = []
+        for g in range(group):
+            cap = step * group + g
+            packed = pl.ds(pl.multiple_of(place_ref[starts + cap] * TILE, TILE), length)
+            plain = pl.ds(pl.multiple_of(cap * length, length), length)
+            for quad in range(quads):
+                items.append((cap, quad, packed, plain, slice(256 * quad, 256 * quad + 256)))
+        probs = [probs_ref[cap * quads + quad] for cap, quad, _, _, _ in items]
+        wide = []
+        for cap, _, packed, _, lanes in items:
+            dm = dm_ref[packed, lanes]
+            wide.append(spread(jnp.where(row < lengths_ref[cap], dm, jnp.zeros_like(dm))))
+        grad_probs = [dot(v_ref[plain, lanes], w, NT) for (_, _, _, plain, lanes), w in zip(items, wide)]
+        grad_values = [dot(p, w, NN) for p, w in zip(probs, wide)]
+        grad_scores = []
+        for p, grad in zip(probs, grad_probs):
+            p = p.astype(F32)
+            along = p * grad
+            grad_scores.append((along - p * jnp.sum(along, axis=0, keepdims=True)).astype(BF16))
+        grad_keys = [
+            dot(g, spread(q_ref[plain, lanes]), NN) * 0.125 for (_, _, _, plain, lanes), g in zip(items, grad_scores)
+        ]
+        grad_query = [
+            collect(dot(g, k_ref[plain, lanes], TN)) * 0.125 for (_, _, _, plain, lanes), g in zip(items, grad_scores)
+        ]
+        for at, (_, _, packed, _, lanes) in enumerate(items):
+            grads_ref[0, packed, lanes] = grad_query[at].astype(BF16)
+            grads_ref[1, packed, lanes] = grad_keys[at].astype(BF16)
+            grads_ref[2, packed, lanes] = grad_values[at].astype(BF16)
+        for quad in range(quads):
+            lanes = slice(256 * quad, 256 * quad + 256)
+            vec_ref[0:1, lanes] += sum(jnp.sum(v, axis=0, keepdims=True) for v in grad_query[quad::quads])
+            vec_ref[1:2, lanes] += sum(jnp.sum(v, axis=0, keepdims=True) for v in grad_values[quad::quads])
+        return carry
+
+    lax.fori_loop(0, captions // group, several, 0)
+
+
+def weight_grad_kernel(grid, size_at, place_ref, grads_ref, branch_ref, normed_ref, mixed_ref, own_ref, other_ref, total):
+    share = total.shape[0] // grid.count
+
+    def send(at):
+        for core, out_ref in ((0, own_ref), (1, other_ref)):
+            for slot, spot in enumerate(outgoing(grid, core)):
+                start = pl.multiple_of(grid.away(*spot) * share, 8)
+                out_ref[slot, at] = total[pl.ds(start, share), :].astype(BF16)
+
+    def matrix(at, carry):
+        def product(rows):
+            total[...] = dot(grads_ref[at, 0:rows, :], normed_ref[0:rows, :], TN)
+
+        by_size(place_ref[size_at], product)
+        send(at)
+        return carry
+
+    lax.fori_loop(0, 3, matrix, 0)
+
+    def product(rows):
+        total[...] = dot(branch_ref[0:rows, :], mixed_ref[0:rows, :], TN)
+
+    by_size(place_ref[size_at], product)
+    send(3)
+
+
+def input_grad_kernel(grid, size_at, place_ref, moved_ref, grad_ref, grads_ref, vec_in, down_vec, up_vec, mid_vec, att_vec, held, out_ref, vec_ref, found):
+    rows = 128
+    width = moved_ref.shape[1]
+    vec_ref[...] = jnp.zeros_like(vec_ref)
+    vec_ref[2:4, :] = att_vec[0:2, :]
+    vec_ref[4:5, :] = mid_vec[2:3, :]
+    vec_ref[5:7, :] = mid_vec[0:2, :]
+    vec_ref[7:8, :] = down_vec[0:1, :]
+    for part in range(4):
+        vec_ref[8 + part : 9 + part, :] = up_vec[8 * part : 8 * part + 1, :]
+
+    def block(step, carry):
+        at = rows_at(step, rows)
+        grads = dot(grads_ref[0, at, :], held[:, 1].reshape(width, width), NN)
+        grads = grads + dot(grads_ref[1, at, :], held[:, 2].reshape(width, width), NN)
+        grads = grads + dot(grads_ref[2, at, :], held[:, 3].reshape(width, width), NN)
+        hat, scale = normal(moved_ref[at, :].astype(F32))
+        found[at, :] = grad_ref[at, :] + normal_back(hat, scale, vec_in[0:1, :], grads)
+        vec_ref[0:1, :] += jnp.sum(grads * hat, axis=0, keepdims=True)
+        vec_ref[1:2, :] += jnp.sum(grads, axis=0, keepdims=True)
+        return carry
+
+    lax.fori_loop(0, lax.div(place_ref[size_at], rows), block, 0)
+    total = place_ref[size_at + 1]
+
+    def tile(index, carry):
+        values = found[tile_rows(place_ref, index), :]
+        out_ref[rows_at(index, TILE), :] = jnp.where(place_ref[index] < total, values, 0.0)
+        return carry
+
+    lax.fori_loop(0, out_ref.shape[0] // TILE, tile, 0)
+
+
+def lower_kernel(place_ref, active_ref, middle_ref, vec_in, weight_ref, out_ref, found):
+    step = pl.program_id(0)
+    rows = middle_ref.shape[0]
+    weight = weight_ref[...].reshape(middle_ref.shape[1], active_ref.shape[1])
+    out = middle_ref[...] + dot(active_ref[...], weight, NT) + vec_in[7:8, :]
+    found[rows_at(step, rows), :] = out.astype(BF16)
+
+    @pl.when(step == pl.num_programs(0) - 1)
+    def _():
+        for index in range(out_ref.shape[0] // TILE):
+            out_ref[index * TILE : (index + 1) * TILE, :] = found[tile_rows(place_ref, index), :]
+
+
+def unpack_kernel(grid, vec_ref, *outs):
+    me = grid.me()
+    eight = pltpu.roll(vec_ref[0:8, :], lax.rem(768 - me * 24, 768), 1)
+    for k in range(8):
+        outs[k][...] = eight[k : k + 1, 0:24]
+    row = lax.broadcasted_iota(jnp.int32, (8, 768), 0)
+    four = jnp.sum(jnp.where(row == lax.div(me, 8), vec_ref[8:16, :], 0.0), axis=0, keepdims=True)
+    four = jnp.broadcast_to(four, (8, 768))
+    four = pltpu.roll(four, lax.rem(768 - lax.rem(me, 8) * 96, 768), 1)
+    outs[8][...] = four[0:1, 0:96]
+
+
+def whole(shape):
+    return pl.BlockSpec(shape, lambda *_: (0,) * len(shape))
+
+
+ANY = pl.BlockSpec(memory_space=pl.ANY)
+SMEM = pl.BlockSpec(memory_space=pltpu.SMEM)
+
+
+FAST = pl.BlockSpec(memory_space=pltpu.VMEM)
+
+
+def call(kernel, steps, in_specs, out_specs, outs, scratch, flops, moved, name, limit=10):
+    return pl.pallas_call(
+        kernel,
+        grid=(steps,),
+        in_specs=in_specs,
+        out_specs=out_specs,
+        out_shape=[jax.ShapeDtypeStruct(s, d) for s, d in outs],
+        scratch_shapes=scratch,
+        compiler_params=pltpu.CompilerParams(vmem_limit_bytes=limit * 1024 * 1024),
+        cost_estimate=pl.CostEstimate(flops=flops, bytes_accessed=moved, transcendentals=0),
+        name=name,
+    )
+
+
+def call_near(kernel, in_specs, outs, scratch, flops, name, limit=10):
+    return pl.pallas_call(
+        kernel,
+        in_specs=in_specs,
+        out_specs=[FAST] * len(outs),
+        out_shape=[jax.ShapeDtypeStruct(s, d) for s, d in outs],
+        scratch_shapes=scratch,
+        compiler_params=pltpu.CompilerParams(vmem_limit_bytes=limit * 1024 * 1024),
+        cost_estimate=pl.CostEstimate(flops=flops, bytes_accessed=1_000_000, transcendentals=0),
+        name=name,
+    )
+
+
+def fast_device(
+    grid,
+    hidden,
+    lengths,
+    cotangent,
+    attgain,
+    attshift,
+    querymat,
+    querybias,
+    keymat,
+    valuemat,
+    valuebias,
+    mixmat,
+    mixbias,
+    mlpgain,
+    mlpshift,
+    upmat_w,
+    upbias,
+    downmat,
+    downbias,
+):
+    captions, length, width = hidden.shape
+    tokens = captions * length
+    hidden2 = hidden.reshape(tokens, width)
+    cot2 = cotangent.reshape(tokens, width)
+    share = width // grid.count
+    ff = downmat.shape[0]
+    small = jnp.stack(
+        [attgain, attshift, querybias, valuebias, mixbias, mlpgain, mlpshift, downbias]
+    ).astype(F32)
+    upsmall = upbias.astype(F32).reshape(1, -1)
+    first = call(
+        functools.partial(pack_kernel, grid),
+        1,
+        [whole((8, share)), whole((1, 96))] + [whole((share, width))] * 3,
+        [whole((4, share, width))],
+        [((4, share, width), BF16)],
+        [pltpu.VMEM((16, width), F32)],
+        1000,
+        1000,
+        "pack",
+    )(small, upsmall, querymat.T, keymat.T, valuemat.T)[0]
+    second = jnp.concatenate([mixmat.T[None], upmat_w.T.reshape(4, share, width)], axis=0)
+    third = downmat.T
+    where = order_of(lengths, length)
+    size_at = captions * (length // TILE) + captions
+    begun = lax.optimization_barrier(gather_begin(grid, first))
+    second_begun = lax.optimization_barrier(gather_begin(grid, tie(second, begun)))
+    third_begun = lax.optimization_barrier(gather_begin(grid, tie(third, second_begun)))
+    begun = lax.optimization_barrier(gather_middle(grid, begun))
+    first_in, places = gather_end(grid, begun)
+    second_begun = gather_middle(grid, tie(second_begun, first_in))
+    half = grid.count // 2
+    unit = 2 * tokens * width * width
+    row = (tokens, width)
+    heads = captions * (width // 256)
+    tall = (tokens + 64, width)
+    square = pltpu.VMEM((width, width), F32)
+    moved, normed, query, keys, values, vec, held_one = call_near(
+        functools.partial(project_kernel, grid, places),
+        [SMEM] + [FAST] * (1 + len(first_in)),
+        [(row, BF16)] * 5 + [((share, width), F32), ((grid.count,) + first.shape, BF16)],
+        [],
+        5 * unit,
+        "project",
+    )(where, hidden2, *first_in)
+    second_begun, third_begun = tie((second_begun, third_begun), vec)
+    second_in, _ = gather_end(grid, second_begun)
+    third_begun = gather_middle(grid, third_begun)
+    probs, mixed = call_near(
+        functools.partial(attend_kernel, length, 4),
+        [SMEM] * 2 + [FAST] * 3,
+        [((heads, length, 256), BF16), (row, BF16)],
+        [],
+        5 * unit,
+        "attend",
+    )(lengths, where, query, keys, values)
+    third_in, _ = gather_end(grid, tie(third_begun, second_in))
+    middle, normed2, active, slope, held_two = call_near(
+        functools.partial(upper_kernel, grid, places),
+        [FAST] * (3 + len(second_in)),
+        [(row, F32), (row, BF16), ((tokens, ff), BF16), ((tokens, ff), BF16), ((grid.count,) + second.shape, BF16)],
+        [],
+        9 * unit,
+        "upper",
+    )(moved, mixed, vec, *second_in)
+    low, down_vec, down_own, down_other = call_near(
+        functools.partial(down_grad_kernel, grid, length, size_at),
+        [SMEM] * 2 + [FAST] * 2,
+        [(row, BF16), ((8, width), F32)] + [((half, share, ff), BF16)] * 2,
+        [square],
+        5 * unit,
+        "down_grad",
+    )(lengths, where, cot2, active)
+    down_came = grid.shift(down_other, kc=1)
+    grad_upper, up_vec, up_own, up_other, lower_w = call_near(
+        functools.partial(upper_grad_kernel, grid, places, size_at),
+        [SMEM] + [FAST] * (3 + len(third_in)),
+        [((tokens, ff), BF16), ((32, width), F32)]
+        + [((half, 4, share, width), BF16)] * 2
+        + [((grid.count, share, ff), BF16)],
+        [square],
+        8 * unit,
+        "upper_grad",
+    )(where, low, slope, normed2, *third_in)
+    down_came = tie(down_came, up_vec)
+    down_part = down_own.astype(F32) + down_came.astype(F32)
+    down_part = down_part.astype(BF16).reshape(half * share, ff)
+    down_part = lax.psum_scatter(down_part, ("x", "y"), scatter_dimension=0, tiled=True)
+    up_one = scatter_core(grid, up_other)
+    grad_middle, branch, dm, mid_vec = call_near(
+        functools.partial(middle_grad_kernel, grid, size_at),
+        [SMEM] + [FAST] * 5,
+        [(row, F32), (row, BF16), (tall, BF16), ((8, width), F32)],
+        [],
+        6 * unit,
+        "middle_grad",
+    )(where, grad_upper, middle, low, vec, held_two)
+    up_two = scatter_first(grid, up_own, tie(up_one, mid_vec))
+    dm = tie(dm, up_two[0])
+    grads, att_vec = call_near(
+        functools.partial(attend_grad_kernel, length, 4),
+        [SMEM] * 2 + [FAST] * 5,
+        [((3, tokens + 256, width), BF16), ((8, width), F32)],
+        [],
+        7 * unit,
+        "attend_grad",
+    )(lengths, where, dm, query, keys, values, probs)
+    up_three = scatter_second(grid, up_two, att_vec)
+    grads = tie(grads, up_three[0])
+    att_own, att_other = call_near(
+        functools.partial(weight_grad_kernel, grid, size_at),
+        [SMEM] + [FAST] * 4,
+        [((half, 4, share, width), BF16)] * 2,
+        [square],
+        5 * unit,
+        "weight_grad",
+    )(where, grads, branch, normed, mixed)
+    up_four = scatter_third(grid, up_three, att_own[0, 0, 0:8, 0:128])
+    att_one = scatter_core(grid, att_other)
+    grad_middle = tie(grad_middle, up_four[0])
+    input_grad, all_vec = call_near(
+        functools.partial(input_grad_kernel, grid, size_at),
+        [SMEM] + [FAST] * 9,
+        [(row, F32), ((16, width), F32)],
+        [pltpu.VMEM(row, F32)],
+        5 * unit,
+        "input_grad",
+    )(where, moved, grad_middle, grads, vec, down_vec, up_vec, mid_vec, att_vec, held_one)
+    att_two = scatter_first(grid, att_own, tie(att_one, all_vec))
+    up_sum = scatter_last(up_four, all_vec)
+    middle = tie(middle, att_two[0])
+    steps = 4
+    rows = tokens // steps
+    block = pl.BlockSpec((rows, width), lambda i: (i, 0))
+    (block_out,) = call(
+        lower_kernel,
+        steps,
+        [SMEM, pl.BlockSpec((rows, ff), lambda i: (i, 0)), block, whole((share, width)), whole((grid.count, share, ff))],
+        [whole(row)],
+        [(row, BF16)],
+        [pltpu.VMEM(row, BF16)],
+        4 * unit,
+        20_000_000,
+        "lower",
+        24,
+    )(where, active, middle, vec, lower_w)
+    att_three = scatter_second(grid, att_two, block_out[0:8, 0:128])
+    att_four = scatter_third(grid, att_three, block_out[0:8, 0:128])
+    att_sum = scatter_last(att_four, block_out[0:8, 0:128])
+    down_sum = lax.psum_scatter(down_part, "z", scatter_dimension=0, tiled=True).astype(F32)
+    all_vec = all_vec + grid.shift(all_vec, kc=1)
+    all_vec = all_vec + grid.shift(all_vec, kx=1)
+    all_vec = all_vec + grid.shift(all_vec, ky=1)
+    all_vec = (
+        all_vec + grid.shift(all_vec, kz=1) + grid.shift(all_vec, kz=2) + grid.shift(all_vec, kz=3)
+    )
+    vecs = call(
+        functools.partial(unpack_kernel, grid),
+        1,
+        [whole((16, width))],
+        [whole((1, share))] * 8 + [whole((1, ff // grid.count))],
+        [((1, share), F32)] * 8 + [((1, ff // grid.count), F32)],
+        [],
+        1000,
+        1000,
+        "unpack",
+    )(all_vec)
+    vecs = [v.reshape(-1) for v in vecs]
+    return (
+        block_out.reshape(hidden.shape),
+        input_grad.reshape(hidden.shape),
+        vecs[0],
+        vecs[1],
+        att_sum[0].T,
+        vecs[2],
+        att_sum[1].T,
+        att_sum[2].T,
+        vecs[3],
+        att_sum[3].T,
+        vecs[4],
+        vecs[5],
+        vecs[6],
+        up_sum.reshape(ff // grid.count, width).T,
+        vecs[8],
+        down_sum.T,
+        vecs[7],
+    )
+
+
+def fits(mesh):
+    return mesh.shape["dp"] == 8 and mesh.shape["fsdp"] == 4
+
+
 def solution(mesh):
+    axes = ("dp", "fsdp")
+    body = per_device
+    if fits(mesh):
+        axes = AXES
+        grid = Grid3(mesh.shape["dp"], mesh.shape["fsdp"])
+        mesh = jax.sharding.Mesh(mesh.devices.reshape(grid.z, grid.x, grid.y, grid.c), AXES)
+        body = functools.partial(fast_device, grid)
     placed = (
-        P(("dp", "fsdp"), None, None),
-        P(("dp", "fsdp")),
-        P(("dp", "fsdp"), None, None),
-        P(("dp", "fsdp")),
-        P(("dp", "fsdp")),
-        P(None, ("dp", "fsdp")),
-        P(("dp", "fsdp")),
-        P(None, ("dp", "fsdp")),
-        P(None, ("dp", "fsdp")),
-        P(("dp", "fsdp")),
-        P(None, ("dp", "fsdp")),
-        P(("dp", "fsdp")),
-        P(("dp", "fsdp")),
-        P(("dp", "fsdp")),
-        P(None, ("dp", "fsdp")),
-        P(("dp", "fsdp")),
-        P(None, ("dp", "fsdp")),
-        P(("dp", "fsdp")),
+        P(axes, None, None),
+        P(axes),
+        P(axes, None, None),
+        P(axes),
+        P(axes),
+        P(None, axes),
+        P(axes),
+        P(None, axes),
+        P(None, axes),
+        P(axes),
+        P(None, axes),
+        P(axes),
+        P(axes),
+        P(axes),
+        P(None, axes),
+        P(axes),
+        P(None, axes),
+        P(axes),
     )
     return jax.shard_map(
-        per_device,
+        body,
         mesh=mesh,
         in_specs=placed,
         out_specs=(
-            P(("dp", "fsdp"), None, None),
-            P(("dp", "fsdp"), None, None),
-            P(("dp", "fsdp")),
-            P(("dp", "fsdp")),
-            P(None, ("dp", "fsdp")),
-            P(("dp", "fsdp")),
-            P(None, ("dp", "fsdp")),
-            P(None, ("dp", "fsdp")),
-            P(("dp", "fsdp")),
-            P(None, ("dp", "fsdp")),
-            P(("dp", "fsdp")),
-            P(("dp", "fsdp")),
-            P(("dp", "fsdp")),
-            P(None, ("dp", "fsdp")),
-            P(("dp", "fsdp")),
-            P(None, ("dp", "fsdp")),
-            P(("dp", "fsdp")),
+            P(axes, None, None),
+            P(axes, None, None),
+            P(axes),
+            P(axes),
+            P(None, axes),
+            P(axes),
+            P(None, axes),
+            P(None, axes),
+            P(axes),
+            P(None, axes),
+            P(axes),
+            P(axes),
+            P(axes),
+            P(None, axes),
+            P(axes),
+            P(None, axes),
+            P(axes),
         ),
         check_vma=False,
     )

time: 1110 us -> 313 us (0.28)
  waiting for transfers between devices: 770 us -> 117 us
  matrix products: 142 us -> 0 us
  Pallas kernels: 0 us -> 91.5 us
  blocking collectives: 83.4 us -> 0 us
  local copies, waits for them, and re-layouts: 71 us -> 12.9 us
  starting transfers between devices: 1.26 us -> 58.4 us
    reduce_scatter x6 -> x2, waiting for transfers between devices: 516 us -> 0.02 us  [the longest x1 0.02 us: fast_device(): lax.psum_scatter(down_part, ('x', 'y'), scatter_dimension=0, tiled=True)]
    all_gather x6 -> x0, waiting for transfers between devices: 251 us -> none  [the longest x1 58.2 us: per_device(): lax.all_gather(upmat_w, ('dp', 'fsdp'), axis=1, tiled=True)]
    dot_general x24 -> x0, matrix products: 142 us -> none  [the longest x6 39.8 us: outer_sum(): jnp.einsum('cli,clj->ij', inputs, grads, preferred_element_type=jnp.float32)]
    ppermute x0 -> x74, waiting for transfers between devices: none -> 117 us  [shift(): return lax.ppermute(values, AXES, pairs)]
    pallas_call x0 -> x12, Pallas kernels: none -> 91.5 us  [the longest x1 18.3 us: fast_device(): call_near(functools.partial(down_grad_kernel, grid, length, size_at), [SM...]
    unnamed x2 -> x0, blocking collectives: 83.4 us -> none
    ppermute x0 -> x74, starting transfers between devices: none -> 58.3 us  [shift(): return lax.ppermute(values, AXES, pairs)]
    reshape x7 -> x0, local copies, waits for them, and re-layouts: 34.2 us -> none  [the longest x1 6.23 us: per_device(): grad_keys_low = grad_keys_low.reshape(captions, length, width)]
  transfers between devices with their start and end apart: 12 -> 76, of which waited for: 11 -> 29; matrix products, arithmetic and copies ran while one was open for 17% -> 5% of each run, Pallas kernels for 0% -> 29%
where the time goes in v2:
time: 313 us; the launch traced here: 311 us
  waiting for transfers between devices  117 us (37%)
  Pallas kernels  91.5 us (29%)
  starting transfers between devices  58.4 us (19%)
  other arithmetic  15.8 us (5%)
  between operations  15.8 us (5%)
  local copies, waits for them, and re-layouts  12.9 us (4%)
    ppermute x74, waiting for transfers between devices, shift(): return lax.ppermute(values, AXES, pairs)  117 us
    ppermute x74, starting transfers between devices, shift(): return lax.ppermute(values, AXES, pairs)  58.3 us
    pallas_call x1, Pallas kernels, fast_device(): call_near(functools.partial(down_grad_kernel, grid, length, size_at), [SM...  18.3 us
    pallas_call x1, Pallas kernels, fast_device(): call_near(functools.partial(upper_kernel, grid, places), [FAST] * (3 + le...  12.7 us
    pallas_call x1, Pallas kernels, fast_device(): call_near(functools.partial(upper_grad_kernel, grid, places, size_at), [S...  12.5 us
    unnamed x82, local copies, waits for them, and re-layouts  10.8 us
    pallas_call x1, Pallas kernels, fast_device(): call_near(functools.partial(middle_grad_kernel, grid, size_at), [SMEM] +...  8.32 us
    pallas_call x1, Pallas kernels, fast_device(): call(lower_kernel, steps, [SMEM, pl.BlockSpec((rows, ff), lambda i: (i, 0...  7.55 us
  transfers between devices with their start and end apart: 76, of which 29 were waited for; matrix products, arithmetic and copies ran while one was open for 5% of the time, Pallas kernels for 29%

profile of v2, /device:TPU:0, one launch (start us, length us, event | category | flops | bytes accessed | tf_op | source)
XLA Modules:
  0.0 311.4 jit_solution(1257111391667069658)
XLA Ops:
  11.1 5.1 %collective-permute-start.2 = (bf16[4,24,768]{2,1,0:T(8,128)(2,1)S(1)}, bf16[4,24,768]{2,1,0:T(8,128)(2,1)S(1)}, u32[]{:S(2)}, u32[]{:S(2)}) collective-permute-start(bf16[4,24,768]{2,1,0:T(8,128)(2,1)S(1)} %pack.1), channel_id=1, source_target_pairs={{0,24},{1,25},{2,26},{3,27},{4,28},{5,29},{6,30},{7,31},{8,0},{9,1... | collective-permute-start | bytes 442376 | tf_op jit(solution)/shard_map/ppermute | solution.py:319
  20.9 7.8 %collective-permute-done.1 = bf16[4,24,768]{2,1,0:T(8,128)(2,1)S(1)} collective-permute-done((bf16[4,24,768]{2,1,0:T(8,128)(2,1)S(1)}, bf16[4,24,768]{2,1,0:T(8,128)(2,1)S(1)}, u32[]{:S(2)}, u32[]{:S(2)}) %collective-permute-start.1) | collective-permute-done | bytes 147488 | tf_op jit(solution)/shard_map/ppermute | solution.py:319
  37.3 10.3 %collective-permute-done.18 = bf16[5,24,768]{2,1,0:T(8,128)(2,1)} collective-permute-done((bf16[5,24,768]{2,1,0:T(8,128)(2,1)S(1)}, bf16[5,24,768]{2,1,0:T(8,128)(2,1)}, u32[]{:S(2)}, u32[]{:S(2)}) %collective-permute-start.18) | collective-permute-done | bytes 184352 | tf_op jit(solution)/shard_map/ppermute | solution.py:319
  54.3 3.4 %collective-permute-done.24 = bf16[24,3072]{1,0:T(8,128)(2,1)S(1)} collective-permute-done((bf16[24,3072]{1,0:T(8,128)(2,1)S(1)}, bf16[24,3072]{1,0:T(8,128)(2,1)S(1)}, u32[]{:S(2)}, u32[]{:S(2)}) %collective-permute-start.24) | collective-permute-done | bytes 147488 | tf_op jit(solution)/shard_map/ppermute | solution.py:319
  59.2 4.7 %collective-permute-done.23 = bf16[24,3072]{1,0:T(8,128)(2,1)S(1)} collective-permute-done((bf16[24,3072]{1,0:T(8,128)(2,1)S(1)}, bf16[24,3072]{1,0:T(8,128)(2,1)S(1)}, u32[]{:S(2)}, u32[]{:S(2)}) %collective-permute-start.23) | collective-permute-done | bytes 147488 | tf_op jit(solution)/shard_map/ppermute | solution.py:319
  66.8 6.5 %collective-permute-done.13.rest_12_ = bf16[2,4,24,768]{3,2,1,0:T(8,128)(2,1)S(1)} collective-permute-done((bf16[2,4,24,768]{3,2,1,0:T(8,128)(2,1)S(1)}, bf16[2,4,24,768]{3,2,1,0:T(8,128)(2,1)S(1)}, u32[]{:S(2)}, u32[]{:S(2)}) %collective-permute-start.13) | collective-permute-done | bytes 294944 | tf_op jit(solution)/shard_map/ppermute | solution.py:319
  78.4 6.4 %project.1 = (bf16[1024,768]{1,0:T(8,128)(2,1)S(1)}, bf16[1024,768]{1,0:T(8,128)(2,1)S(1)}, bf16[1024,768]{1,0:T(8,128)(2,1)S(1)}, bf16[1024,768]{1,0:T(8,128)(2...) custom-call(s32[82]{0:T(128)S(1)} %pad_add_fusion.place_ref, ...), custom_call_target="tpu_custom_call" | custom-call | flops 6039797760 | bytes 1000000 | tf_op jit(solution)/shard_map/project/pallas_call | solution.py:967
  91.6 6.9 %collective-permute-done.37.rest_4_ = bf16[2,24,3072]{2,1,0:T(8,128)(2,1)S(1)} collective-permute-done((bf16[2,24,3072]{2,1,0:T(8,128)(2,1)S(1)}, bf16[2,24,3072]{2,1,0:T(8,128)(2,1)S(1)}, u32[]{:S(2)}, u32[]{:S(2)}) %collective-permute-start.37) | collective-permute-done | bytes 294944 | tf_op jit(solution)/shard_map/ppermute | solution.py:319
  98.6 4.8 %collective-permute-done.38.rest_6_ = bf16[2,24,3072]{2,1,0:T(8,128)(2,1)S(1)} collective-permute-done((bf16[2,24,3072]{2,1,0:T(8,128)(2,1)S(1)}, bf16[2,24,3072]{2,1,0:T(8,128)(2,1)S(1)}, u32[]{:S(2)}, u32[]{:S(2)}) %collective-permute-start.38) | collective-permute-done | bytes 294944 | tf_op jit(solution)/shard_map/ppermute | solution.py:319
  106.6 5.3 %collective-permute-done.33.rest_12_ = bf16[2,5,24,768]{3,2,1,0:T(8,128)(2,1)S(1)} collective-permute-done((bf16[2,5,24,768]{3,2,1,0:T(8,128)(2,1)S(1)}, bf16[2,5,24,768]{3,2,1,0:T(8,128)(2,1)S(1)}, u32[]{:S(2)}, u32[]{:S(2)}) %collective-permute-start.33) | collective-permute-done | bytes 368672 | tf_op jit(solution)/shard_map/ppermute | solution.py:319
  118.1 4.8 %attend.1 = (bf16[48,64,256]{2,1,0:T(8,128)(2,1)S(1)}, bf16[1024,768]{1,0:T(8,128)(2,1)S(1)}) custom-call(s32[16]{0:T(128)S(1)} %copy-done.3, s32[82]{0:T(128)S(1)} %pad_add_fusion.place_ref, bf16[1024,768]{1,0:T(8,128)(2,1)S(1)} %get-tuple-element.111.q_ref, bf16[1024,768]{1,0:T(8,128)(2,1)S(1)} %get-tuple-element.112.k_ref, ...), custom_call_target="tpu_custom_call" | custom-call | flops 6039797760 | bytes 1000000 | tf_op jit(solution)/shard_map/attend/pallas_call | solution.py:978
  127.6 12.7 %upper.1 = (f32[1024,768]{1,0:T(8,128)S(1)}, bf16[1024,768]{1,0:T(8,128)(2,1)S(1)}, bf16[1024,3072]{1,0:T(8,128)(2,1)S(1)}, bf16[1024,3072]{1,0:T(8,128)(2,1)S(1)}, bf16[32,5,24,768]{3,2,1,0:T(8,128)(2,1)S(1)}) custom-call(bf16[1024,768]{1,0:T(8,128)(2,1)S(1)} %get-tuple-element.110.moved_ref, bf16[1024,768]{1,0:T(8,128)(2,1)S(1)} %get-tuple-element.114.mixed_ref, ...), custom_call_target="tpu_custom_call" | custom-call | flops 10871635968 | bytes 1000000 | tf_op jit(solution)/shard_map/upper/pallas_call | solution.py:987
  141.6 18.3 %down_grad.1 = (bf16[1024,768]{1,0:T(8,128)(2,1)S(1)}, f32[8,768]{1,0:T(8,128)S(1)}, bf16[16,24,3072]{2,1,0:T(8,128)(2,1)S(1)}, bf16[16,24,3072]{2,1,0:T(8,128)(2,1)S(1)}) custom-call(s32[16]{0:T(128)S(1)} %copy-done.3, s32[82]{0:T(128)S(1)} %pad_add_fusion.place_ref, bf16[1024,768]{1,0:T(8,128)(2,1)S(1)} %bitcast.196, ...), custom_call_target="tpu_custom_call" | custom-call | flops 6039797760 | bytes 1000000 | tf_op jit(solution)/shard_map/down_grad/pallas_call | solution.py:995
  162.9 12.5 %upper_grad.1 = (bf16[1024,3072]{1,0:T(8,128)(2,1)S(1)}, f32[32,768]{1,0:T(8,128)S(1)}, bf16[16,4,24,768]{3,2,1,0:T(8,128)(2,1)S(1)}, bf16[16,4,24,768]{3,2,1,0:T(8,128)(2,1)}, bf16[32,24,3072]{2,1,0:T(8,128)(2,1)S(1)}) custom-call(s32[82]{0:T(128)S(1)} %pad_add_fusion.place_ref, bf16[1024,768]{1,0:T(8,128)(2,1)S(1)} %get-tuple-element.130.low_ref, ...), custom_call_target="tpu_custom_call" | custom-call | flops 9663676416 | bytes 1000000 | tf_op jit(solution)/shard_map/upper_grad/pallas_call | solution.py:1004
  175.4 8.3 %middle_grad.1 = (f32[1024,768]{1,0:T(8,128)S(1)}, bf16[1024,768]{1,0:T(8,128)(2,1)S(1)}, bf16[1088,768]{1,0:T(8,128)(2,1)S(1)}, f32[8,768]{1,0:T(8,128)S(1)}) custom-call(s32[82]{0:T(128)S(1)} %pad_add_fusion.place_ref, bf16[1024,3072]{1,0:T(8,128)(2,1)S(1)} %get-tuple-element.139.upper_ref, f32[1024,768]{1,0:T(8,128)S(1)} %get-tuple-element.165.middle_ref, ...), custom_call_target="tpu_custom_call" | custom-call | flops 7247757312 | bytes 1000000 | tf_op jit(solution)/shard_map/middle_grad/pallas_call | solution.py:1019
  192.9 7.2 %attend_grad.1 = (bf16[3,1280,768]{2,1,0:T(8,128)(2,1)S(1)}, f32[8,768]{1,0:T(8,128)S(1)}) custom-call(s32[16]{0:T(128)S(1)} %copy-done.3, s32[82]{0:T(128)S(1)} %pad_add_fusion.place_ref, bf16[1088,768]{1,0:T(8,128)(2,1)S(1)} %copy-done.16, bf16[1024,768]{1,0:T(8,128)(2,1)S(1)} %copy-done.26, bf16[1024,768]{1,0:T(8,128)(2,1)S(1)} %copy-done.28, ...), custom_call_target="tpu_custom_call" | custom-call | flops 8455716864 | bytes 1000000 | tf_op jit(solution)/shard_map/attend_grad/pallas_call | solution.py:1029
  200.2 16.5 %collective-permute-done.53 = bf16[2,2,4,24,768]{4,3,2,1,0:T(8,128)(2,1)S(1)} collective-permute-done((bf16[2,2,4,24,768]{4,3,2,1,0:T(8,128)(2,1)S(1)}, bf16[2,2,4,24,768]{4,3,2,1,0:T(8,128)(2,1)S(1)}, u32[]{:S(2)}, u32[]{:S(2)}) %collective-permute-start.53) | collective-permute-done | bytes 589856 | tf_op jit(solution)/shard_map/ppermute | solution.py:319
  216.8 5.9 %weight_grad.1 = (bf16[16,4,24,768]{3,2,1,0:T(8,128)(2,1)S(1)}, bf16[16,4,24,768]{3,2,1,0:T(8,128)(2,1)S(1)}) custom-call(s32[82]{0:T(128)S(1)} %pad_add_fusion.place_ref, bf16[3,1280,768]{2,1,0:T(8,128)(2,1)S(1)} %get-tuple-element.151.grads_ref, bf16[1024,768]{1,0:T(8,128)(2,1)S(1)} %copy-done.18, bf16[1024,768]{1,0:T(8,128)(2,1)S(1)} %copy-done.22, ...), custom_call_target="tpu_custom_call" | custom-call | flops 6039797760 | bytes 1000000 | tf_op jit(solution)/shard_map/weight_grad/pallas_call | solution.py:1039
  224.0 14.6 %collective-permute-done.56 = bf16[2,4,24,768]{3,2,1,0:T(8,128)(2,1)S(1)} collective-permute-done((bf16[2,4,24,768]{3,2,1,0:T(8,128)(2,1)S(1)}, bf16[2,4,24,768]{3,2,1,0:T(8,128)(2,1)S(1)}, u32[]{:S(2)}, u32[]{:S(2)}) %collective-permute-start.56) | collective-permute-done | bytes 294944 | tf_op jit(solution)/shard_map/ppermute | solution.py:319
  239.6 7.2 %input_grad.1 = (f32[1024,768]{1,0:T(8,128)}, f32[16,768]{1,0:T(8,128)S(1)}) custom-call(s32[82]{0:T(128)S(1)} %pad_add_fusion.place_ref, bf16[1024,768]{1,0:T(8,128)(2,1)S(1)} %copy-done.14, f32[1024,768]{1,0:T(8,128)S(1)} %copy-done.12, bf16[3,1280,768]{2,1,0:T(8,128)(2,1)S(1)} %get-tuple-element.151.grads_ref, ...), custom_call_target="tpu_custom_call" | custom-call | flops 6039797760 | bytes 1000000 | tf_op jit(solution)/shard_map/input_grad/pallas_call | solution.py:1050
  251.1 3.9 %collective-permute-start.71 = (bf16[4,24,768]{2,1,0:T(8,128)(2,1)S(1)}, bf16[4,24,768]{2,1,0:T(8,128)(2,1)S(1)}, u32[]{:S(2)}, u32[]{:S(2)}) collective-permute-start(bf16[4,24,768]{2,1,0:T(8,128)(2,1)S(1)} %get-tuple-element.212), channel_id=1, source_target_pairs={{0,16},{1,17},{2,18},{3,19},{4,20},{5,21},{6,22},{7,23},{8,24},{9,... | collective-permute-start | bytes 442376 | tf_op jit(solution)/shard_map/ppermute | solution.py:319
  257.1 7.5 %lower.1 = bf16[1024,768]{1,0:T(8,128)(2,1)} custom-call(s32[82]{0:T(128)S(1)} %pad_add_fusion.place_ref, bf16[1024,3072]{1,0:T(8,128)(2,1)S(1)} %bitcast.198, f32[1024,768]{1,0:T(8,128)S(1)} %copy-done.9, f32[24,768]{1,0:T(8,128)S(1)} %get-tuple-element.115.vec_ref.vec_in, bf16[32,24,3072]{2,1,0:T(8,128)(2,1)S(1)} %bitcast.200), custom_call_target="tpu_custom_call" | custom-call | flops 4831838208 | bytes 20000000 | tf_op jit(solution)/shard_map/lower/pallas_call | solution.py:1064
  280.0 3.9 %collective-permute-start.69 = (bf16[4,24,768]{2,1,0:T(8,128)(2,1)S(1)}, bf16[4,24,768]{2,1,0:T(8,128)(2,1)S(1)}, u32[]{:S(2)}, u32[]{:S(2)}) collective-permute-start(bf16[4,24,768]{2,1,0:T(8,128)(2,1)S(1)} %get-tuple-element.215), channel_id=1, source_target_pairs={{0,24},{1,25},{2,26},{3,27},{4,28},{5,29},{6,30},{7,31},{8,0},{9,1... | collective-permute-start | bytes 442376 | tf_op jit(solution)/shard_map/ppermute | solution.py:319
  290.9 11.1 %collective-permute-done.68 = bf16[4,24,768]{2,1,0:T(8,128)(2,1)S(1)} collective-permute-done((bf16[4,24,768]{2,1,0:T(8,128)(2,1)S(1)}, bf16[4,24,768]{2,1,0:T(8,128)(2,1)S(1)}, u32[]{:S(2)}, u32[]{:S(2)}) %collective-permute-start.68) | collective-permute-done | bytes 147488 | tf_op jit(solution)/shard_map/ppermute | solution.py:319
  (271 shorter events, 100.2 us)
Async XLA Ops:
  7.2 272.6 %reduce-scatter.3.cloned.1.call-start = ((), (), s32[]{:S(2)}) async-start(), calls=%async_computation.2 | async-start | bytes 2949120 | tf_op jit(solution)/shard_map/reduce_scatter | solution.py:1017
  30.3 17.3 %collective-permute-start.18 = (bf16[5,24,768]{2,1,0:T(8,128)(2,1)S(1)}, bf16[5,24,768]{2,1,0:T(8,128)(2,1)}, u32[]{:S(2)}, u32[]{:S(2)}) collective-permute-start(bf16[5,24,768]{2,1,0:T(8,128)(2,1)S(1)} %pad_maximum_fusion.6), channel_id=1, source_target_pairs={{0,16},{1,17},{2,18},{3,19},{4,20},{5,21},{6,22},{7,23},{8,24},{9,... | collective-permute-start | bytes 552968 | tf_op jit(solution)/shard_map/ppermute | solution.py:319
  31.7 18.5 %collective-permute-start.17 = (bf16[5,24,768]{2,1,0:T(8,128)(2,1)S(1)}, bf16[5,24,768]{2,1,0:T(8,128)(2,1)S(1)}, u32[]{:S(2)}, u32[]{:S(2)}) collective-permute-start(bf16[5,24,768]{2,1,0:T(8,128)(2,1)S(1)} %pad_maximum_fusion.6), channel_id=1, source_target_pairs={{0,8},{1,9},{2,10},{3,11},{4,12},{5,13},{6,14},{7,15},{8,16},{9,17... | collective-permute-start | bytes 552968 | tf_op jit(solution)/shard_map/ppermute | solution.py:319
  48.6 15.8 %collective-permute-start.9 = (bf16[2,4,24,768]{3,2,1,0:T(8,128)(2,1)S(1)}, bf16[2,4,24,768]{3,2,1,0:T(8,128)(2,1)S(1)}, u32[]{:S(2)}, u32[]{:S(2)}) collective-permute-start(bf16[2,4,24,768]{3,2,1,0:T(8,128)(2,1)S(1)} %pad_maximum_fusion.2.rest_0_), channel_id=1, source_target_pairs={{0,2},{1,3},{2,0},{3,1},{4,6},{5,7},{6,4},{7,5},{8,10},{9,11},{10,... | collective-permute-start | bytes 884744 | tf_op jit(solution)/shard_map/ppermute | solution.py:319
  87.6 17.0 %collective-permute-start.29 = (bf16[2,5,24,768]{3,2,1,0:T(8,128)(2,1)S(1)}, bf16[2,5,24,768]{3,2,1,0:T(8,128)(2,1)S(1)}, u32[]{:S(2)}, u32[]{:S(2)}) collective-permute-start(bf16[2,5,24,768]{3,2,1,0:T(8,128)(2,1)S(1)} %pad_maximum_fusion.rest_0_), channel_id=1, source_target_pairs={{0,2},{1,3},{2,0},{3,1},{4,6},{5,7},{6,4},{7,5},{8,10},{9,11},{10,... | collective-permute-start | bytes 1105928 | tf_op jit(solution)/shard_map/ppermute | solution.py:319
  88.8 15.8 %collective-permute-start.25 = (bf16[2,5,24,768]{3,2,1,0:T(8,128)(2,1)S(1)}, bf16[2,5,24,768]{3,2,1,0:T(8,128)(2,1)S(1)}, u32[]{:S(2)}, u32[]{:S(2)}) collective-permute-start(bf16[2,5,24,768]{3,2,1,0:T(8,128)(2,1)S(1)} %pad_maximum_fusion.rest_0_), channel_id=1, source_target_pairs={{0,1},{1,0},{2,3},{3,2},{4,5},{5,4},{6,7},{7,6},{8,9},{9,8},{10,11... | collective-permute-start | bytes 1105928 | tf_op jit(solution)/shard_map/ppermute | solution.py:319
  90.1 16.0 %collective-permute-start.31 = (bf16[2,5,24,768]{3,2,1,0:T(8,128)(2,1)S(1)}, bf16[2,5,24,768]{3,2,1,0:T(8,128)(2,1)S(1)}, u32[]{:S(2)}, u32[]{:S(2)}) collective-permute-start(bf16[2,5,24,768]{3,2,1,0:T(8,128)(2,1)S(1)} %pad_maximum_fusion.1.rest_2_), channel_id=1, source_target_pairs={{0,4},{1,5},{2,6},{3,7},{4,0},{5,1},{6,2},{7,3},{8,12},{9,13},{10,... | collective-permute-start | bytes 1105928 | tf_op jit(solution)/shard_map/ppermute | solution.py:319
  124.1 16.3 %collective-permute-start.45 = (bf16[2,24,3072]{2,1,0:T(8,128)(2,1)S(1)}, bf16[2,24,3072]{2,1,0:T(8,128)(2,1)S(1)}, u32[]{:S(2)}, u32[]{:S(2)}) collective-permute-start(bf16[2,24,3072]{2,1,0:T(8,128)(2,1)S(1)} %pad_maximum_fusion.5.rest_2_), channel_id=1, source_target_pairs={{0,4},{1,5},{2,6},{3,7},{4,0},{5,1},{6,2},{7,3},{8,12},{9,13},{10,... | collective-permute-start | bytes 884744 | tf_op jit(solution)/shard_map/ppermute | solution.py:319
  124.7 15.9 %collective-permute-start.40 = (bf16[2,24,3072]{2,1,0:T(8,128)(2,1)S(1)}, bf16[2,24,3072]{2,1,0:T(8,128)(2,1)S(1)}, u32[]{:S(2)}, u32[]{:S(2)}) collective-permute-start(bf16[2,24,3072]{2,1,0:T(8,128)(2,1)S(1)} %pad_maximum_fusion.5.rest_2_), channel_id=1, source_target_pairs={{0,1},{1,0},{2,3},{3,2},{4,5},{5,4},{6,7},{7,6},{8,9},{9,8},{10,11... | collective-permute-start | bytes 884744 | tf_op jit(solution)/shard_map/ppermute | solution.py:319
  124.9 16.0 %collective-permute-start.47 = (bf16[2,24,3072]{2,1,0:T(8,128)(2,1)S(1)}, bf16[2,24,3072]{2,1,0:T(8,128)(2,1)S(1)}, u32[]{:S(2)}, u32[]{:S(2)}) collective-permute-start(bf16[2,24,3072]{2,1,0:T(8,128)(2,1)S(1)} %collective-permute-done.37.rest_4_), channel_id=1, source_target_pairs={{0,2},{1,3},{2,0},{3,1},{4,6},{5,7},{6,4},{7,5},{8,10},{9,11},{10,... | collective-permute-start | bytes 884744 | tf_op jit(solution)/shard_map/ppermute | solution.py:319
  140.4 19.6 %collective-permute-start.42 = (bf16[2,24,3072]{2,1,0:T(8,128)(2,1)S(1)}, bf16[2,24,3072]{2,1,0:T(8,128)(2,1)S(1)}, u32[]{:S(2)}, u32[]{:S(2)}) collective-permute-start(bf16[2,24,3072]{2,1,0:T(8,128)(2,1)S(1)} %collective-permute-done.38.rest_6_), channel_id=1, source_target_pairs={{0,1},{1,0},{2,3},{3,2},{4,5},{5,4},{6,7},{7,6},{8,9},{9,8},{10,11... | collective-permute-start | bytes 884744 | tf_op jit(solution)/shard_map/ppermute | solution.py:319
  140.6 19.5 %collective-permute-start.44 = (bf16[2,24,3072]{2,1,0:T(8,128)(2,1)S(1)}, bf16[2,24,3072]{2,1,0:T(8,128)(2,1)S(1)}, u32[]{:S(2)}, u32[]{:S(2)}) collective-permute-start(bf16[2,24,3072]{2,1,0:T(8,128)(2,1)S(1)} %collective-permute-done.43.rest_8_), channel_id=1, source_target_pairs={{0,1},{1,0},{2,3},{3,2},{4,5},{5,4},{6,7},{7,6},{8,9},{9,8},{10,11... | collective-permute-start | bytes 884744 | tf_op jit(solution)/shard_map/ppermute | solution.py:319
  141.0 19.1 %collective-permute-start.46 = (bf16[2,24,3072]{2,1,0:T(8,128)(2,1)S(1)}, bf16[2,24,3072]{2,1,0:T(8,128)(2,1)S(1)}, u32[]{:S(2)}, u32[]{:S(2)}) collective-permute-start(bf16[2,24,3072]{2,1,0:T(8,128)(2,1)S(1)} %collective-permute-done.45.rest_10_), channel_id=1, source_target_pairs={{0,1},{1,0},{2,3},{3,2},{4,5},{5,4},{6,7},{7,6},{8,9},{9,8},{10,11... | collective-permute-start | bytes 884744 | tf_op jit(solution)/shard_map/ppermute | solution.py:319
  141.1 19.0 %collective-permute-start.48 = (bf16[2,24,3072]{2,1,0:T(8,128)(2,1)S(1)}, bf16[2,24,3072]{2,1,0:T(8,128)(2,1)S(1)}, u32[]{:S(2)}, u32[]{:S(2)}) collective-permute-start(bf16[2,24,3072]{2,1,0:T(8,128)(2,1)S(1)} %collective-permute-done.47.rest_12_), channel_id=1, source_target_pairs={{0,1},{1,0},{2,3},{3,2},{4,5},{5,4},{6,7},{7,6},{8,9},{9,8},{10,11... | collective-permute-start | bytes 884744 | tf_op jit(solution)/shard_map/ppermute | solution.py:319
  141.5 18.6 %collective-permute-start.50 = (bf16[2,24,3072]{2,1,0:T(8,128)(2,1)S(1)}, bf16[2,24,3072]{2,1,0:T(8,128)(2,1)S(1)}, u32[]{:S(2)}, u32[]{:S(2)}) collective-permute-start(bf16[2,24,3072]{2,1,0:T(8,128)(2,1)S(1)} %collective-permute-done.49.rest_14_), channel_id=1, source_target_pairs={{0,1},{1,0},{2,3},{3,2},{4,5},{5,4},{6,7},{7,6},{8,9},{9,8},{10,11... | collective-permute-start | bytes 884744 | tf_op jit(solution)/shard_map/ppermute | solution.py:319
  160.0 25.4 %collective-permute-start.73 = (bf16[16,24,3072]{2,1,0:T(8,128)(2,1)S(1)}, bf16[16,24,3072]{2,1,0:T(8,128)(2,1)S(1)}, u32[]{:S(2)}, u32[]{:S(2)}) collective-permute-start(bf16[16,24,3072]{2,1,0:T(8,128)(2,1)S(1)} %get-tuple-element.188), channel_id=1, source_target_pairs={{0,1},{1,0},{2,3},{3,2},{4,5},{5,4},{6,7},{7,6},{8,9},{9,8},{10,11... | collective-permute-start | bytes 7077896 | tf_op jit(solution)/shard_map/ppermute | solution.py:319
  187.9 114.9 %reduce-scatter.5.cloned.1.call-start = ((), (), s32[]{:S(2)}) async-start(), calls=%async_computation.3 | async-start | bytes 737280 | tf_op jit(solution)/shard_map/reduce_scatter | solution.py:1079
  190.4 26.2 %collective-permute-start.52 = (bf16[2,2,4,24,768]{4,3,2,1,0:T(8,128)(2,1)S(1)}, bf16[2,2,4,24,768]{4,3,2,1,0:T(8,128)(2,1)S(1)}, u32[]{:S(2)}, u32[]{:S(2)}) collective-permute-start(bf16[2,2,4,24,768]{4,3,2,1,0:T(8,128)(2,1)S(1)} %get-tuple-element.202), channel_id=1, source_target_pairs={{0,4},{1,5},{2,6},{3,7},{4,0},{5,1},{6,2},{7,3},{8,12},{9,13},{10,... | collective-permute-start | bytes 1769480 | tf_op jit(solution)/shard_map/ppermute | solution.py:319
  191.3 25.3 %collective-permute-start.53 = (bf16[2,2,4,24,768]{4,3,2,1,0:T(8,128)(2,1)S(1)}, bf16[2,2,4,24,768]{4,3,2,1,0:T(8,128)(2,1)S(1)}, u32[]{:S(2)}, u32[]{:S(2)}) collective-permute-start(bf16[2,2,4,24,768]{4,3,2,1,0:T(8,128)(2,1)S(1)} %get-tuple-element.200), channel_id=1, source_target_pairs={{0,2},{1,3},{2,0},{3,1},{4,6},{5,7},{6,4},{7,5},{8,10},{9,11},{10,... | collective-permute-start | bytes 1769480 | tf_op jit(solution)/shard_map/ppermute | solution.py:319
  222.8 26.4 %collective-permute-start.54 = (bf16[16,4,24,768]{3,2,1,0:T(8,128)(2,1)S(1)}, bf16[16,4,24,768]{3,2,1,0:T(8,128)(2,1)S(1)}, u32[]{:S(2)}, u32[]{:S(2)}) collective-permute-start(bf16[16,4,24,768]{3,2,1,0:T(8,128)(2,1)S(1)} %get-tuple-element.155), channel_id=1, source_target_pairs={{0,1},{1,0},{2,3},{3,2},{4,5},{5,4},{6,7},{7,6},{8,9},{9,8},{10,11... | collective-permute-start | bytes 7077896 | tf_op jit(solution)/shard_map/ppermute | solution.py:319
  251.0 18.4 %collective-permute-start.72 = (bf16[4,24,768]{2,1,0:T(8,128)(2,1)S(1)}, bf16[4,24,768]{2,1,0:T(8,128)(2,1)S(1)}, u32[]{:S(2)}, u32[]{:S(2)}) collective-permute-start(bf16[4,24,768]{2,1,0:T(8,128)(2,1)S(1)} %get-tuple-element.211), channel_id=1, source_target_pairs={{0,24},{1,25},{2,26},{3,27},{4,28},{5,29},{6,30},{7,31},{8,0},{9,1... | collective-permute-start | bytes 442376 | tf_op jit(solution)/shard_map/ppermute | solution.py:319
  251.1 20.8 %collective-permute-start.71 = (bf16[4,24,768]{2,1,0:T(8,128)(2,1)S(1)}, bf16[4,24,768]{2,1,0:T(8,128)(2,1)S(1)}, u32[]{:S(2)}, u32[]{:S(2)}) collective-permute-start(bf16[4,24,768]{2,1,0:T(8,128)(2,1)S(1)} %get-tuple-element.212), channel_id=1, source_target_pairs={{0,16},{1,17},{2,18},{3,19},{4,20},{5,21},{6,22},{7,23},{8,24},{9,... | collective-permute-start | bytes 442376 | tf_op jit(solution)/shard_map/ppermute | solution.py:319
  255.0 18.6 %collective-permute-start.70 = (bf16[4,24,768]{2,1,0:T(8,128)(2,1)S(1)}, bf16[4,24,768]{2,1,0:T(8,128)(2,1)S(1)}, u32[]{:S(2)}, u32[]{:S(2)}) collective-permute-start(bf16[4,24,768]{2,1,0:T(8,128)(2,1)S(1)} %get-tuple-element.213), channel_id=1, source_target_pairs={{0,8},{1,9},{2,10},{3,11},{4,12},{5,13},{6,14},{7,15},{8,16},{9,17... | collective-permute-start | bytes 442376 | tf_op jit(solution)/shard_map/ppermute | solution.py:319
  283.9 18.1 %collective-permute-start.68 = (bf16[4,24,768]{2,1,0:T(8,128)(2,1)S(1)}, bf16[4,24,768]{2,1,0:T(8,128)(2,1)S(1)}, u32[]{:S(2)}, u32[]{:S(2)}) collective-permute-start(bf16[4,24,768]{2,1,0:T(8,128)(2,1)S(1)} %get-tuple-element.216), channel_id=1, source_target_pairs={{0,16},{1,17},{2,18},{3,19},{4,20},{5,21},{6,22},{7,23},{8,24},{9,... | collective-permute-start | bytes 442376 | tf_op jit(solution)/shard_map/ppermute | solution.py:319
  (93 other events, 1242.4 us)
Sparse Core Ops, SparseCore 0:
  188.0 52.5 reduce-scatter.2
  279.9 22.5 reduce-scatter.4

commit v3 on v2

--- a/solution.py
+++ b/solution.py
@@ -312,10 +312,7 @@
             for x in range(self.x):
                 for y in range(self.y):
                     for c in range(self.c):
-                        target = self.index(
-                            (z + kz) % self.z, (x + kx) % self.x, (y + ky) % self.y, (c + kc) % self.c
-                        )
-                        pairs.append((self.index(z, x, y, c), target))
+                        pairs.append((self.index(z, x, y, c), self.index(z ^ kz, x ^ kx, y ^ ky, c ^ kc)))
         return lax.ppermute(values, AXES, pairs)
 
     def here(self):
@@ -324,58 +321,43 @@
     def me(self):
         return self.index(*self.here())
 
-    def away(self, kz, kx, ky, kc):
-        z, x, y, c = self.here()
-        return self.index(
-            lax.rem(z + (kz % self.z), self.z),
-            lax.rem(x + (kx % self.x), self.x),
-            lax.rem(y + (ky % self.y), self.y),
-            lax.rem(c + (kc % self.c), self.c),
-        )
+    def away(self, *bits):
+        return self.index(*(lax.bitwise_xor(at, jnp.int32(bit)) for at, bit in zip(self.here(), bits)))
 
 
 def tie(values, gate):
     return lax.optimization_barrier((values, gate))[0]
 
 
-def gather_begin(grid, own):
-    rows = [own]
-    for k in range(1, grid.z):
-        rows.append(grid.shift(own, kz=k))
-    half = grid.z // 2
-    first = jnp.stack(rows[:half])
-    second = jnp.stack(rows[half:])
-    return first, second
-
-
-def gather_middle(grid, begun):
-    first, second = begun
+def together(values):
+    return lax.optimization_barrier(values)
+
+
+COLUMN = (0, 3, 1, 2)
+
+
+def gather_one(grid, first, second):
     return first, second, grid.shift(first, kx=1), grid.shift(second, ky=1)
 
 
-def gather_end(grid, begun):
-    first, second, first_x, second_y = begun
-    half = grid.z // 2
-    first_y = grid.shift(first, ky=1)
-    second_x = grid.shift(second, kx=1)
-    first_xy = grid.shift(first_x, ky=1)
-    second_xy = grid.shift(second_y, kx=1)
-    arrays, places = [], []
-    for array, start, kx, ky in (
-        (first, 0, 0, 0),
-        (second, half, 0, 0),
-        (first_x, 0, 1, 0),
-        (second_y, half, 0, 1),
-        (first_y, 0, 0, 1),
-        (second_x, half, 1, 0),
-        (first_xy, 0, 1, 1),
-        (second_xy, half, 1, 1),
-    ):
-        arrays.append(array)
-        places.append([(-(start + k), -kx, -ky, 0) for k in range(half)])
-        arrays.append(grid.shift(array, kc=1))
-        places.append([(-(start + k), -kx, -ky, -1) for k in range(half)])
-    return arrays, places
+def gather_two(grid, four):
+    first, second, first_x, second_y = four
+    one = jnp.concatenate([first, first_x])
+    two = jnp.concatenate([second, second_y])
+    return one, two, grid.shift(one, ky=1), grid.shift(two, kx=1)
+
+
+def gather_core(grid, arrays):
+    return tuple(grid.shift(array, kc=1) for array in arrays)
+
+
+def gather_places():
+    first, second = COLUMN[:2], COLUMN[2:]
+    one = [(z, x, 0) for x in range(2) for z in first]
+    two = [(z, 0, y) for y in range(2) for z in second]
+    one_y = [(z, x, 1) for z, x, _ in one]
+    two_x = [(z, 1, y) for z, _, y in two]
+    return [[spot + (core,) for spot in group] for core, pair in ((0, 0), (0, 1), (1, 0), (1, 1)) for group in ((one, two), (one_y, two_x))[pair]]
 
 
 def place(grid, places, refs, held):
@@ -392,7 +374,7 @@
             for two in range(2):
                 for low in range(half):
                     kx, ky = (one, two) if which == 0 else (two, one)
-                    slots.append((which * half + low, kx, ky, core))
+                    slots.append((COLUMN[which * half + low], kx, ky, core))
     return slots
 
 
@@ -404,7 +386,17 @@
     return grid.shift(other, kc=1)
 
 
-def scatter_first(grid, own, arrived):
+def join(values, extra):
+    values = values.reshape(-1, 8, values.shape[-1])
+    return values if extra is None else jnp.concatenate([values, extra])
+
+
+def part(values, shape):
+    count = math.prod(shape[:-1]) // 8
+    return values[:count].reshape(shape), values[count:]
+
+
+def scatter_first(grid, own, arrived, extra=None):
     shape = (2, 2, 2, grid.z // 2) + own.shape[1:]
     own = own.reshape(shape)
     arrived = arrived.reshape(shape)
@@ -412,34 +404,51 @@
     send_b = plus(own[1, 1], arrived[1, 1])
     keep_a = plus(own[0, 0], arrived[0, 0])
     keep_b = plus(own[1, 0], arrived[1, 0])
-    return send_a, send_b, keep_a, keep_b, grid.shift(send_a, kx=1), grid.shift(send_b, ky=1)
+    if extra is not None:
+        send_a = join(send_a, extra.astype(BF16))
+    return keep_a, keep_b, grid.shift(send_a, kx=1), grid.shift(send_b, ky=1), extra
 
 
 def scatter_second(grid, state, gate):
-    _, _, keep_a, keep_b, got_a, got_b = state
+    keep_a, keep_b, got_a, got_b, extra = state
     got_a, got_b = tie((got_a, got_b), gate)
+    if extra is not None:
+        got_a, more = part(got_a, keep_a.shape)
+        extra = extra + more.astype(F32)
     next_a = plus(keep_a[1], got_a[1])
     next_b = plus(keep_b[1], got_b[1])
     rest_a = plus(keep_a[0], got_a[0])
     rest_b = plus(keep_b[0], got_b[0])
-    return next_a, rest_a, rest_b, grid.shift(next_a, ky=1), grid.shift(next_b, kx=1)
+    if extra is not None:
+        next_a = join(next_a, extra.astype(BF16))
+    return rest_a, rest_b, grid.shift(next_a, ky=1), grid.shift(next_b, kx=1), extra
 
 
 def scatter_third(grid, state, gate):
-    _, rest_a, rest_b, last_a, last_b = state
+    rest_a, rest_b, last_a, last_b, extra = state
     last_a, last_b = tie((last_a, last_b), gate)
+    if extra is not None:
+        last_a, more = part(last_a, rest_a.shape)
+        extra = extra + more.astype(F32)
     half = grid.z // 2
     parts = [plus(rest_a[k], last_a[k]) for k in range(half)] + [plus(rest_b[k], last_b[k]) for k in range(half)]
-    return parts + [grid.shift(parts[k], kz=k) for k in range(1, grid.z)]
+    sends = parts[1:]
+    if extra is not None:
+        sends = [join(send, extra.astype(BF16)) for send in sends]
+    return parts[0], [grid.shift(send, kz=k) for send, k in zip(sends, COLUMN[1:])], extra
 
 
 def scatter_last(state, gate):
-    count = (len(state) + 1) // 2
-    came = tie(list(state[count:]), gate)
-    total = state[0].astype(F32)
-    for part in came:
-        total = total + part.astype(F32)
-    return total
+    total, came, extra = state
+    shape = total.shape
+    came = tie(came, gate)
+    total = total.astype(F32)
+    for values in came:
+        if extra is not None:
+            values, more = part(values, shape)
+            extra = extra + more.astype(F32)
+        total = total + values.astype(F32)
+    return total if extra is None else (total, extra)
 
 
 def lanes_of(rows):
@@ -527,12 +536,13 @@
     count = len(places)
     refs, rest = rest[:count], rest[count:]
     moved_ref, normed_out, q_ref, k_ref, v_ref, vec_ref, held = rest
-    place(grid, places, refs, held)
+    total = jnp.zeros(vec_ref.shape, F32)
+    for ref, spots in zip(refs, places):
+        for slot, spot in enumerate(spots):
+            total = total + ref[slot, 0].astype(F32)
+            held[grid.away(*spot)] = ref[slot, 1:4]
+    vec_ref[...] = total
     width = hidden_ref.shape[1]
-    total = held[0, 0].astype(F32)
-    for j in range(1, grid.count):
-        total = total + held[j, 0].astype(F32)
-    vec_ref[...] = total
     rows = 256
 
     def block(step, carry):
@@ -540,9 +550,9 @@
         hidden = hidden_ref[at, :]
         hat, _ = normal(hidden.astype(F32))
         normed = (hat * vec_ref[0:1, :] + vec_ref[1:2, :]).astype(BF16)
-        q_ref[at, :] = (dot(normed, held[:, 1].reshape(width, width), NT) + vec_ref[2:3, :]).astype(BF16)
-        k_ref[at, :] = dot(normed, held[:, 2].reshape(width, width), NT).astype(BF16)
-        v_ref[at, :] = (dot(normed, held[:, 3].reshape(width, width), NT) + vec_ref[3:4, :]).astype(BF16)
+        q_ref[at, :] = (dot(normed, held[:, 0].reshape(width, width), NT) + vec_ref[2:3, :]).astype(BF16)
+        k_ref[at, :] = dot(normed, held[:, 1].reshape(width, width), NT).astype(BF16)
+        v_ref[at, :] = (dot(normed, held[:, 2].reshape(width, width), NT) + vec_ref[3:4, :]).astype(BF16)
         for t in range(rows // TILE):
             to = tile_rows(place_ref, step * (rows // TILE) + t)
             part = slice(t * TILE, (t + 1) * TILE)
@@ -642,7 +652,6 @@
 
     lax.fori_loop(0, captions, caption, 0)
     share = width // grid.count
-    core = lax.axis_index("c")
 
     def column(step, carry):
         lanes = rows_at(step, width)
@@ -651,14 +660,10 @@
             total[...] = dot(low_ref[0:rows, :], active_ref[0:rows, lanes], TN)
 
         by_size(place_ref[size_at], product)
-        for out_ref, owner in ((own_ref, core), (other_ref, 1 - core)):
-            slot = 0
-            for x in range(grid.x):
-                for y in range(grid.y):
-                    for z in range(grid.z):
-                        at = pl.multiple_of(grid.index(z, x, y, owner) * share, 8)
-                        out_ref[slot, :, lanes] = total[pl.ds(at, share), :].astype(BF16)
-                        slot += 1
+        for core, out_ref in ((0, own_ref), (1, other_ref)):
+            for slot, spot in enumerate(outgoing(grid, core)):
+                at = pl.multiple_of(grid.away(*spot) * share, 8)
+                out_ref[slot, :, lanes] = total[pl.ds(at, share), :].astype(BF16)
         return carry
 
     lax.fori_loop(0, active_ref.shape[1] // width, column, 0)
@@ -690,13 +695,14 @@
         by_size(place_ref[size_at], product)
         for k in range(per // 2):
             chip = step * (per // 2) + k
-            kz = lax.rem(lax.div(chip, grid.x * grid.y) - z + grid.z, grid.z)
-            kx = lax.rem(lax.rem(lax.div(chip, grid.y), grid.x) - x + grid.x, grid.x)
-            ky = lax.rem(lax.rem(chip, grid.y) - y + grid.y, grid.y)
-            which = lax.div(kz, half)
+            kz = lax.bitwise_xor(lax.div(chip, grid.x * grid.y), z)
+            kx = lax.bitwise_xor(lax.rem(lax.div(chip, grid.y), grid.x), x)
+            ky = lax.bitwise_xor(lax.rem(chip, grid.y), y)
+            low = lax.div(kz, 2)
+            which = lax.bitwise_xor(low, lax.rem(kz, 2))
             one = jnp.where(which == 0, kx, ky)
             two = jnp.where(which == 0, ky, kx)
-            slot = ((which * 2 + one) * 2 + two) * half + lax.rem(kz, half)
+            slot = ((which * 2 + one) * 2 + two) * half + low
             own_at = pl.multiple_of(2 * share * k + mine, 8)
             other_at = pl.multiple_of(2 * share * k + (share - mine), 8)
             own_ref[slot] = total[pl.ds(own_at, share), :].astype(BF16).reshape(shape)
@@ -823,9 +829,9 @@
 
     def block(step, carry):
         at = rows_at(step, rows)
-        grads = dot(grads_ref[0, at, :], held[:, 1].reshape(width, width), NN)
-        grads = grads + dot(grads_ref[1, at, :], held[:, 2].reshape(width, width), NN)
-        grads = grads + dot(grads_ref[2, at, :], held[:, 3].reshape(width, width), NN)
+        grads = dot(grads_ref[0, at, :], held[:, 0].reshape(width, width), NN)
+        grads = grads + dot(grads_ref[1, at, :], held[:, 1].reshape(width, width), NN)
+        grads = grads + dot(grads_ref[2, at, :], held[:, 2].reshape(width, width), NN)
         hat, scale = normal(moved_ref[at, :].astype(F32))
         found[at, :] = grad_ref[at, :] + normal_back(hat, scale, vec_in[0:1, :], grads)
         vec_ref[0:1, :] += jnp.sum(grads * hat, axis=0, keepdims=True)
@@ -879,7 +885,7 @@
 FAST = pl.BlockSpec(memory_space=pltpu.VMEM)
 
 
-def call(kernel, steps, in_specs, out_specs, outs, scratch, flops, moved, name, limit=10):
+def call(kernel, steps, in_specs, out_specs, outs, scratch, flops, moved, name, limit=8):
     return pl.pallas_call(
         kernel,
         grid=(steps,),
@@ -893,11 +899,12 @@
     )
 
 
-def call_near(kernel, in_specs, outs, scratch, flops, name, limit=10):
+def call_near(kernel, in_specs, outs, scratch, flops, name, limit=8, aliases=None):
     return pl.pallas_call(
         kernel,
         in_specs=in_specs,
         out_specs=[FAST] * len(outs),
+        input_output_aliases=aliases or {},
         out_shape=[jax.ShapeDtypeStruct(s, d) for s, d in outs],
         scratch_shapes=scratch,
         compiler_params=pltpu.CompilerParams(vmem_limit_bytes=limit * 1024 * 1024),
@@ -952,12 +959,22 @@
     third = downmat.T
     where = order_of(lengths, length)
     size_at = captions * (length // TILE) + captions
-    begun = lax.optimization_barrier(gather_begin(grid, first))
-    second_begun = lax.optimization_barrier(gather_begin(grid, tie(second, begun)))
-    third_begun = lax.optimization_barrier(gather_begin(grid, tie(third, second_begun)))
-    begun = lax.optimization_barrier(gather_middle(grid, begun))
-    first_in, places = gather_end(grid, begun)
-    second_begun = gather_middle(grid, tie(second_begun, first_in))
+    places = gather_places()
+    first_a = jnp.stack([first, grid.shift(first, kz=3)])
+    first_a, second = together((first_a, second))
+    first_z = grid.shift(first_a, kz=1)
+    second_a = jnp.stack([second, grid.shift(second, kz=3)])
+    first_a, first_z, second_a = together((first_a, first_z, second_a))
+    first_a = gather_one(grid, first_a, first_z)
+    second_z = grid.shift(second_a, kz=1)
+    first_a, second_z, third = together((first_a, second_z, third))
+    first_b = gather_two(grid, first_a)
+    first_c = gather_core(grid, first_b[:2])
+    third_a = jnp.stack([third, grid.shift(third, kz=3)])
+    first_b, first_c, third_a = together((first_b, first_c, third_a))
+    first_in = first_b + first_c + gather_core(grid, first_b[2:])
+    second_a = gather_one(grid, second_a, tie(second_z, first_b))
+    third_z = grid.shift(third_a, kz=1)
     half = grid.count // 2
     unit = 2 * tokens * width * width
     row = (tokens, width)
@@ -967,14 +984,14 @@
     moved, normed, query, keys, values, vec, held_one = call_near(
         functools.partial(project_kernel, grid, places),
         [SMEM] + [FAST] * (1 + len(first_in)),
-        [(row, BF16)] * 5 + [((share, width), F32), ((grid.count,) + first.shape, BF16)],
+        [(row, BF16)] * 5 + [((share, width), F32), ((grid.count, 3, share, width), BF16)],
         [],
         5 * unit,
         "project",
     )(where, hidden2, *first_in)
-    second_begun, third_begun = tie((second_begun, third_begun), vec)
-    second_in, _ = gather_end(grid, second_begun)
-    third_begun = gather_middle(grid, third_begun)
+    second_a, third_z, query = together((second_a, third_z, query))
+    second_b = gather_two(grid, second_a)
+    second_c = gather_core(grid, second_b[:2])
     probs, mixed = call_near(
         functools.partial(attend_kernel, length, 4),
         [SMEM] * 2 + [FAST] * 3,
@@ -983,7 +1000,9 @@
         5 * unit,
         "attend",
     )(lengths, where, query, keys, values)
-    third_in, _ = gather_end(grid, tie(third_begun, second_in))
+    second_b, second_c, third_z, mixed = together((second_b, second_c, third_z, mixed))
+    second_in = second_b + second_c + gather_core(grid, second_b[2:])
+    third_a = gather_one(grid, third_a, third_z)
     middle, normed2, active, slope, held_two = call_near(
         functools.partial(upper_kernel, grid, places),
         [FAST] * (3 + len(second_in)),
@@ -992,6 +1011,9 @@
         9 * unit,
         "upper",
     )(moved, mixed, vec, *second_in)
+    third_a, active = together((third_a, active))
+    third_b = gather_two(grid, third_a)
+    third_c = gather_core(grid, third_b[:2])
     low, down_vec, down_own, down_other = call_near(
         functools.partial(down_grad_kernel, grid, length, size_at),
         [SMEM] * 2 + [FAST] * 2,
@@ -1000,7 +1022,10 @@
         5 * unit,
         "down_grad",
     )(lengths, where, cot2, active)
-    down_came = grid.shift(down_other, kc=1)
+    third_b, third_c, down_own = together((third_b, third_c, down_own))
+    third_in = third_b + third_c + gather_core(grid, third_b[2:])
+    down_two = scatter_first(grid, down_own, scatter_core(grid, down_other))
+    low = tie(low, down_two[0])
     grad_upper, up_vec, up_own, up_other, lower_w = call_near(
         functools.partial(upper_grad_kernel, grid, places, size_at),
         [SMEM] + [FAST] * (3 + len(third_in)),
@@ -1010,12 +1035,11 @@
         [square],
         8 * unit,
         "upper_grad",
+        aliases={2: 0},
     )(where, low, slope, normed2, *third_in)
-    down_came = tie(down_came, up_vec)
-    down_part = down_own.astype(F32) + down_came.astype(F32)
-    down_part = down_part.astype(BF16).reshape(half * share, ff)
-    down_part = lax.psum_scatter(down_part, ("x", "y"), scatter_dimension=0, tiled=True)
+    down_three = scatter_second(grid, down_two, up_vec)
     up_one = scatter_core(grid, up_other)
+    grad_upper = tie(grad_upper, down_three[0])
     grad_middle, branch, dm, mid_vec = call_near(
         functools.partial(middle_grad_kernel, grid, size_at),
         [SMEM] + [FAST] * 5,
@@ -1024,8 +1048,9 @@
         6 * unit,
         "middle_grad",
     )(where, grad_upper, middle, low, vec, held_two)
+    down_four = scatter_third(grid, down_three, mid_vec)
     up_two = scatter_first(grid, up_own, tie(up_one, mid_vec))
-    dm = tie(dm, up_two[0])
+    dm = tie(dm, (up_two[0], down_four[0]))
     grads, att_vec = call_near(
         functools.partial(attend_grad_kernel, length, 4),
         [SMEM] * 2 + [FAST] * 5,
@@ -1044,7 +1069,8 @@
         5 * unit,
         "weight_grad",
     )(where, grads, branch, normed, mixed)
-    up_four = scatter_third(grid, up_three, att_own[0, 0, 0:8, 0:128])
+    att_gate = att_own[0, 0, 0:8, 0:128]
+    up_four = scatter_third(grid, up_three, att_gate)
     att_one = scatter_core(grid, att_other)
     grad_middle = tie(grad_middle, up_four[0])
     input_grad, all_vec = call_near(
@@ -1055,8 +1081,10 @@
         5 * unit,
         "input_grad",
     )(where, moved, grad_middle, grads, vec, down_vec, up_vec, mid_vec, att_vec, held_one)
-    att_two = scatter_first(grid, att_own, tie(att_one, all_vec))
+    down_sum = scatter_last(down_four, all_vec)
     up_sum = scatter_last(up_four, all_vec)
+    all_vec = (all_vec + grid.shift(all_vec, kc=1)).reshape(2, 8, width)
+    att_two = scatter_first(grid, att_own, tie(att_one, all_vec), all_vec)
     middle = tie(middle, att_two[0])
     steps = 4
     rows = tokens // steps
@@ -1073,16 +1101,11 @@
         "lower",
         24,
     )(where, active, middle, vec, lower_w)
-    att_three = scatter_second(grid, att_two, block_out[0:8, 0:128])
-    att_four = scatter_third(grid, att_three, block_out[0:8, 0:128])
-    att_sum = scatter_last(att_four, block_out[0:8, 0:128])
-    down_sum = lax.psum_scatter(down_part, "z", scatter_dimension=0, tiled=True).astype(F32)
-    all_vec = all_vec + grid.shift(all_vec, kc=1)
-    all_vec = all_vec + grid.shift(all_vec, kx=1)
-    all_vec = all_vec + grid.shift(all_vec, ky=1)
-    all_vec = (
-        all_vec + grid.shift(all_vec, kz=1) + grid.shift(all_vec, kz=2) + grid.shift(all_vec, kz=3)
-    )
+    out_gate = block_out[0:8, 0:128]
+    att_three = scatter_second(grid, att_two, out_gate)
+    att_four = scatter_third(grid, att_three, out_gate)
+    att_sum, all_vec = scatter_last(att_four, out_gate)
+    all_vec = all_vec.reshape(16, width)
     vecs = call(
         functools.partial(unpack_kernel, grid),
         1,

time: 313 us -> 257 us (0.82)
  waiting for transfers between devices: 117 us -> 82.8 us
  Pallas kernels: 91.5 us -> 72.8 us
  between operations: 15.8 us -> 2.33 us
  local copies, waits for them, and re-layouts: 12.9 us -> 23.2 us
  other arithmetic: 15.8 us -> 12.3 us
    ppermute x74 -> x55, waiting for transfers between devices: 117 us -> 82.8 us  [shift(): return lax.ppermute(values, AXES, pairs)]
    pallas_call x1, Pallas kernels: 18.3 us -> 5.16 us  [fast_device(): call_near(functools.partial(down_grad_kernel, grid, length, size_at), [SM...]
    unnamed x82 -> x74, local copies, waits for them, and re-layouts: 10.8 us -> 20.9 us
    pallas_call x1, Pallas kernels: 12.5 us -> 8.98 us  [fast_device(): call_near(functools.partial(upper_grad_kernel, grid, places, size_at), [S...]
    ppermute x74 -> x55, starting transfers between devices: 58.3 us -> 60.5 us  [shift(): return lax.ppermute(values, AXES, pairs)]
  transfers between devices with their start and end apart: 76 -> 55, of which waited for: 29 -> 27; matrix products, arithmetic and copies ran while one was open for 5% -> 4% of each run, Pallas kernels for 29% -> 26%
where the time goes in v3:
time: 257 us; the launch traced here: 254 us
  waiting for transfers between devices  82.8 us (32%)
  Pallas kernels  72.8 us (28%)
  starting transfers between devices  60.5 us (24%)
  local copies, waits for them, and re-layouts  23.2 us (9%)
  other arithmetic  12.3 us (5%)
    ppermute x55, waiting for transfers between devices, shift(): return lax.ppermute(values, AXES, pairs)  82.8 us
    ppermute x55, starting transfers between devices, shift(): return lax.ppermute(values, AXES, pairs)  60.5 us
    unnamed x74, local copies, waits for them, and re-layouts  20.9 us
    pallas_call x1, Pallas kernels, fast_device(): call_near(functools.partial(upper_kernel, grid, places), [FAST] * (3 + le...  12.9 us
    pallas_call x1, Pallas kernels, fast_device(): call_near(functools.partial(upper_grad_kernel, grid, places, size_at), [S...  8.98 us
    pallas_call x1, Pallas kernels, fast_device(): call_near(functools.partial(project_kernel, grid, places), [SMEM] + [FAST...  7.82 us
    pallas_call x1, Pallas kernels, fast_device(): call(lower_kernel, steps, [SMEM, pl.BlockSpec((rows, ff), lambda i: (i, 0...  7.55 us
    pallas_call x1, Pallas kernels, fast_device(): call_near(functools.partial(attend_grad_kernel, length, 4), [SMEM] * 2 +...  7.16 us
  transfers between devices with their start and end apart: 55, of which 27 were waited for; matrix products, arithmetic and copies ran while one was open for 4% of the time, Pallas kernels for 26%

profile of v3, /device:TPU:0, one launch (start us, length us, event | category | flops | bytes accessed | tf_op | source)
XLA Modules:
  0.0 254.0 jit_solution(16575884432734253128)
XLA Ops:
  4.5 5.1 %collective-permute-start = (bf16[4,24,768]{2,1,0:T(8,128)(2,1)S(1)}, bf16[4,24,768]{2,1,0:T(8,128)(2,1)S(1)}, u32[]{:S(2)}, u32[]{:S(2)}) collective-permute-start(bf16[4,24,768]{2,1,0:T(8,128)(2,1)S(1)} %pack.1), channel_id=1, source_target_pairs={{0,24},{1,25},{2,26},{3,27},{4,28},{5,29},{6,30},{7,31},{8,16},{9,... | collective-permute-start | bytes 442376 | tf_op jit(solution)/shard_map/ppermute | solution.py:316
  10.6 3.0 %collective-permute-done = bf16[4,24,768]{2,1,0:T(8,128)(2,1)S(1)} collective-permute-done((bf16[4,24,768]{2,1,0:T(8,128)(2,1)S(1)}, bf16[4,24,768]{2,1,0:T(8,128)(2,1)S(1)}, u32[]{:S(2)}, u32[]{:S(2)}) %collective-permute-start) | collective-permute-done | bytes 147488 | tf_op jit(solution)/shard_map/ppermute | solution.py:316
  13.6 3.6 %collective-permute-start.2 = (bf16[5,24,768]{2,1,0:T(8,128)(2,1)S(1)}, bf16[5,24,768]{2,1,0:T(8,128)(2,1)S(1)}, u32[]{:S(2)}, u32[]{:S(2)}) collective-permute-start(bf16[5,24,768]{2,1,0:T(8,128)(2,1)S(1)} %pad_maximum_fusion.8), channel_id=1, source_target_pairs={{0,24},{1,25},{2,26},{3,27},{4,28},{5,29},{6,30},{7,31},{8,16},{9,... | collective-permute-start | bytes 552968 | tf_op jit(solution)/shard_map/ppermute | solution.py:316
  18.1 5.1 %collective-permute-done.2 = bf16[5,24,768]{2,1,0:T(8,128)(2,1)S(1)} collective-permute-done((bf16[5,24,768]{2,1,0:T(8,128)(2,1)S(1)}, bf16[5,24,768]{2,1,0:T(8,128)(2,1)S(1)}, u32[]{:S(2)}, u32[]{:S(2)}) %collective-permute-start.2) | collective-permute-done | bytes 184352 | tf_op jit(solution)/shard_map/ppermute | solution.py:316
  23.2 4.5 %collective-permute-done.1 = bf16[2,4,24,768]{3,2,1,0:T(8,128)(2,1)S(1)} collective-permute-done((bf16[2,4,24,768]{3,2,1,0:T(8,128)(2,1)S(1)}, bf16[2,4,24,768]{3,2,1,0:T(8,128)(2,1)S(1)}, u32[]{:S(2)}, u32[]{:S(2)}) %collective-permute-start.1) | collective-permute-done | bytes 294944 | tf_op jit(solution)/shard_map/ppermute | solution.py:316
  32.1 3.9 %collective-permute-done.3 = bf16[2,4,24,768]{3,2,1,0:T(8,128)(2,1)S(1)} collective-permute-done((bf16[2,4,24,768]{3,2,1,0:T(8,128)(2,1)S(1)}, bf16[2,4,24,768]{3,2,1,0:T(8,128)(2,1)S(1)}, u32[]{:S(2)}, u32[]{:S(2)}) %collective-permute-start.3) | collective-permute-done | bytes 294944 | tf_op jit(solution)/shard_map/ppermute | solution.py:316
  44.1 5.4 %collective-permute-done.10 = bf16[24,3072]{1,0:T(8,128)(2,1)} collective-permute-done((bf16[24,3072]{1,0:T(8,128)(2,1)}, bf16[24,3072]{1,0:T(8,128)(2,1)}, u32[]{:S(2)}, u32[]{:S(2)}) %collective-permute-start.10) | collective-permute-done | bytes 147488 | tf_op jit(solution)/shard_map/ppermute | solution.py:316
  51.2 3.1 %collective-permute-done.7.rest_3_ = bf16[4,4,24,768]{3,2,1,0:T(8,128)(2,1)} collective-permute-done((bf16[4,4,24,768]{3,2,1,0:T(8,128)(2,1)S(1)}, bf16[4,4,24,768]{3,2,1,0:T(8,128)(2,1)}, u32[]{:S(2)}, u32[]{:S(2)}) %collective-permute-start.7) | collective-permute-done | bytes 589856 | tf_op jit(solution)/shard_map/ppermute | solution.py:316
  62.9 7.8 %project.1 = (bf16[1024,768]{1,0:T(8,128)(2,1)S(1)}, bf16[1024,768]{1,0:T(8,128)(2,1)S(1)}, bf16[1024,768]{1,0:T(8,128)(2,1)S(1)}, bf16[1024,768]{1,0:T(8,128)(2...) custom-call(s32[82]{0:T(128)S(1)} %pad_add_fusion.place_ref, ...), custom_call_target="tpu_custom_call" | custom-call | flops 6039797760 | bytes 1000000 | tf_op jit(solution)/shard_map/project/pallas_call | solution.py:984
  74.1 4.8 %attend.1 = (bf16[48,64,256]{2,1,0:T(8,128)(2,1)S(1)}, bf16[1024,768]{1,0:T(8,128)(2,1)S(1)}) custom-call(s32[16]{0:T(128)S(1)} %copy-done.3, s32[82]{0:T(128)S(1)} %pad_add_fusion.place_ref, bf16[1024,768]{1,0:T(8,128)(2,1)S(1)} %get-tuple-element.154.q_ref, bf16[1024,768]{1,0:T(8,128)(2,1)S(1)} %get-tuple-element.155.k_ref, ...), custom_call_target="tpu_custom_call" | custom-call | flops 6039797760 | bytes 1000000 | tf_op jit(solution)/shard_map/attend/pallas_call | solution.py:995
  78.9 12.1 %collective-permute-done.17.rest_3_ = bf16[4,5,24,768]{3,2,1,0:T(8,128)(2,1)S(1)} collective-permute-done((bf16[4,5,24,768]{3,2,1,0:T(8,128)(2,1)S(1)}, bf16[4,5,24,768]{3,2,1,0:T(8,128)(2,1)S(1)}, u32[]{:S(2)}, u32[]{:S(2)}) %collective-permute-start.17) | collective-permute-done | bytes 737312 | tf_op jit(solution)/shard_map/ppermute | solution.py:316
  95.5 12.9 %upper.1 = (f32[1024,768]{1,0:T(8,128)S(1)}, bf16[1024,768]{1,0:T(8,128)(2,1)S(1)}, bf16[1024,3072]{1,0:T(8,128)(2,1)S(1)}, bf16[1024,3072]{1,0:T(8,128)(2,1)S(1)}, bf16[32,5,24,768]{3,2,1,0:T(8,128)(2,1)S(1)}) custom-call(bf16[1024,768]{1,0:T(8,128)(2,1)S(1)} %get-tuple-element.159.moved_ref, bf16[1024,768]{1,0:T(8,128)(2,1)S(1)} %get-tuple-element.160.mixed_ref, ...), custom_call_target="tpu_custom_call" | custom-call | flops 10871635968 | bytes 1000000 | tf_op jit(solution)/shard_map/upper/pallas_call | solution.py:1006
  113.6 5.2 %down_grad.1 = (bf16[1024,768]{1,0:T(8,128)(2,1)S(1)}, f32[8,768]{1,0:T(8,128)S(1)}, bf16[16,24,3072]{2,1,0:T(8,128)(2,1)S(1)}, bf16[16,24,3072]{2,1,0:T(8,128)(2,1)S(1)}) custom-call(s32[16]{0:T(128)S(1)} %copy-done.3, s32[82]{0:T(128)S(1)} %pad_add_fusion.place_ref, bf16[1024,768]{1,0:T(8,128)(2,1)S(1)} %bitcast.253, ...), custom_call_target="tpu_custom_call" | custom-call | flops 6039797760 | bytes 1000000 | tf_op jit(solution)/shard_map/down_grad/pallas_call | solution.py:1017
  124.2 11.0 %collective-permute-done.25.rest_3_ = bf16[4,24,3072]{2,1,0:T(8,128)(2,1)S(1)} collective-permute-done((bf16[4,24,3072]{2,1,0:T(8,128)(2,1)S(1)}, bf16[4,24,3072]{2,1,0:T(8,128)(2,1)S(1)}, u32[]{:S(2)}, u32[]{:S(2)}) %collective-permute-start.25) | collective-permute-done | bytes 589856 | tf_op jit(solution)/shard_map/ppermute | solution.py:316
  143.2 9.0 %upper_grad.1 = (bf16[1024,3072]{1,0:T(8,128)(2,1)S(1)}, f32[32,768]{1,0:T(8,128)S(1)}, bf16[16,4,24,768]{3,2,1,0:T(8,128)(2,1)S(1)}, bf16[16,4,24,768]{3,2,1,0:T(8,128)(2,1)S(1)}, bf16[32,24,3072]{2,1,0:T(8,128)(2,1)S(1)}) custom-call(s32[82]{0:T(128)S(1)} %pad_add_fusion.place_ref, ...), custom_call_target="tpu_custom_call", output_to_operand_aliasing={{0}: (2, {})} | custom-call | flops 9663676416 | bytes 1000000 | tf_op jit(solution)/shard_map/upper_grad/pallas_call | solution.py:1029
  155.1 4.1 %collective-permute-start.37 = (bf16[2,24,3072]{2,1,0:T(8,128)(2,1)S(1)}, bf16[2,24,3072]{2,1,0:T(8,128)(2,1)S(1)}, u32[]{:S(2)}, u32[]{:S(2)}) collective-permute-start(bf16[2,24,3072]{2,1,0:T(8,128)(2,1)S(1)} %get-tuple-element.260), channel_id=1, source_target_pairs={{0,4},{1,5},{2,6},{3,7},{4,0},{5,1},{6,2},{7,3},{8,12},{9,13},{10,... | collective-permute-start | bytes 884744 | tf_op jit(solution)/shard_map/ppermute | solution.py:316
  165.9 6.7 %middle_grad.1 = (f32[1024,768]{1,0:T(8,128)S(1)}, bf16[1024,768]{1,0:T(8,128)(2,1)S(1)}, bf16[1088,768]{1,0:T(8,128)(2,1)S(1)}, f32[8,768]{1,0:T(8,128)S(1)}) custom-call(s32[82]{0:T(128)S(1)} %pad_add_fusion.place_ref, bf16[1024,3072]{1,0:T(8,128)(2,1)S(1)} %copy-done.9, f32[1024,768]{1,0:T(8,128)S(1)} %get-tuple-element.170.middle_ref, ...), custom_call_target="tpu_custom_call" | custom-call | flops 7247757312 | bytes 1000000 | tf_op jit(solution)/shard_map/middle_grad/pallas_call | solution.py:1043
  176.2 7.2 %attend_grad.1 = (bf16[3,1280,768]{2,1,0:T(8,128)(2,1)S(1)}, f32[8,768]{1,0:T(8,128)S(1)}) custom-call(s32[16]{0:T(128)S(1)} %copy-done.3, s32[82]{0:T(128)S(1)} %pad_add_fusion.place_ref, bf16[1088,768]{1,0:T(8,128)(2,1)S(1)} %get-tuple-element.200.dm_ref, bf16[1024,768]{1,0:T(8,128)(2,1)S(1)} %copy-done.21, bf16[1024,768]{1,0:T(8,128)(2,1)S(1)} %copy-done.23, ...), custom_call_target="tpu_custom_call" | custom-call | flops 8455716864 | bytes 1000000 | tf_op jit(solution)/shard_map/attend_grad/pallas_call | solution.py:1054
  183.4 4.7 %weight_grad.1 = (bf16[16,4,24,768]{3,2,1,0:T(8,128)(2,1)S(1)}, bf16[16,4,24,768]{3,2,1,0:T(8,128)(2,1)S(1)}) custom-call(s32[82]{0:T(128)S(1)} %pad_add_fusion.place_ref, bf16[3,1280,768]{2,1,0:T(8,128)(2,1)S(1)} %get-tuple-element.207.grads_ref, bf16[1024,768]{1,0:T(8,128)(2,1)S(1)} %get-tuple-element.212.branch_ref, bf16[1024,768]{1,0:T(8,128)(2,1)S(1)} %copy-done.17, ...), custom_call_target="tpu_custom_call" | custom-call | flops 6039797760 | bytes 1000000 | tf_op jit(solution)/shard_map/weight_grad/pallas_call | solution.py:1064
  192.1 7.2 %collective-permute-done.39 = bf16[2,4,24,768]{3,2,1,0:T(8,128)(2,1)S(1)} collective-permute-done((bf16[2,4,24,768]{3,2,1,0:T(8,128)(2,1)S(1)}, bf16[2,4,24,768]{3,2,1,0:T(8,128)(2,1)S(1)}, u32[]{:S(2)}, u32[]{:S(2)}) %collective-permute-start.39) | collective-permute-done | bytes 294944 | tf_op jit(solution)/shard_map/ppermute | solution.py:316
  200.5 6.3 %input_grad.1 = (f32[1024,768]{1,0:T(8,128)}, f32[16,768]{1,0:T(8,128)S(1)}) custom-call(s32[82]{0:T(128)S(1)} %pad_add_fusion.place_ref, bf16[1024,768]{1,0:T(8,128)(2,1)S(1)} %copy-done.15, f32[1024,768]{1,0:T(8,128)S(1)} %get-tuple-element.206.grad_ref, bf16[3,1280,768]{2,1,0:T(8,128)(2,1)S(1)} %get-tuple-element.207.grads_ref, ...), custom_call_target="tpu_custom_call" | custom-call | flops 6039797760 | bytes 1000000 | tf_op jit(solution)/shard_map/input_grad/pallas_call | solution.py:1076
  215.1 7.6 %lower.1 = bf16[1024,768]{1,0:T(8,128)(2,1)} custom-call(s32[82]{0:T(128)S(1)} %pad_add_fusion.place_ref, bf16[1024,3072]{1,0:T(8,128)(2,1)S(1)} %get-tuple-element.169.active_ref, f32[1024,768]{1,0:T(8,128)S(1)} %get-tuple-element.170.middle_ref, f32[24,768]{1,0:T(8,128)S(1)} %get-tuple-element.161.vec_ref.vec_in, ...), custom_call_target="tpu_custom_call" | custom-call | flops 4831838208 | bytes 20000000 | tf_op jit(solution)/shard_map/lower/pallas_call | solution.py:1092
  232.4 4.2 %collective-permute-done.51 = bf16[4,24,768]{2,1,0:T(8,128)(2,1)S(1)} collective-permute-done((bf16[4,24,768]{2,1,0:T(8,128)(2,1)S(1)}, bf16[4,24,768]{2,1,0:T(8,128)(2,1)S(1)}, u32[]{:S(2)}, u32[]{:S(2)}) %collective-permute-start.51) | collective-permute-done | bytes 147488 | tf_op jit(solution)/shard_map/ppermute | solution.py:316
  243.7 8.5 %collective-permute-done.48 = bf16[14,8,768]{2,1,0:T(8,128)(2,1)S(1)} collective-permute-done((bf16[14,8,768]{2,1,0:T(8,128)(2,1)S(1)}, bf16[14,8,768]{2,1,0:T(8,128)(2,1)S(1)}, u32[]{:S(2)}, u32[]{:S(2)}) %collective-permute-start.48) | collective-permute-done | bytes 172064 | tf_op jit(solution)/shard_map/ppermute | solution.py:316
  (234 shorter events, 98.7 us)
Async XLA Ops:
  38.5 15.8 %collective-permute-start.7 = (bf16[4,4,24,768]{3,2,1,0:T(8,128)(2,1)S(1)}, bf16[4,4,24,768]{3,2,1,0:T(8,128)(2,1)}, u32[]{:S(2)}, u32[]{:S(2)}) collective-permute-start(bf16[4,4,24,768]{3,2,1,0:T(8,128)(2,1)S(1)} %constant_dynamic-update-slice_fusion.2.rest_1_), channel_id=1, source_target_pairs={{0,4},{1,5},{2,6},{3,7},{4,0},{5,1},{6,2},{7,3},{8,12},{9,13},{10,... | collective-permute-start | bytes 1769480 | tf_op jit(solution)/shard_map/ppermute | solution.py:316
  39.7 14.6 %collective-permute-start.8 = (bf16[4,4,24,768]{3,2,1,0:T(8,128)(2,1)S(1)}, bf16[4,4,24,768]{3,2,1,0:T(8,128)(2,1)}, u32[]{:S(2)}, u32[]{:S(2)}) collective-permute-start(bf16[4,4,24,768]{3,2,1,0:T(8,128)(2,1)S(1)} %constant_dynamic-update-slice_fusion.rest_0_), channel_id=1, source_target_pairs={{0,1},{1,0},{2,3},{3,2},{4,5},{5,4},{6,7},{7,6},{8,9},{9,8},{10,11... | collective-permute-start | bytes 1769480 | tf_op jit(solution)/shard_map/ppermute | solution.py:316
  39.9 15.7 %collective-permute-start.6 = (bf16[4,4,24,768]{3,2,1,0:T(8,128)(2,1)S(1)}, bf16[4,4,24,768]{3,2,1,0:T(8,128)(2,1)}, u32[]{:S(2)}, u32[]{:S(2)}) collective-permute-start(bf16[4,4,24,768]{3,2,1,0:T(8,128)(2,1)S(1)} %constant_dynamic-update-slice_fusion.rest_0_), channel_id=1, source_target_pairs={{0,2},{1,3},{2,0},{3,1},{4,6},{5,7},{6,4},{7,5},{8,10},{9,11},{10,... | collective-permute-start | bytes 1769480 | tf_op jit(solution)/shard_map/ppermute | solution.py:316
  72.1 18.9 %collective-permute-start.17 = (bf16[4,5,24,768]{3,2,1,0:T(8,128)(2,1)S(1)}, bf16[4,5,24,768]{3,2,1,0:T(8,128)(2,1)S(1)}, u32[]{:S(2)}, u32[]{:S(2)}) collective-permute-start(bf16[4,5,24,768]{3,2,1,0:T(8,128)(2,1)S(1)} %constant_dynamic-update-slice_fusion.6.rest_1_), channel_id=1, source_target_pairs={{0,4},{1,5},{2,6},{3,7},{4,0},{5,1},{6,2},{7,3},{8,12},{9,13},{10,... | collective-permute-start | bytes 2211848 | tf_op jit(solution)/shard_map/ppermute | solution.py:316
  73.2 17.8 %collective-permute-start.18 = (bf16[4,5,24,768]{3,2,1,0:T(8,128)(2,1)S(1)}, bf16[4,5,24,768]{3,2,1,0:T(8,128)(2,1)S(1)}, u32[]{:S(2)}, u32[]{:S(2)}) collective-permute-start(bf16[4,5,24,768]{3,2,1,0:T(8,128)(2,1)S(1)} %constant_dynamic-update-slice_fusion.4.rest_0_), channel_id=1, source_target_pairs={{0,1},{1,0},{2,3},{3,2},{4,5},{5,4},{6,7},{7,6},{8,9},{9,8},{10,11... | collective-permute-start | bytes 2211848 | tf_op jit(solution)/shard_map/ppermute | solution.py:316
  73.3 18.9 %collective-permute-start.16 = (bf16[4,5,24,768]{3,2,1,0:T(8,128)(2,1)S(1)}, bf16[4,5,24,768]{3,2,1,0:T(8,128)(2,1)S(1)}, u32[]{:S(2)}, u32[]{:S(2)}) collective-permute-start(bf16[4,5,24,768]{3,2,1,0:T(8,128)(2,1)S(1)} %constant_dynamic-update-slice_fusion.4.rest_0_), channel_id=1, source_target_pairs={{0,2},{1,3},{2,0},{3,1},{4,6},{5,7},{6,4},{7,5},{8,10},{9,11},{10,... | collective-permute-start | bytes 2211848 | tf_op jit(solution)/shard_map/ppermute | solution.py:316
  92.7 20.8 %collective-permute-start.20 = (bf16[2,24,3072]{2,1,0:T(8,128)(2,1)S(1)}, bf16[2,24,3072]{2,1,0:T(8,128)(2,1)S(1)}, u32[]{:S(2)}, u32[]{:S(2)}) collective-permute-start(bf16[2,24,3072]{2,1,0:T(8,128)(2,1)S(1)} %copy-done.30), channel_id=1, source_target_pairs={{0,4},{1,5},{2,6},{3,7},{4,0},{5,1},{6,2},{7,3},{8,12},{9,13},{10,... | collective-permute-start | bytes 884744 | tf_op jit(solution)/shard_map/ppermute | solution.py:316
  93.7 19.8 %collective-permute-start.21 = (bf16[2,24,3072]{2,1,0:T(8,128)(2,1)S(1)}, bf16[2,24,3072]{2,1,0:T(8,128)(2,1)S(1)}, u32[]{:S(2)}, u32[]{:S(2)}) collective-permute-start(bf16[2,24,3072]{2,1,0:T(8,128)(2,1)S(1)} %collective-permute-done.13), channel_id=1, source_target_pairs={{0,2},{1,3},{2,0},{3,1},{4,6},{5,7},{6,4},{7,5},{8,10},{9,11},{10,... | collective-permute-start | bytes 884744 | tf_op jit(solution)/shard_map/ppermute | solution.py:316
  118.8 19.3 %collective-permute-start.33 = (bf16[16,24,3072]{2,1,0:T(8,128)(2,1)S(1)}, bf16[16,24,3072]{2,1,0:T(8,128)(2,1)S(1)}, u32[]{:S(2)}, u32[]{:S(2)}) collective-permute-start(bf16[16,24,3072]{2,1,0:T(8,128)(2,1)S(1)} %get-tuple-element.195), channel_id=1, source_target_pairs={{0,1},{1,0},{2,3},{3,2},{4,5},{5,4},{6,7},{7,6},{8,9},{9,8},{10,11... | collective-permute-start | bytes 7077896 | tf_op jit(solution)/shard_map/ppermute | solution.py:316
  119.4 15.8 %collective-permute-start.25 = (bf16[4,24,3072]{2,1,0:T(8,128)(2,1)S(1)}, bf16[4,24,3072]{2,1,0:T(8,128)(2,1)S(1)}, u32[]{:S(2)}, u32[]{:S(2)}) collective-permute-start(bf16[4,24,3072]{2,1,0:T(8,128)(2,1)S(1)} %constant_dynamic-update-slice_fusion.10.rest_1_), channel_id=1, source_target_pairs={{0,4},{1,5},{2,6},{3,7},{4,0},{5,1},{6,2},{7,3},{8,12},{9,13},{10,... | collective-permute-start | bytes 1769480 | tf_op jit(solution)/shard_map/ppermute | solution.py:316
  121.8 15.7 %collective-permute-start.24 = (bf16[4,24,3072]{2,1,0:T(8,128)(2,1)S(1)}, bf16[4,24,3072]{2,1,0:T(8,128)(2,1)S(1)}, u32[]{:S(2)}, u32[]{:S(2)}) collective-permute-start(bf16[4,24,3072]{2,1,0:T(8,128)(2,1)S(1)} %constant_dynamic-update-slice_fusion.8.rest_0_), channel_id=1, source_target_pairs={{0,2},{1,3},{2,0},{3,1},{4,6},{5,7},{6,4},{7,5},{8,10},{9,11},{10,... | collective-permute-start | bytes 1769480 | tf_op jit(solution)/shard_map/ppermute | solution.py:316
  138.9 15.9 %collective-permute-start.35 = (bf16[2,2,24,3072]{3,2,1,0:T(8,128)(2,1)S(1)}, bf16[2,2,24,3072]{3,2,1,0:T(8,128)(2,1)S(1)}, u32[]{:S(2)}, u32[]{:S(2)}) collective-permute-start(bf16[2,2,24,3072]{3,2,1,0:T(8,128)(2,1)S(1)} %get-tuple-element.256), channel_id=1, source_target_pairs={{0,2},{1,3},{2,0},{3,1},{4,6},{5,7},{6,4},{7,5},{8,10},{9,11},{10,... | collective-permute-start | bytes 1769480 | tf_op jit(solution)/shard_map/ppermute | solution.py:316
  140.0 15.0 %collective-permute-start.34 = (bf16[2,2,24,3072]{3,2,1,0:T(8,128)(2,1)S(1)}, bf16[2,2,24,3072]{3,2,1,0:T(8,128)(2,1)S(1)}, u32[]{:S(2)}, u32[]{:S(2)}) collective-permute-start(bf16[2,2,24,3072]{3,2,1,0:T(8,128)(2,1)S(1)} %get-tuple-element.257), channel_id=1, source_target_pairs={{0,4},{1,5},{2,6},{3,7},{4,0},{5,1},{6,2},{7,3},{8,12},{9,13},{10,... | collective-permute-start | bytes 1769480 | tf_op jit(solution)/shard_map/ppermute | solution.py:316
  154.7 18.0 %collective-permute-start.30 = (bf16[16,4,24,768]{3,2,1,0:T(8,128)(2,1)S(1)}, bf16[16,4,24,768]{3,2,1,0:T(8,128)(2,1)S(1)}, u32[]{:S(2)}, u32[]{:S(2)}) collective-permute-start(bf16[16,4,24,768]{3,2,1,0:T(8,128)(2,1)S(1)} %get-tuple-element.190), channel_id=1, source_target_pairs={{0,1},{1,0},{2,3},{3,2},{4,5},{5,4},{6,7},{7,6},{8,9},{9,8},{10,11... | collective-permute-start | bytes 7077896 | tf_op jit(solution)/shard_map/ppermute | solution.py:316
  155.1 17.5 %collective-permute-start.37 = (bf16[2,24,3072]{2,1,0:T(8,128)(2,1)S(1)}, bf16[2,24,3072]{2,1,0:T(8,128)(2,1)S(1)}, u32[]{:S(2)}, u32[]{:S(2)}) collective-permute-start(bf16[2,24,3072]{2,1,0:T(8,128)(2,1)S(1)} %get-tuple-element.260), channel_id=1, source_target_pairs={{0,4},{1,5},{2,6},{3,7},{4,0},{5,1},{6,2},{7,3},{8,12},{9,13},{10,... | collective-permute-start | bytes 884744 | tf_op jit(solution)/shard_map/ppermute | solution.py:316
  173.5 16.0 %collective-permute-start.32 = (bf16[2,2,4,24,768]{4,3,2,1,0:T(8,128)(2,1)S(1)}, bf16[2,2,4,24,768]{4,3,2,1,0:T(8,128)(2,1)S(1)}, u32[]{:S(2)}, u32[]{:S(2)}) collective-permute-start(bf16[2,2,4,24,768]{4,3,2,1,0:T(8,128)(2,1)S(1)} %get-tuple-element.252), channel_id=1, source_target_pairs={{0,2},{1,3},{2,0},{3,1},{4,6},{5,7},{6,4},{7,5},{8,10},{9,11},{10,... | collective-permute-start | bytes 1769480 | tf_op jit(solution)/shard_map/ppermute | solution.py:316
  173.6 16.1 %collective-permute-start.31 = (bf16[2,2,4,24,768]{4,3,2,1,0:T(8,128)(2,1)S(1)}, bf16[2,2,4,24,768]{4,3,2,1,0:T(8,128)(2,1)S(1)}, u32[]{:S(2)}, u32[]{:S(2)}) collective-permute-start(bf16[2,2,4,24,768]{4,3,2,1,0:T(8,128)(2,1)S(1)} %get-tuple-element.253), channel_id=1, source_target_pairs={{0,4},{1,5},{2,6},{3,7},{4,0},{5,1},{6,2},{7,3},{8,12},{9,13},{10,... | collective-permute-start | bytes 1769480 | tf_op jit(solution)/shard_map/ppermute | solution.py:316
  188.1 23.6 %collective-permute-start.41 = (bf16[16,4,24,768]{3,2,1,0:T(8,128)(2,1)S(1)}, bf16[16,4,24,768]{3,2,1,0:T(8,128)(2,1)S(1)}, u32[]{:S(2)}, u32[]{:S(2)}) collective-permute-start(bf16[16,4,24,768]{3,2,1,0:T(8,128)(2,1)S(1)} %get-tuple-element.215), channel_id=1, source_target_pairs={{0,1},{1,0},{2,3},{3,2},{4,5},{5,4},{6,7},{7,6},{8,9},{9,8},{10,11... | collective-permute-start | bytes 7077896 | tf_op jit(solution)/shard_map/ppermute | solution.py:316
  206.9 15.7 %collective-permute-start.54 = (bf16[24,3072]{1,0:T(8,128)(2,1)S(1)}, bf16[24,3072]{1,0:T(8,128)(2,1)S(1)}, u32[]{:S(2)}, u32[]{:S(2)}) collective-permute-start(bf16[24,3072]{1,0:T(8,128)(2,1)S(1)} %get-tuple-element.269), channel_id=1, source_target_pairs={{0,16},{1,17},{2,18},{3,19},{4,20},{5,21},{6,22},{7,23},{8,24},{9,... | collective-permute-start | bytes 442376 | tf_op jit(solution)/shard_map/ppermute | solution.py:316
  207.6 15.0 %collective-permute-start.53 = (bf16[24,3072]{1,0:T(8,128)(2,1)S(1)}, bf16[24,3072]{1,0:T(8,128)(2,1)S(1)}, u32[]{:S(2)}, u32[]{:S(2)}) collective-permute-start(bf16[24,3072]{1,0:T(8,128)(2,1)S(1)} %get-tuple-element.270), channel_id=1, source_target_pairs={{0,8},{1,9},{2,10},{3,11},{4,12},{5,13},{6,14},{7,15},{8,0},{9,1},... | collective-permute-start | bytes 442376 | tf_op jit(solution)/shard_map/ppermute | solution.py:316
  212.5 15.2 %collective-permute-start.43 = (bf16[2,2,4,24,768]{4,3,2,1,0:T(8,128)(2,1)S(1)}, bf16[2,2,4,24,768]{4,3,2,1,0:T(8,128)(2,1)S(1)}, u32[]{:S(2)}, u32[]{:S(2)}) collective-permute-start(bf16[2,2,4,24,768]{4,3,2,1,0:T(8,128)(2,1)S(1)} %get-tuple-element.249), channel_id=1, source_target_pairs={{0,2},{1,3},{2,0},{3,1},{4,6},{5,7},{6,4},{7,5},{8,10},{9,11},{10,... | collective-permute-start | bytes 1769480 | tf_op jit(solution)/shard_map/ppermute | solution.py:316
  213.7 15.5 %collective-permute-start.42 = (bf16[50,8,768]{2,1,0:T(8,128)(2,1)S(1)}, bf16[50,8,768]{2,1,0:T(8,128)(2,1)S(1)}, u32[]{:S(2)}, u32[]{:S(2)}) collective-permute-start(bf16[50,8,768]{2,1,0:T(8,128)(2,1)S(1)} %pad_maximum_fusion), channel_id=1, source_target_pairs={{0,4},{1,5},{2,6},{3,7},{4,0},{5,1},{6,2},{7,3},{8,12},{9,13},{10,... | collective-permute-start | bytes 1843208 | tf_op jit(solution)/shard_map/ppermute | solution.py:316
  222.7 13.9 %collective-permute-start.51 = (bf16[4,24,768]{2,1,0:T(8,128)(2,1)S(1)}, bf16[4,24,768]{2,1,0:T(8,128)(2,1)S(1)}, u32[]{:S(2)}, u32[]{:S(2)}) collective-permute-start(bf16[4,24,768]{2,1,0:T(8,128)(2,1)S(1)} %get-tuple-element.273), channel_id=1, source_target_pairs={{0,16},{1,17},{2,18},{3,19},{4,20},{5,21},{6,22},{7,23},{8,24},{9,... | collective-permute-start | bytes 442376 | tf_op jit(solution)/shard_map/ppermute | solution.py:316
  238.4 13.8 %collective-permute-start.48 = (bf16[14,8,768]{2,1,0:T(8,128)(2,1)S(1)}, bf16[14,8,768]{2,1,0:T(8,128)(2,1)S(1)}, u32[]{:S(2)}, u32[]{:S(2)}) collective-permute-start(bf16[14,8,768]{2,1,0:T(8,128)(2,1)S(1)} %get-tuple-element.283), channel_id=1, source_target_pairs={{0,16},{1,17},{2,18},{3,19},{4,20},{5,21},{6,22},{7,23},{8,24},{9,... | collective-permute-start | bytes 516104 | tf_op jit(solution)/shard_map/ppermute | solution.py:316
  (65 other events, 625.9 us)

commit v4 on v3

--- a/solution.py
+++ b/solution.py
@@ -406,11 +406,11 @@
     keep_b = plus(own[1, 0], arrived[1, 0])
     if extra is not None:
         send_a = join(send_a, extra.astype(BF16))
-    return keep_a, keep_b, grid.shift(send_a, kx=1), grid.shift(send_b, ky=1), extra
+    return keep_a, keep_b, grid.shift(send_a, kx=1), grid.shift(send_b, ky=1), extra, (send_a, send_b)
 
 
 def scatter_second(grid, state, gate):
-    keep_a, keep_b, got_a, got_b, extra = state
+    keep_a, keep_b, got_a, got_b, extra, _ = state
     got_a, got_b = tie((got_a, got_b), gate)
     if extra is not None:
         got_a, more = part(got_a, keep_a.shape)
@@ -421,11 +421,11 @@
     rest_b = plus(keep_b[0], got_b[0])
     if extra is not None:
         next_a = join(next_a, extra.astype(BF16))
-    return rest_a, rest_b, grid.shift(next_a, ky=1), grid.shift(next_b, kx=1), extra
+    return rest_a, rest_b, grid.shift(next_a, ky=1), grid.shift(next_b, kx=1), extra, (next_a, next_b)
 
 
 def scatter_third(grid, state, gate):
-    rest_a, rest_b, last_a, last_b, extra = state
+    rest_a, rest_b, last_a, last_b, extra, _ = state
     last_a, last_b = tie((last_a, last_b), gate)
     if extra is not None:
         last_a, more = part(last_a, rest_a.shape)
@@ -435,11 +435,11 @@
     sends = parts[1:]
     if extra is not None:
         sends = [join(send, extra.astype(BF16)) for send in sends]
-    return parts[0], [grid.shift(send, kz=k) for send, k in zip(sends, COLUMN[1:])], extra
+    return parts[0], [grid.shift(send, kz=k) for send, k in zip(sends, COLUMN[1:])], extra, sends
 
 
 def scatter_last(state, gate):
-    total, came, extra = state
+    total, came, extra, _ = state
     shape = total.shape
     came = tie(came, gate)
     total = total.astype(F32)
@@ -634,7 +634,9 @@
     lax.fori_loop(0, moved_ref.shape[0] // rows, block, 0)
 
 
-def down_grad_kernel(grid, length, size_at, lengths_ref, place_ref, cot_ref, active_ref, low_ref, vec_ref, own_ref, other_ref, total):
+def down_grad_kernel(grid, length, size_at, lengths_ref, place_ref, cot_ref, active_ref, low_ref, vec_ref, own_ref, other_ref, far_ref, total, sem):
+    keep = pltpu.make_async_copy(active_ref, far_ref, sem)
+    keep.start()
     width = cot_ref.shape[1]
     captions = cot_ref.shape[0] // length
     tiles = length // TILE
@@ -667,13 +669,16 @@
         return carry
 
     lax.fori_loop(0, active_ref.shape[1] // width, column, 0)
+    keep.wait()
 
 
 def upper_grad_kernel(grid, places, size_at, place_ref, low_ref, slope_ref, normed_ref, *rest):
     count = len(places)
     refs, rest = rest[:count], rest[count:]
-    upper_ref, vec_ref, own_ref, other_ref, held, total = rest
+    upper_ref, vec_ref, own_ref, other_ref, far_ref, held, total, sem = rest
     place(grid, places, refs, held)
+    keep = pltpu.make_async_copy(held, far_ref, sem)
+    keep.start()
     width = low_ref.shape[1]
     per = grid.count // 4
     share = width // per
@@ -710,6 +715,7 @@
         return carry
 
     lax.fori_loop(0, upper_ref.shape[1] // width, column, 0)
+    keep.wait()
 
 
 def middle_grad_kernel(grid, size_at, place_ref, upper_ref, middle_ref, low_ref, vec_in, held, grad_ref, branch_ref, dm_ref, vec_ref):
@@ -883,6 +889,7 @@
 
 
 FAST = pl.BlockSpec(memory_space=pltpu.VMEM)
+FAR = pl.BlockSpec(memory_space=pltpu.HBM)
 
 
 def call(kernel, steps, in_specs, out_specs, outs, scratch, flops, moved, name, limit=8):
@@ -899,11 +906,11 @@
     )
 
 
-def call_near(kernel, in_specs, outs, scratch, flops, name, limit=8, aliases=None):
+def call_near(kernel, in_specs, outs, scratch, flops, name, limit=8, aliases=None, far=0):
     return pl.pallas_call(
         kernel,
         in_specs=in_specs,
-        out_specs=[FAST] * len(outs),
+        out_specs=[FAST] * (len(outs) - far) + [FAR] * far,
         input_output_aliases=aliases or {},
         out_shape=[jax.ShapeDtypeStruct(s, d) for s, d in outs],
         scratch_shapes=scratch,
@@ -961,20 +968,18 @@
     size_at = captions * (length // TILE) + captions
     places = gather_places()
     first_a = jnp.stack([first, grid.shift(first, kz=3)])
-    first_a, second = together((first_a, second))
     first_z = grid.shift(first_a, kz=1)
+    first_a, first_z, second = together((first_a, first_z, second))
+    first_a = gather_one(grid, first_a, first_z)
     second_a = jnp.stack([second, grid.shift(second, kz=3)])
-    first_a, first_z, second_a = together((first_a, first_z, second_a))
-    first_a = gather_one(grid, first_a, first_z)
-    second_z = grid.shift(second_a, kz=1)
-    first_a, second_z, third = together((first_a, second_z, third))
+    first_a, second_a, where = together((first_a, second_a, where))
     first_b = gather_two(grid, first_a)
     first_c = gather_core(grid, first_b[:2])
+    second_z = grid.shift(second_a, kz=1)
+    first_b, first_c, second_z, third = together((first_b, first_c, second_z, third))
+    first_in = first_b + first_c + gather_core(grid, first_b[2:])
+    second_a = gather_one(grid, second_a, second_z)
     third_a = jnp.stack([third, grid.shift(third, kz=3)])
-    first_b, first_c, third_a = together((first_b, first_c, third_a))
-    first_in = first_b + first_c + gather_core(grid, first_b[2:])
-    second_a = gather_one(grid, second_a, tie(second_z, first_b))
-    third_z = grid.shift(third_a, kz=1)
     half = grid.count // 2
     unit = 2 * tokens * width * width
     row = (tokens, width)
@@ -989,7 +994,8 @@
         5 * unit,
         "project",
     )(where, hidden2, *first_in)
-    second_a, third_z, query = together((second_a, third_z, query))
+    second_a, third_a, query = together((second_a, third_a, query))
+    third_z = grid.shift(third_a, kz=1)
     second_b = gather_two(grid, second_a)
     second_c = gather_core(grid, second_b[:2])
     probs, mixed = call_near(
@@ -1014,32 +1020,36 @@
     third_a, active = together((third_a, active))
     third_b = gather_two(grid, third_a)
     third_c = gather_core(grid, third_b[:2])
-    low, down_vec, down_own, down_other = call_near(
+    low, down_vec, down_own, down_other, active = call_near(
         functools.partial(down_grad_kernel, grid, length, size_at),
         [SMEM] * 2 + [FAST] * 2,
-        [(row, BF16), ((8, width), F32)] + [((half, share, ff), BF16)] * 2,
-        [square],
+        [(row, BF16), ((8, width), F32)] + [((half, share, ff), BF16)] * 2 + [((tokens, ff), BF16)],
+        [square, pltpu.SemaphoreType.DMA],
         5 * unit,
         "down_grad",
+        far=1,
     )(lengths, where, cot2, active)
-    third_b, third_c, down_own = together((third_b, third_c, down_own))
+    third_b, third_c, down_own, down_other = together((third_b, third_c, down_own, down_other))
     third_in = third_b + third_c + gather_core(grid, third_b[2:])
     down_two = scatter_first(grid, down_own, scatter_core(grid, down_other))
-    low = tie(low, down_two[0])
+    low = tie(low, down_two[-1])
     grad_upper, up_vec, up_own, up_other, lower_w = call_near(
         functools.partial(upper_grad_kernel, grid, places, size_at),
         [SMEM] + [FAST] * (3 + len(third_in)),
         [((tokens, ff), BF16), ((32, width), F32)]
         + [((half, 4, share, width), BF16)] * 2
         + [((grid.count, share, ff), BF16)],
-        [square],
+        [pltpu.VMEM((grid.count, share, ff), BF16), square, pltpu.SemaphoreType.DMA],
         8 * unit,
         "upper_grad",
+        limit=12,
         aliases={2: 0},
+        far=1,
     )(where, low, slope, normed2, *third_in)
+    down_two, up_vec, up_own, up_other = together((down_two, up_vec, up_own, up_other))
     down_three = scatter_second(grid, down_two, up_vec)
     up_one = scatter_core(grid, up_other)
-    grad_upper = tie(grad_upper, down_three[0])
+    grad_upper = tie(grad_upper, down_three[-1])
     grad_middle, branch, dm, mid_vec = call_near(
         functools.partial(middle_grad_kernel, grid, size_at),
         [SMEM] + [FAST] * 5,
@@ -1050,7 +1060,7 @@
     )(where, grad_upper, middle, low, vec, held_two)
     down_four = scatter_third(grid, down_three, mid_vec)
     up_two = scatter_first(grid, up_own, tie(up_one, mid_vec))
-    dm = tie(dm, (up_two[0], down_four[0]))
+    dm = tie(dm, (up_two[-1], down_four[-1]))
     grads, att_vec = call_near(
         functools.partial(attend_grad_kernel, length, 4),
         [SMEM] * 2 + [FAST] * 5,
@@ -1059,8 +1069,15 @@
         7 * unit,
         "attend_grad",
     )(lengths, where, dm, query, keys, values, probs)
-    up_three = scatter_second(grid, up_two, att_vec)
-    grads = tie(grads, up_three[0])
+    input_grad, all_vec = call_near(
+        functools.partial(input_grad_kernel, grid, size_at),
+        [SMEM] + [FAST] * 9,
+        [(row, F32), ((16, width), F32)],
+        [pltpu.VMEM(row, F32)],
+        5 * unit,
+        "input_grad",
+    )(where, moved, grad_middle, grads, vec, down_vec, up_vec, mid_vec, att_vec, held_one)
+    grads, all_vec = together((grads, all_vec))
     att_own, att_other = call_near(
         functools.partial(weight_grad_kernel, grid, size_at),
         [SMEM] + [FAST] * 4,
@@ -1069,23 +1086,15 @@
         5 * unit,
         "weight_grad",
     )(where, grads, branch, normed, mixed)
-    att_gate = att_own[0, 0, 0:8, 0:128]
-    up_four = scatter_third(grid, up_three, att_gate)
+    down_four, up_two, att_own, att_other, all_vec = together((down_four, up_two, att_own, att_other, all_vec))
+    down_sum = scatter_last(down_four, all_vec)
+    up_three = scatter_second(grid, up_two, all_vec)
     att_one = scatter_core(grid, att_other)
-    grad_middle = tie(grad_middle, up_four[0])
-    input_grad, all_vec = call_near(
-        functools.partial(input_grad_kernel, grid, size_at),
-        [SMEM] + [FAST] * 9,
-        [(row, F32), ((16, width), F32)],
-        [pltpu.VMEM(row, F32)],
-        5 * unit,
-        "input_grad",
-    )(where, moved, grad_middle, grads, vec, down_vec, up_vec, mid_vec, att_vec, held_one)
-    down_sum = scatter_last(down_four, all_vec)
-    up_sum = scatter_last(up_four, all_vec)
     all_vec = (all_vec + grid.shift(all_vec, kc=1)).reshape(2, 8, width)
-    att_two = scatter_first(grid, att_own, tie(att_one, all_vec), all_vec)
-    middle = tie(middle, att_two[0])
+    att_one = tie(att_one, up_three[-1])
+    att_two = scatter_first(grid, att_own, att_one, all_vec)
+    up_four = scatter_third(grid, up_three, att_two[-1])
+    middle = tie(middle, (att_two[-1], up_four[-1]))
     steps = 4
     rows = tokens // steps
     block = pl.BlockSpec((rows, width), lambda i: (i, 0))
@@ -1103,6 +1112,7 @@
     )(where, active, middle, vec, lower_w)
     out_gate = block_out[0:8, 0:128]
     att_three = scatter_second(grid, att_two, out_gate)
+    up_sum = scatter_last(up_four, att_three[-1])
     att_four = scatter_third(grid, att_three, out_gate)
     att_sum, all_vec = scatter_last(att_four, out_gate)
     all_vec = all_vec.reshape(16, width)

time: 257 us -> 239 us (0.930)
  local copies, waits for them, and re-layouts: 23.2 us -> 12.9 us
  waiting for transfers between devices: 82.8 us -> 74.4 us
    unnamed x74 -> x56, local copies, waits for them, and re-layouts: 20.9 us -> 10.5 us
    ppermute x55, waiting for transfers between devices: 82.8 us -> 74.4 us  [shift(): return lax.ppermute(values, AXES, pairs)]
  transfers between devices with their start and end apart: 55 -> 55, of which waited for: 27 -> 24; matrix products, arithmetic and copies ran while one was open for 4% -> 5% of each run, Pallas kernels for 26% -> 30%
where the time goes in v4:
time: 239 us; the launch traced here: 236 us
  waiting for transfers between devices  74.4 us (31%)
  Pallas kernels  72.3 us (30%)
  starting transfers between devices  62.3 us (26%)
  local copies, waits for them, and re-layouts  12.9 us (5%)
  other arithmetic  11.9 us (5%)
    ppermute x55, waiting for transfers between devices, shift(): return lax.ppermute(values, AXES, pairs)  74.4 us
    ppermute x55, starting transfers between devices, shift(): return lax.ppermute(values, AXES, pairs)  62.3 us
    pallas_call x1, Pallas kernels, fast_device(): call_near(functools.partial(upper_kernel, grid, places), [FAST] * (3 + le...  12.9 us
    unnamed x56, local copies, waits for them, and re-layouts  10.5 us
    pallas_call x1, Pallas kernels, fast_device(): call_near(functools.partial(upper_grad_kernel, grid, places, size_at), [S...  9.33 us
    pallas_call x1, Pallas kernels, fast_device(): call(lower_kernel, steps, [SMEM, pl.BlockSpec((rows, ff), lambda i: (i, 0...  7.5 us
    pallas_call x1, Pallas kernels, fast_device(): call_near(functools.partial(attend_grad_kernel, length, 4), [SMEM] * 2 +...  7.11 us
    pallas_call x1, Pallas kernels, fast_device(): call_near(functools.partial(middle_grad_kernel, grid, size_at), [SMEM] +...  6.83 us
  transfers between devices with their start and end apart: 55, of which 24 were waited for; matrix products, arithmetic and copies ran while one was open for 5% of the time, Pallas kernels for 30%

profile of v4, /device:TPU:0, one launch (start us, length us, event | category | flops | bytes accessed | tf_op | source)
XLA Modules:
  0.0 236.0 jit_solution(12628976062623139463)
XLA Ops:
  4.5 5.1 %collective-permute-start = (bf16[4,24,768]{2,1,0:T(8,128)(2,1)S(1)}, bf16[4,24,768]{2,1,0:T(8,128)(2,1)S(1)}, u32[]{:S(2)}, u32[]{:S(2)}) collective-permute-start(bf16[4,24,768]{2,1,0:T(8,128)(2,1)S(1)} %pack.1), channel_id=1, source_target_pairs={{0,24},{1,25},{2,26},{3,27},{4,28},{5,29},{6,30},{7,31},{8,16},{9,... | collective-permute-start | bytes 442376 | tf_op jit(solution)/shard_map/ppermute | solution.py:316
  17.4 5.4 %collective-permute-done.1 = bf16[2,4,24,768]{3,2,1,0:T(8,128)(2,1)S(1)} collective-permute-done((bf16[2,4,24,768]{3,2,1,0:T(8,128)(2,1)S(1)}, bf16[2,4,24,768]{3,2,1,0:T(8,128)(2,1)S(1)}, u32[]{:S(2)}, u32[]{:S(2)}) %collective-permute-start.1) | collective-permute-done | bytes 294944 | tf_op jit(solution)/shard_map/ppermute | solution.py:316
  36.8 9.8 %collective-permute-done.9 = bf16[2,5,24,768]{3,2,1,0:T(8,128)(2,1)S(1)} collective-permute-done((bf16[2,5,24,768]{3,2,1,0:T(8,128)(2,1)S(1)}, bf16[2,5,24,768]{3,2,1,0:T(8,128)(2,1)S(1)}, u32[]{:S(2)}, u32[]{:S(2)}) %collective-permute-start.9) | collective-permute-done | bytes 368672 | tf_op jit(solution)/shard_map/ppermute | solution.py:316
  46.6 3.2 %collective-permute-done.5.rest_2_ = bf16[4,4,24,768]{3,2,1,0:T(8,128)(2,1)S(1)} collective-permute-done((bf16[4,4,24,768]{3,2,1,0:T(8,128)(2,1)S(1)}, bf16[4,4,24,768]{3,2,1,0:T(8,128)(2,1)S(1)}, u32[]{:S(2)}, u32[]{:S(2)}) %collective-permute-start.5) | collective-permute-done | bytes 589856 | tf_op jit(solution)/shard_map/ppermute | solution.py:316
  55.0 3.0 %collective-permute-done.12 = bf16[24,3072]{1,0:T(8,128)(2,1)S(1)} collective-permute-done((bf16[24,3072]{1,0:T(8,128)(2,1)S(1)}, bf16[24,3072]{1,0:T(8,128)(2,1)S(1)}, u32[]{:S(2)}, u32[]{:S(2)}) %collective-permute-start.12) | collective-permute-done | bytes 147488 | tf_op jit(solution)/shard_map/ppermute | solution.py:316
  58.1 6.5 %project.1 = (bf16[1024,768]{1,0:T(8,128)(2,1)S(1)}, bf16[1024,768]{1,0:T(8,128)(2,1)S(1)}, bf16[1024,768]{1,0:T(8,128)(2,1)S(1)}, bf16[1024,768]{1,0:T(8,128)(2...) custom-call(s32[82]{0:T(128)S(1)} %pad_add_fusion.place_ref, ...), custom_call_target="tpu_custom_call" | custom-call | flops 6039797760 | bytes 1000000 | tf_op jit(solution)/shard_map/project/pallas_call | solution.py:989
  69.5 4.8 %attend.1 = (bf16[48,64,256]{2,1,0:T(8,128)(2,1)S(1)}, bf16[1024,768]{1,0:T(8,128)(2,1)S(1)}) custom-call(s32[16]{0:T(128)S(1)} %copy-done.3, s32[82]{0:T(128)S(1)} %pad_add_fusion.place_ref, bf16[1024,768]{1,0:T(8,128)(2,1)S(1)} %get-tuple-element.174.q_ref, bf16[1024,768]{1,0:T(8,128)(2,1)S(1)} %get-tuple-element.175.k_ref, ...), custom_call_target="tpu_custom_call" | custom-call | flops 6039797760 | bytes 1000000 | tf_op jit(solution)/shard_map/attend/pallas_call | solution.py:1001
  77.4 4.9 %collective-permute-done.16.rest_3_ = bf16[4,5,24,768]{3,2,1,0:T(8,128)(2,1)S(1)} collective-permute-done((bf16[4,5,24,768]{3,2,1,0:T(8,128)(2,1)S(1)}, bf16[4,5,24,768]{3,2,1,0:T(8,128)(2,1)S(1)}, u32[]{:S(2)}, u32[]{:S(2)}) %collective-permute-start.16) | collective-permute-done | bytes 737312 | tf_op jit(solution)/shard_map/ppermute | solution.py:316
  82.3 3.0 %collective-permute-done.15.rest_2_ = bf16[4,5,24,768]{3,2,1,0:T(8,128)(2,1)S(1)} collective-permute-done((bf16[4,5,24,768]{3,2,1,0:T(8,128)(2,1)S(1)}, bf16[4,5,24,768]{3,2,1,0:T(8,128)(2,1)S(1)}, u32[]{:S(2)}, u32[]{:S(2)}) %collective-permute-start.15) | collective-permute-done | bytes 737312 | tf_op jit(solution)/shard_map/ppermute | solution.py:316
  88.6 12.9 %upper.1 = (f32[1024,768]{1,0:T(8,128)S(1)}, bf16[1024,768]{1,0:T(8,128)(2,1)S(1)}, bf16[1024,3072]{1,0:T(8,128)(2,1)S(1)}, bf16[1024,3072]{1,0:T(8,128)(2,1)S(1)}, bf16[32,5,24,768]{3,2,1,0:T(8,128)(2,1)S(1)}) custom-call(bf16[1024,768]{1,0:T(8,128)(2,1)S(1)} %get-tuple-element.179.moved_ref, bf16[1024,768]{1,0:T(8,128)(2,1)S(1)} %get-tuple-element.180.mixed_ref, ...), custom_call_target="tpu_custom_call" | custom-call | flops 10871635968 | bytes 1000000 | tf_op jit(solution)/shard_map/upper/pallas_call | solution.py:1012
  106.6 5.6 %down_grad.1 = (bf16[1024,768]{1,0:T(8,128)(2,1)S(1)}, f32[8,768]{1,0:T(8,128)S(1)}, bf16[16,24,3072]{2,1,0:T(8,128)(2,1)S(1)}, bf16[16,24,3072]{2,1,0:T(8,128)(2,1)S(1)}, bf16[1024,3072]{1,0:T(8,128)(2,1)S(1)}) custom-call(s32[16]{0:T(128)S(1)} %copy-done.3, s32[82]{0:T(128)S(1)} %pad_add_fusion.place_ref, bf16[1024,768]{1,0:T(8,128)(2,1)S(1)} %bitcast.225, ...), custom_call_target="tpu_custom_call" | custom-call | flops 6039797760 | bytes 1000000 | tf_op jit(solution)/shard_map/down_grad/pallas_call | solution.py:1023
  112.2 7.4 %collective-permute-done.25.rest_3_ = bf16[4,24,3072]{2,1,0:T(8,128)(2,1)S(1)} collective-permute-done((bf16[4,24,3072]{2,1,0:T(8,128)(2,1)S(1)}, bf16[4,24,3072]{2,1,0:T(8,128)(2,1)S(1)}, u32[]{:S(2)}, u32[]{:S(2)}) %collective-permute-start.25) | collective-permute-done | bytes 589856 | tf_op jit(solution)/shard_map/ppermute | solution.py:316
  121.4 4.0 %collective-permute-done.28 = bf16[16,24,3072]{2,1,0:T(8,128)(2,1)S(1)} collective-permute-done((bf16[16,24,3072]{2,1,0:T(8,128)(2,1)S(1)}, bf16[16,24,3072]{2,1,0:T(8,128)(2,1)S(1)}, u32[]{:S(2)}, u32[]{:S(2)}) %collective-permute-start.28) | collective-permute-done | bytes 2359328 | tf_op jit(solution)/shard_map/ppermute | solution.py:316
  129.1 9.3 %upper_grad.1 = (bf16[1024,3072]{1,0:T(8,128)(2,1)S(1)}, f32[32,768]{1,0:T(8,128)S(1)}, bf16[16,4,24,768]{3,2,1,0:T(8,128)(2,1)S(1)}, bf16[16,4,24,768]{3,2,1,0:T(8,128)(2,1)S(1)}, bf16[32,24,3072]{2,1,0:T(8,128)(2,1)S(1)}) custom-call(s32[82]{0:T(128)S(1)} %pad_add_fusion.place_ref, ...), custom_call_target="tpu_custom_call", output_to_operand_aliasing={{0}: (2, {})} | custom-call | flops 9663676416 | bytes 1000000 | tf_op jit(solution)/shard_map/upper_grad/pallas_call | solution.py:1036
  138.4 3.3 %collective-permute-done.29 = bf16[2,2,24,3072]{3,2,1,0:T(8,128)(2,1)S(1)} collective-permute-done((bf16[2,2,24,3072]{3,2,1,0:T(8,128)(2,1)S(1)}, bf16[2,2,24,3072]{3,2,1,0:T(8,128)(2,1)S(1)}, u32[]{:S(2)}, u32[]{:S(2)}) %collective-permute-start.29) | collective-permute-done | bytes 589856 | tf_op jit(solution)/shard_map/ppermute | solution.py:316
  147.8 6.8 %middle_grad.1 = (f32[1024,768]{1,0:T(8,128)S(1)}, bf16[1024,768]{1,0:T(8,128)(2,1)S(1)}, bf16[1088,768]{1,0:T(8,128)(2,1)S(1)}, f32[8,768]{1,0:T(8,128)S(1)}) custom-call(s32[82]{0:T(128)S(1)} %pad_add_fusion.place_ref, bf16[1024,3072]{1,0:T(8,128)(2,1)S(1)} %get-tuple-element.221.upper_ref, f32[1024,768]{1,0:T(8,128)S(1)} %get-tuple-element.256.middle_ref, ...), custom_call_target="tpu_custom_call" | custom-call | flops 7247757312 | bytes 1000000 | tf_op jit(solution)/shard_map/middle_grad/pallas_call | solution.py:1053
  164.2 7.1 %attend_grad.1 = (bf16[3,1280,768]{2,1,0:T(8,128)(2,1)S(1)}, f32[8,768]{1,0:T(8,128)S(1)}) custom-call(s32[16]{0:T(128)S(1)} %copy-done.3, s32[82]{0:T(128)S(1)} %pad_add_fusion.place_ref, bf16[1088,768]{1,0:T(8,128)(2,1)S(1)} %get-tuple-element.230.dm_ref, bf16[1024,768]{1,0:T(8,128)(2,1)S(1)} %copy-done.17, bf16[1024,768]{1,0:T(8,128)(2,1)S(1)} %copy-done.19, ...), custom_call_target="tpu_custom_call" | custom-call | flops 8455716864 | bytes 1000000 | tf_op jit(solution)/shard_map/attend_grad/pallas_call | solution.py:1064
  171.4 6.2 %input_grad.1 = (f32[1024,768]{1,0:T(8,128)}, f32[16,768]{1,0:T(8,128)S(1)}) custom-call(s32[82]{0:T(128)S(1)} %pad_add_fusion.place_ref, bf16[1024,768]{1,0:T(8,128)(2,1)S(1)} %get-tuple-element.179.moved_ref, f32[1024,768]{1,0:T(8,128)S(1)} %copy-done.11, bf16[3,1280,768]{2,1,0:T(8,128)(2,1)S(1)} %get-tuple-element.238.grads_ref, ...), custom_call_target="tpu_custom_call" | custom-call | flops 6039797760 | bytes 1000000 | tf_op jit(solution)/shard_map/input_grad/pallas_call | solution.py:1072
  177.6 4.7 %weight_grad.1 = (bf16[16,4,24,768]{3,2,1,0:T(8,128)(2,1)S(1)}, bf16[16,4,24,768]{3,2,1,0:T(8,128)(2,1)S(1)}) custom-call(s32[82]{0:T(128)S(1)} %pad_add_fusion.place_ref, bf16[3,1280,768]{2,1,0:T(8,128)(2,1)S(1)} %get-tuple-element.238.grads_ref, bf16[1024,768]{1,0:T(8,128)(2,1)S(1)} %get-tuple-element.239.branch_ref, bf16[1024,768]{1,0:T(8,128)(2,1)S(1)} %copy-done.13, ...), custom_call_target="tpu_custom_call" | custom-call | flops 6039797760 | bytes 1000000 | tf_op jit(solution)/shard_map/weight_grad/pallas_call | solution.py:1081
  195.4 3.1 %collective-permute-start.53 = (bf16[4,24,768]{2,1,0:T(8,128)(2,1)S(1)}, bf16[4,24,768]{2,1,0:T(8,128)(2,1)S(1)}, u32[]{:S(2)}, u32[]{:S(2)}) collective-permute-start(bf16[4,24,768]{2,1,0:T(8,128)(2,1)S(1)} %get-tuple-element.316), channel_id=1, source_target_pairs={{0,8},{1,9},{2,10},{3,11},{4,12},{5,13},{6,14},{7,15},{8,0},{9,1},... | collective-permute-start | bytes 442376 | tf_op jit(solution)/shard_map/ppermute | solution.py:316
  201.0 7.5 %lower.1 = bf16[1024,768]{1,0:T(8,128)(2,1)} custom-call(s32[82]{0:T(128)S(1)} %pad_add_fusion.place_ref, bf16[1024,3072]{1,0:T(8,128)(2,1)S(1)} %get-tuple-element.190.active_ref, f32[1024,768]{1,0:T(8,128)S(1)} %get-tuple-element.256.middle_ref, f32[24,768]{1,0:T(8,128)S(1)} %get-tuple-element.181.vec_ref.vec_in, ...), custom_call_target="tpu_custom_call" | custom-call | flops 4831838208 | bytes 20000000 | tf_op jit(solution)/shard_map/lower/pallas_call | solution.py:1101
  212.0 3.6 %collective-permute-done.48 = bf16[2,4,24,768]{3,2,1,0:T(8,128)(2,1)S(1)} collective-permute-done((bf16[2,4,24,768]{3,2,1,0:T(8,128)(2,1)S(1)}, bf16[2,4,24,768]{3,2,1,0:T(8,128)(2,1)S(1)}, u32[]{:S(2)}, u32[]{:S(2)}) %collective-permute-start.48) | collective-permute-done | bytes 294944 | tf_op jit(solution)/shard_map/ppermute | solution.py:316
  222.7 4.0 %collective-permute-done.49 = bf16[14,8,768]{2,1,0:T(8,128)(2,1)S(1)} collective-permute-done((bf16[14,8,768]{2,1,0:T(8,128)(2,1)S(1)}, bf16[14,8,768]{2,1,0:T(8,128)(2,1)S(1)}, u32[]{:S(2)}, u32[]{:S(2)}) %collective-permute-start.49) | collective-permute-done | bytes 172064 | tf_op jit(solution)/shard_map/ppermute | solution.py:316
  227.1 7.1 %collective-permute-done.51 = bf16[14,8,768]{2,1,0:T(8,128)(2,1)S(1)} collective-permute-done((bf16[14,8,768]{2,1,0:T(8,128)(2,1)S(1)}, bf16[14,8,768]{2,1,0:T(8,128)(2,1)S(1)}, u32[]{:S(2)}, u32[]{:S(2)}) %collective-permute-start.51) | collective-permute-done | bytes 172064 | tf_op jit(solution)/shard_map/ppermute | solution.py:316
  (216 shorter events, 95.2 us)
Async XLA Ops:
  34.0 15.8 %collective-permute-start.5 = (bf16[4,4,24,768]{3,2,1,0:T(8,128)(2,1)S(1)}, bf16[4,4,24,768]{3,2,1,0:T(8,128)(2,1)S(1)}, u32[]{:S(2)}, u32[]{:S(2)}) collective-permute-start(bf16[4,4,24,768]{3,2,1,0:T(8,128)(2,1)S(1)} %constant_dynamic-update-slice_fusion.rest_0_), channel_id=1, source_target_pairs={{0,2},{1,3},{2,0},{3,1},{4,6},{5,7},{6,4},{7,5},{8,10},{9,11},{10,... | collective-permute-start | bytes 1769480 | tf_op jit(solution)/shard_map/ppermute | solution.py:316
  35.6 14.2 %collective-permute-start.7 = (bf16[4,4,24,768]{3,2,1,0:T(8,128)(2,1)S(1)}, bf16[4,4,24,768]{3,2,1,0:T(8,128)(2,1)S(1)}, u32[]{:S(2)}, u32[]{:S(2)}) collective-permute-start(bf16[4,4,24,768]{3,2,1,0:T(8,128)(2,1)S(1)} %constant_dynamic-update-slice_fusion.rest_0_), channel_id=1, source_target_pairs={{0,1},{1,0},{2,3},{3,2},{4,5},{5,4},{6,7},{7,6},{8,9},{9,8},{10,11... | collective-permute-start | bytes 1769480 | tf_op jit(solution)/shard_map/ppermute | solution.py:316
  64.8 17.6 %collective-permute-start.16 = (bf16[4,5,24,768]{3,2,1,0:T(8,128)(2,1)S(1)}, bf16[4,5,24,768]{3,2,1,0:T(8,128)(2,1)S(1)}, u32[]{:S(2)}, u32[]{:S(2)}) collective-permute-start(bf16[4,5,24,768]{3,2,1,0:T(8,128)(2,1)S(1)} %constant_dynamic-update-slice_fusion.6.rest_1_), channel_id=1, source_target_pairs={{0,4},{1,5},{2,6},{3,7},{4,0},{5,1},{6,2},{7,3},{8,12},{9,13},{10,... | collective-permute-start | bytes 2211848 | tf_op jit(solution)/shard_map/ppermute | solution.py:316
  66.3 16.0 %collective-permute-start.18 = (bf16[4,5,24,768]{3,2,1,0:T(8,128)(2,1)S(1)}, bf16[4,5,24,768]{3,2,1,0:T(8,128)(2,1)S(1)}, u32[]{:S(2)}, u32[]{:S(2)}) collective-permute-start(bf16[4,5,24,768]{3,2,1,0:T(8,128)(2,1)S(1)} %constant_dynamic-update-slice_fusion.6.rest_1_), channel_id=1, source_target_pairs={{0,1},{1,0},{2,3},{3,2},{4,5},{5,4},{6,7},{7,6},{8,9},{9,8},{10,11... | collective-permute-start | bytes 2211848 | tf_op jit(solution)/shard_map/ppermute | solution.py:316
  66.4 19.0 %collective-permute-start.15 = (bf16[4,5,24,768]{3,2,1,0:T(8,128)(2,1)S(1)}, bf16[4,5,24,768]{3,2,1,0:T(8,128)(2,1)S(1)}, u32[]{:S(2)}, u32[]{:S(2)}) collective-permute-start(bf16[4,5,24,768]{3,2,1,0:T(8,128)(2,1)S(1)} %constant_dynamic-update-slice_fusion.4.rest_0_), channel_id=1, source_target_pairs={{0,2},{1,3},{2,0},{3,1},{4,6},{5,7},{6,4},{7,5},{8,10},{9,11},{10,... | collective-permute-start | bytes 2211848 | tf_op jit(solution)/shard_map/ppermute | solution.py:316
  68.0 17.4 %collective-permute-start.17 = (bf16[4,5,24,768]{3,2,1,0:T(8,128)(2,1)S(1)}, bf16[4,5,24,768]{3,2,1,0:T(8,128)(2,1)S(1)}, u32[]{:S(2)}, u32[]{:S(2)}) collective-permute-start(bf16[4,5,24,768]{3,2,1,0:T(8,128)(2,1)S(1)} %constant_dynamic-update-slice_fusion.4.rest_0_), channel_id=1, source_target_pairs={{0,1},{1,0},{2,3},{3,2},{4,5},{5,4},{6,7},{7,6},{8,9},{9,8},{10,11... | collective-permute-start | bytes 2211848 | tf_op jit(solution)/shard_map/ppermute | solution.py:316
  85.9 18.2 %collective-permute-start.20 = (bf16[2,24,3072]{2,1,0:T(8,128)(2,1)S(1)}, bf16[2,24,3072]{2,1,0:T(8,128)(2,1)S(1)}, u32[]{:S(2)}, u32[]{:S(2)}) collective-permute-start(bf16[2,24,3072]{2,1,0:T(8,128)(2,1)S(1)} %pad_maximum_fusion.4), channel_id=1, source_target_pairs={{0,4},{1,5},{2,6},{3,7},{4,0},{5,1},{6,2},{7,3},{8,12},{9,13},{10,... | collective-permute-start | bytes 884744 | tf_op jit(solution)/shard_map/ppermute | solution.py:316
  86.4 17.7 %collective-permute-start.21 = (bf16[2,24,3072]{2,1,0:T(8,128)(2,1)S(1)}, bf16[2,24,3072]{2,1,0:T(8,128)(2,1)S(1)}, u32[]{:S(2)}, u32[]{:S(2)}) collective-permute-start(bf16[2,24,3072]{2,1,0:T(8,128)(2,1)S(1)} %collective-permute-done.19), channel_id=1, source_target_pairs={{0,2},{1,3},{2,0},{3,1},{4,6},{5,7},{6,4},{7,5},{8,10},{9,11},{10,... | collective-permute-start | bytes 884744 | tf_op jit(solution)/shard_map/ppermute | solution.py:316
  104.2 15.4 %collective-permute-start.25 = (bf16[4,24,3072]{2,1,0:T(8,128)(2,1)S(1)}, bf16[4,24,3072]{2,1,0:T(8,128)(2,1)S(1)}, u32[]{:S(2)}, u32[]{:S(2)}) collective-permute-start(bf16[4,24,3072]{2,1,0:T(8,128)(2,1)S(1)} %constant_dynamic-update-slice_fusion.10.rest_1_), channel_id=1, source_target_pairs={{0,4},{1,5},{2,6},{3,7},{4,0},{5,1},{6,2},{7,3},{8,12},{9,13},{10,... | collective-permute-start | bytes 1769480 | tf_op jit(solution)/shard_map/ppermute | solution.py:316
  105.0 14.6 %collective-permute-start.27 = (bf16[4,24,3072]{2,1,0:T(8,128)(2,1)S(1)}, bf16[4,24,3072]{2,1,0:T(8,128)(2,1)S(1)}, u32[]{:S(2)}, u32[]{:S(2)}) collective-permute-start(bf16[4,24,3072]{2,1,0:T(8,128)(2,1)S(1)} %constant_dynamic-update-slice_fusion.10.rest_1_), channel_id=1, source_target_pairs={{0,1},{1,0},{2,3},{3,2},{4,5},{5,4},{6,7},{7,6},{8,9},{9,8},{10,11... | collective-permute-start | bytes 1769480 | tf_op jit(solution)/shard_map/ppermute | solution.py:316
  105.1 15.8 %collective-permute-start.24 = (bf16[4,24,3072]{2,1,0:T(8,128)(2,1)S(1)}, bf16[4,24,3072]{2,1,0:T(8,128)(2,1)S(1)}, u32[]{:S(2)}, u32[]{:S(2)}) collective-permute-start(bf16[4,24,3072]{2,1,0:T(8,128)(2,1)S(1)} %constant_dynamic-update-slice_fusion.8.rest_0_), channel_id=1, source_target_pairs={{0,2},{1,3},{2,0},{3,1},{4,6},{5,7},{6,4},{7,5},{8,10},{9,11},{10,... | collective-permute-start | bytes 1769480 | tf_op jit(solution)/shard_map/ppermute | solution.py:316
  106.4 14.5 %collective-permute-start.26 = (bf16[4,24,3072]{2,1,0:T(8,128)(2,1)S(1)}, bf16[4,24,3072]{2,1,0:T(8,128)(2,1)S(1)}, u32[]{:S(2)}, u32[]{:S(2)}) collective-permute-start(bf16[4,24,3072]{2,1,0:T(8,128)(2,1)S(1)} %constant_dynamic-update-slice_fusion.8.rest_0_), channel_id=1, source_target_pairs={{0,1},{1,0},{2,3},{3,2},{4,5},{5,4},{6,7},{7,6},{8,9},{9,8},{10,11... | collective-permute-start | bytes 1769480 | tf_op jit(solution)/shard_map/ppermute | solution.py:316
  126.3 15.4 %collective-permute-start.29 = (bf16[2,2,24,3072]{3,2,1,0:T(8,128)(2,1)S(1)}, bf16[2,2,24,3072]{3,2,1,0:T(8,128)(2,1)S(1)}, u32[]{:S(2)}, u32[]{:S(2)}) collective-permute-start(bf16[2,2,24,3072]{3,2,1,0:T(8,128)(2,1)S(1)} %get-tuple-element.300), channel_id=1, source_target_pairs={{0,4},{1,5},{2,6},{3,7},{4,0},{5,1},{6,2},{7,3},{8,12},{9,13},{10,... | collective-permute-start | bytes 1769480 | tf_op jit(solution)/shard_map/ppermute | solution.py:316
  127.6 15.1 %collective-permute-start.30 = (bf16[2,2,24,3072]{3,2,1,0:T(8,128)(2,1)S(1)}, bf16[2,2,24,3072]{3,2,1,0:T(8,128)(2,1)S(1)}, u32[]{:S(2)}, u32[]{:S(2)}) collective-permute-start(bf16[2,2,24,3072]{3,2,1,0:T(8,128)(2,1)S(1)} %get-tuple-element.299), channel_id=1, source_target_pairs={{0,2},{1,3},{2,0},{3,1},{4,6},{5,7},{6,4},{7,5},{8,10},{9,11},{10,... | collective-permute-start | bytes 1769480 | tf_op jit(solution)/shard_map/ppermute | solution.py:316
  142.7 18.6 %collective-permute-start.38 = (bf16[16,4,24,768]{3,2,1,0:T(8,128)(2,1)S(1)}, bf16[16,4,24,768]{3,2,1,0:T(8,128)(2,1)S(1)}, u32[]{:S(2)}, u32[]{:S(2)}) collective-permute-start(bf16[16,4,24,768]{3,2,1,0:T(8,128)(2,1)S(1)} %get-tuple-element.227), channel_id=1, source_target_pairs={{0,1},{1,0},{2,3},{3,2},{4,5},{5,4},{6,7},{7,6},{8,9},{9,8},{10,11... | collective-permute-start | bytes 7077896 | tf_op jit(solution)/shard_map/ppermute | solution.py:316
  156.4 25.9 %collective-permute-start.36 = (bf16[24,3072]{1,0:T(8,128)(2,1)S(1)}, bf16[24,3072]{1,0:T(8,128)(2,1)S(1)}, u32[]{:S(2)}, u32[]{:S(2)}) collective-permute-start(bf16[24,3072]{1,0:T(8,128)(2,1)S(1)} %get-tuple-element.318), channel_id=1, source_target_pairs={{0,8},{1,9},{2,10},{3,11},{4,12},{5,13},{6,14},{7,15},{8,0},{9,1},... | collective-permute-start | bytes 442376 | tf_op jit(solution)/shard_map/ppermute | solution.py:316
  158.7 23.6 %collective-permute-start.37 = (bf16[24,3072]{1,0:T(8,128)(2,1)S(1)}, bf16[24,3072]{1,0:T(8,128)(2,1)S(1)}, u32[]{:S(2)}, u32[]{:S(2)}) collective-permute-start(bf16[24,3072]{1,0:T(8,128)(2,1)S(1)} %get-tuple-element.317), channel_id=1, source_target_pairs={{0,16},{1,17},{2,18},{3,19},{4,20},{5,21},{6,22},{7,23},{8,24},{9,... | collective-permute-start | bytes 442376 | tf_op jit(solution)/shard_map/ppermute | solution.py:316
  160.3 22.1 %collective-permute-start.35 = (bf16[24,3072]{1,0:T(8,128)(2,1)S(1)}, bf16[24,3072]{1,0:T(8,128)(2,1)S(1)}, u32[]{:S(2)}, u32[]{:S(2)}) collective-permute-start(bf16[24,3072]{1,0:T(8,128)(2,1)S(1)} %get-tuple-element.319), channel_id=1, source_target_pairs={{0,24},{1,25},{2,26},{3,27},{4,28},{5,29},{6,30},{7,31},{8,16},{9,... | collective-permute-start | bytes 442376 | tf_op jit(solution)/shard_map/ppermute | solution.py:316
  162.0 20.4 %collective-permute-start.39 = (bf16[2,2,4,24,768]{4,3,2,1,0:T(8,128)(2,1)S(1)}, bf16[2,2,4,24,768]{4,3,2,1,0:T(8,128)(2,1)S(1)}, u32[]{:S(2)}, u32[]{:S(2)}) collective-permute-start(bf16[2,2,4,24,768]{4,3,2,1,0:T(8,128)(2,1)S(1)} %get-tuple-element.296), channel_id=1, source_target_pairs={{0,4},{1,5},{2,6},{3,7},{4,0},{5,1},{6,2},{7,3},{8,12},{9,13},{10,... | collective-permute-start | bytes 1769480 | tf_op jit(solution)/shard_map/ppermute | solution.py:316
  164.2 18.2 %collective-permute-start.40 = (bf16[2,2,4,24,768]{4,3,2,1,0:T(8,128)(2,1)S(1)}, bf16[2,2,4,24,768]{4,3,2,1,0:T(8,128)(2,1)S(1)}, u32[]{:S(2)}, u32[]{:S(2)}) collective-permute-start(bf16[2,2,4,24,768]{4,3,2,1,0:T(8,128)(2,1)S(1)} %get-tuple-element.295), channel_id=1, source_target_pairs={{0,2},{1,3},{2,0},{3,1},{4,6},{5,7},{6,4},{7,5},{8,10},{9,11},{10,... | collective-permute-start | bytes 1769480 | tf_op jit(solution)/shard_map/ppermute | solution.py:316
  187.9 20.7 %collective-permute-start.45 = (bf16[50,8,768]{2,1,0:T(8,128)(2,1)S(1)}, bf16[50,8,768]{2,1,0:T(8,128)(2,1)S(1)}, u32[]{:S(2)}, u32[]{:S(2)}) collective-permute-start(bf16[50,8,768]{2,1,0:T(8,128)(2,1)S(1)} %pad_maximum_fusion), channel_id=1, source_target_pairs={{0,4},{1,5},{2,6},{3,7},{4,0},{5,1},{6,2},{7,3},{8,12},{9,13},{10,... | collective-permute-start | bytes 1843208 | tf_op jit(solution)/shard_map/ppermute | solution.py:316
  189.9 18.6 %collective-permute-start.46 = (bf16[2,2,4,24,768]{4,3,2,1,0:T(8,128)(2,1)S(1)}, bf16[2,2,4,24,768]{4,3,2,1,0:T(8,128)(2,1)S(1)}, u32[]{:S(2)}, u32[]{:S(2)}) collective-permute-start(bf16[2,2,4,24,768]{4,3,2,1,0:T(8,128)(2,1)S(1)} %get-tuple-element.293), channel_id=1, source_target_pairs={{0,2},{1,3},{2,0},{3,1},{4,6},{5,7},{6,4},{7,5},{8,10},{9,11},{10,... | collective-permute-start | bytes 1769480 | tf_op jit(solution)/shard_map/ppermute | solution.py:316
  195.4 16.5 %collective-permute-start.53 = (bf16[4,24,768]{2,1,0:T(8,128)(2,1)S(1)}, bf16[4,24,768]{2,1,0:T(8,128)(2,1)S(1)}, u32[]{:S(2)}, u32[]{:S(2)}) collective-permute-start(bf16[4,24,768]{2,1,0:T(8,128)(2,1)S(1)} %get-tuple-element.316), channel_id=1, source_target_pairs={{0,8},{1,9},{2,10},{3,11},{4,12},{5,13},{6,14},{7,15},{8,0},{9,1},... | collective-permute-start | bytes 442376 | tf_op jit(solution)/shard_map/ppermute | solution.py:316
  220.4 13.9 %collective-permute-start.51 = (bf16[14,8,768]{2,1,0:T(8,128)(2,1)S(1)}, bf16[14,8,768]{2,1,0:T(8,128)(2,1)S(1)}, u32[]{:S(2)}, u32[]{:S(2)}) collective-permute-start(bf16[14,8,768]{2,1,0:T(8,128)(2,1)S(1)} %get-tuple-element.325), channel_id=1, source_target_pairs={{0,16},{1,17},{2,18},{3,19},{4,20},{5,21},{6,22},{7,23},{8,24},{9,... | collective-permute-start | bytes 516104 | tf_op jit(solution)/shard_map/ppermute | solution.py:316
  (56 other events, 463.1 us)
